TPU v7x, 32 devices: a whole 2x2x4 slice. The times are simulated.
32 devices in a mesh: group: 4 (over x, core), orb: 8 (over z, y).
Axes of the slice: x: 2, y: 2, z: 4, core: 2. Of those that a mesh axis runs over, the one named last changes fastest.
Arguments:
- orbitals: bfloat16 [96, 64, 1024], P(None, 'orb'), may hold values from -40 to 40
- potential: float32 [64, 1024], P('orb'), may hold values from -5 to 5
- box_shift: int32 [96], replicated, may hold values from 0 to 31, as said below
- pair_partner: int32 [24, 56], replicated, may hold values from -1 to 191, as said below
- pair_member: int32 [24, 56], replicated, may hold values from 0 to 7
Outputs:
- hamiltonian: float32 [96, 64, 1024], P(None, 'orb')
Inputs may be any that keep to these rules, and one draw needn't show every extreme that they name: Exactly 24 colors have each value of box_shift // 8. `pair_partner`: -1 marks an empty slot; a live slot p of block b names a home orbital of slab (b // 3 + p // 8 - 3) mod (8); some block has every slot live.
All inputs are finite; a program needn't handle non-finite values.
Results may differ from a plain program's by a relative error of at most 0.0004.
Values may be sent and summed in bfloat16 or wider, within the bound.
No kernel may reach another device: no remote copies, remote signals or barrier semaphores. Data moves between devices by JAX's collectives and lax.ppermute only.
A program may use at most 128 MiB of HBM per device.

v0:
```python
import jax
import jax.numpy as jnp
from jax import lax
from jax.sharding import PartitionSpec as P

B = 32
MEMBERS = 8


lap_weights = (
    -5369.0 / 1800.0,
    12.0 / 7.0,
    -15.0 / 56.0,
    10.0 / 189.0,
    -1.0 / 112.0,
    2.0 / 1925.0,
    -1.0 / 16632.0,
)
stencil_reach = 6
mixing = 0.25
batch_slots = 8


def extended(x, sides, width):
    for axis, dim in sides:
        peers, length = (lax.axis_size(axis), x.shape[dim])
        up = [(i, (i + 1) % peers) for i in range(peers)]
        down = [(j, i) for i, j in up]
        last = lax.slice_in_dim(x, length - width, length, axis=dim)
        leading = lax.slice_in_dim(x, 0, width, axis=dim)
        before = lax.ppermute(last, axis, up)
        after = lax.ppermute(leading, axis, down)
        x = jnp.concatenate([before, x, after], axis=dim)
    return x


def from_behind(block, axis, distance):
    devices = range(lax.axis_size(axis))
    route = [((i - distance) % len(devices), i) for i in devices]
    return lax.ppermute(block, axis, route)


def sine_rows(box_edge):
    counter = jnp.arange(1, box_edge + 1, dtype=jnp.float32)
    angles = jnp.pi * counter[:, None] * counter[None, :] / (box_edge + 1)
    return jnp.sqrt(2.0 / (box_edge + 1)) * jnp.sin(angles)


def mode_sums(box_edge):
    counter = jnp.arange(1, box_edge + 1, dtype=jnp.float32)
    single = 2.0 - 2.0 * jnp.cos(jnp.pi * counter / (box_edge + 1))
    cube_sum = single[:, None, None] + single[None, :, None] + single[None, None, :]
    return cube_sum.reshape(box_edge, box_edge * box_edge)


def sine_batch(values, sine_mat):
    box_edge = sine_mat.shape[0]
    count = values.shape[0]
    cubes = values.reshape(count, box_edge, box_edge, box_edge)
    cubes = jnp.einsum("ax,gxyz->gayz", sine_mat, cubes, precision=lax.Precision.HIGHEST)
    cubes = jnp.einsum("by,gayz->gabz", sine_mat, cubes, precision=lax.Precision.HIGHEST)
    cubes = jnp.einsum("cz,gabz->gabc", sine_mat, cubes, precision=lax.Precision.HIGHEST)
    return cubes.reshape(count, box_edge, box_edge * box_edge)


def pair_batch(member_boxes, partner_boxes, offsets, sine_mat, mode_sum):
    box_edge = sine_mat.shape[0]

    def place_rows(partner_box, offset):
        padded = jnp.pad(partner_box, ((box_edge, box_edge), (0, 0)))
        return lax.dynamic_slice_in_dim(padded, box_edge - offset, box_edge, 0)

    shifted = jax.vmap(place_rows)(partner_boxes, offsets).astype(jnp.float32)
    density = member_boxes.astype(jnp.float32) * shifted
    solved = sine_batch(sine_batch(density, sine_mat) / mode_sum[None], sine_mat)
    return -mixing * solved * shifted


def cut_box(window, row_start):
    return lax.dynamic_slice_in_dim(window, row_start, B, 0)


def body(orbitals, potential, box_shift, pair_partner, pair_member):
    color_total, slab_rows, cross_size = orbitals.shape
    slab_count = lax.axis_size("orb")
    exch_groups = lax.axis_size("group") - 1
    grid_rows = slab_count * slab_rows
    width_slabs = B // slab_rows
    home_size = MEMBERS * exch_groups
    slot_span = pair_partner.shape[1]
    per_shift = slot_span // (2 * width_slabs - 1)
    boxes_per_color = grid_rows // B
    slab_here = lax.axis_index("orb")
    group_id = lax.axis_index("group")
    classes = box_shift // slab_rows
    subrows = box_shift % slab_rows
    color_ids = jnp.arange(color_total, dtype=jnp.int32)
    color_order = jnp.argsort(classes * color_total + color_ids).reshape(width_slabs, home_size)
    same_class = (classes[:, None] == classes[None, :]) & (color_ids[None, :] < color_ids[:, None])
    class_rank = jnp.sum(same_class.astype(jnp.int32), axis=1)
    haloed = extended(orbitals, (("orb", 1),), stencil_reach)

    def grid_part():
        centre_bf = haloed[:, stencil_reach : stencil_reach + slab_rows]
        centre = centre_bf.astype(jnp.float32)
        global_rows = slab_here * slab_rows + jnp.arange(slab_rows, dtype=jnp.int32)
        own_box = (global_rows[None, :] - box_shift[:, None]) % grid_rows // B
        summed = 3.0 * lap_weights[0] * centre
        flat_pad = jnp.pad(centre_bf, ((0, 0), (0, 0), (stencil_reach * B, stencil_reach * B)))
        along_z = jnp.arange(cross_size, dtype=jnp.int32) % B
        for offset in range(1, stencil_reach + 1):
            for signed in (offset, -offset):
                other_box = (global_rows[None, :] + signed - box_shift[:, None]) % grid_rows // B
                same_box = (other_box == own_box).astype(jnp.float32)[:, :, None]
                near_x = haloed[
                    :, stencil_reach + signed : stencil_reach + signed + slab_rows
                ].astype(jnp.float32)
                start_y = stencil_reach * B + signed * B
                near_y = flat_pad[:, :, start_y : start_y + cross_size].astype(jnp.float32)
                start_z = stencil_reach * B + signed
                inside = ((along_z + signed >= 0) & (along_z + signed < B)).astype(jnp.float32)
                near_z = flat_pad[:, :, start_z : start_z + cross_size].astype(jnp.float32) * inside
                summed = summed + lap_weights[offset] * (same_box * near_x + near_y + near_z)
        return -0.5 * summed + potential[None] * centre

    def empty_part():
        return jnp.zeros((color_total, slab_rows, cross_size), jnp.float32)

    slab_sum = lax.cond(group_id == 0, grid_part, empty_part)
    home_colors = lax.dynamic_index_in_dim(color_order, slab_here % width_slabs, 0, keepdims=False)
    pieces = [jnp.take(orbitals, home_colors, axis=0)]
    for step_no in range(1, width_slabs + 1):
        target_colors = lax.dynamic_index_in_dim(
            color_order, (slab_here - step_no) % width_slabs, 0, keepdims=False
        )
        outgoing = jnp.take(orbitals, target_colors, axis=0)
        pieces.append(from_behind(outgoing, "orb", -step_no))
    window = jnp.concatenate(pieces, axis=1)
    home_subrows = jnp.take(subrows, home_colors)
    home_boxes = jax.vmap(cut_box)(window, home_subrows)
    own_block = jnp.maximum(group_id - 1, 0)
    block_list = own_block[None]
    block_count = block_list.shape[0]
    own_partners = jnp.take(pair_partner, slab_here * exch_groups + block_list, axis=0)
    own_members = jnp.take(pair_member, slab_here * exch_groups + block_list, axis=0)
    shift_parts = []
    for reach_no in range(1 - width_slabs, width_slabs):
        first_slot = (reach_no + width_slabs - 1) * per_shift
        if reach_no == 0:
            wanted = (
                jnp.maximum(own_partners[:, first_slot : first_slot + per_shift], 0)
                // boxes_per_color
            )
            shift_parts.append(jnp.take(home_boxes, jnp.take(class_rank, wanted), axis=0))
        else:
            receiver = (slab_here - reach_no) % slab_count
            their_slots = jnp.take(pair_partner, receiver * exch_groups + block_list, axis=0)[
                :, first_slot : first_slot + per_shift
            ]
            wanted = jnp.maximum(their_slots, 0) // boxes_per_color
            outgoing = jnp.take(home_boxes, jnp.take(class_rank, wanted), axis=0)
            arrived = from_behind(outgoing, "orb", -reach_no)
            shift_parts.append(arrived)
    partner_boxes = jnp.concatenate(shift_parts, axis=1)
    slot_total = block_count * slot_span
    flat_partner = own_partners.reshape(-1)
    flat_member = own_members.reshape(-1)
    living = flat_partner >= 0
    chosen = living & (group_id > 0)
    slot_order = jnp.argsort(
        jnp.where(chosen, 0, 1) * slot_total + jnp.arange(slot_total, dtype=jnp.int32)
    )
    padded_total = -(-slot_total // batch_slots) * batch_slots
    slot_order = jnp.concatenate([slot_order, jnp.zeros((padded_total - slot_total,), jnp.int32)])
    chosen_count = jnp.sum(chosen.astype(jnp.int32))
    turn_count = (chosen_count + batch_slots - 1) // batch_slots
    sine_mat = sine_rows(B)
    mode_sum = mode_sums(B)
    flat_boxes = partner_boxes.reshape(slot_total, B, cross_size)
    lane_ids = jnp.arange(batch_slots, dtype=jnp.int32)

    def add_batch(counter, accum):
        slot_ids = lax.dynamic_slice_in_dim(slot_order, counter * batch_slots, batch_slots)
        live_mask = (counter * batch_slots + lane_ids < chosen_count).astype(jnp.float32)
        local_block = slot_ids // slot_span
        member_num = jnp.take(flat_member, slot_ids)
        member_at = jnp.take(block_list, local_block) * MEMBERS + member_num
        member_color = jnp.take(home_colors, member_at)
        member_anchor = slab_here * slab_rows + jnp.take(subrows, member_color)
        partner_id = jnp.maximum(jnp.take(flat_partner, slot_ids), 0)
        partner_anchor = partner_id % boxes_per_color * B + jnp.take(
            box_shift, partner_id // boxes_per_color
        )
        offsets = (partner_anchor - member_anchor + grid_rows // 2) % grid_rows - grid_rows // 2
        member_boxes = jnp.take(home_boxes, member_at, axis=0)
        partner_set = jnp.take(flat_boxes, slot_ids, axis=0)
        pair_values = pair_batch(member_boxes, partner_set, offsets, sine_mat, mode_sum)
        accum_at = local_block * MEMBERS + member_num
        return accum.at[accum_at].add(pair_values * live_mask[:, None, None])

    exchange = lax.fori_loop(
        0, turn_count, add_batch, jnp.zeros((block_count * MEMBERS, B, cross_size), jnp.float32)
    )
    member_slots = (
        block_list[:, None] * MEMBERS + jnp.arange(MEMBERS, dtype=jnp.int32)[None, :]
    ).reshape(-1)
    exch_colors = jnp.take(home_colors, member_slots)
    exch_subrows = jnp.take(subrows, exch_colors)

    def place_box(box_vals, row_start):
        blank = jnp.zeros(((width_slabs + 1) * slab_rows, cross_size), jnp.float32)
        return lax.dynamic_update_slice_in_dim(blank, box_vals, row_start, 0)

    spread_rows = jax.vmap(place_box)(exchange, exch_subrows)
    slab_sum = slab_sum.at[exch_colors].add(spread_rows[:, :slab_rows])
    for step_no in range(1, width_slabs + 1):
        outgoing = spread_rows[:, step_no * slab_rows : (step_no + 1) * slab_rows]
        arrived = from_behind(outgoing, "orb", step_no)
        sender_home = lax.dynamic_index_in_dim(
            color_order, (slab_here - step_no) % width_slabs, 0, keepdims=False
        )
        sender_colors = jnp.take(sender_home, member_slots)
        slab_sum = slab_sum.at[sender_colors].add(arrived)
    group_total = lax.psum(slab_sum, "group")
    return group_total


def solution(mesh):
    placed = (P(None, "orb", None), P("orb", None), P(), P(), P())
    return jax.shard_map(
        body, mesh=mesh, in_specs=placed, out_specs=P(None, "orb", None), check_vma=False
    )
```

profile of v0, /device:TPU:0, one launch (start us, length us, event | category | flops | bytes accessed | tf_op | source)
XLA Modules:
  0.0 968.5 jit_solution(9830849626246314489)
XLA Ops:
  12.8 6.0 collective-permute-start.2
  25.1 3.0 collective-permute-start.5
  54.8 3.2 collective-permute-start.1
  63.4 7.4 collective-permute-done.5
  75.2 7.8 gather_fusion.10
  83.0 3.5 copy.69
  91.4 10.8 %collective-permute-start.8 = (bf16[1,8,32,1024]{3,2,1,0:T(8,128)(2,1)}, bf16[1,8,32,1024]{3,2,1,0:T(8,128)(2,1)S(1)}, u32[]{:S(2)}, u32[]{:S(2)}) collective-permute-start(bf16[1,8,32,1024]{3,2,1,0:T(8,128)(2,1)} %bitcast_select_fusion.4), channel_id=1, source_target_pairs={{7,0},{0,1},{1,2},{2,3},{3,4},{4,5},{5,6},{6,7},{15,8},{8,9},{9,10... | collective-permute-start | bytes 1572872 | tf_op jit(solution)/shard_map/ppermute | solution.py:40
  105.2 14.8 %collective-permute-start.7 = (bf16[1,8,32,1024]{3,2,1,0:T(8,128)(2,1)}, bf16[1,8,32,1024]{3,2,1,0:T(8,128)(2,1)S(1)}, u32[]{:S(2)}, u32[]{:S(2)}) collective-permute-start(bf16[1,8,32,1024]{3,2,1,0:T(8,128)(2,1)} %bitcast_select_fusion.5), channel_id=1, source_target_pairs={{6,0},{7,1},{0,2},{1,3},{2,4},{3,5},{4,6},{5,7},{14,8},{15,9},{8,1... | collective-permute-start | bytes 1572872 | tf_op jit(solution)/shard_map/ppermute | solution.py:40
  122.9 4.9 collective-permute-start.6
  134.9 25.2 %collective-permute-done.6 = bf16[1,8,32,1024]{3,2,1,0:T(8,128)(2,1)S(1)} collective-permute-done((bf16[1,8,32,1024]{3,2,1,0:T(8,128)(2,1)}, bf16[1,8,32,1024]{3,2,1,0:T(8,128)(2,1)S(1)}, u32[]{:S(2)}, u32[]{:S(2)}) %collective-permute-start.6) | collective-permute-done | bytes 524320 | tf_op jit(solution)/shard_map/ppermute | solution.py:40
  161.9 12.1 %collective-permute-done.9 = bf16[1,8,32,1024]{3,2,1,0:T(8,128)(2,1)S(1)} collective-permute-done((bf16[1,8,32,1024]{3,2,1,0:T(8,128)(2,1)S(1)}, bf16[1,8,32,1024]{3,2,1,0:T(8,128)(2,1)S(1)}, u32[]{:S(2)}, u32[]{:S(2)}) %collective-permute-start.9) | collective-permute-done | bytes 524320 | tf_op jit(solution)/shard_map/ppermute | solution.py:40
  174.0 9.8 %collective-permute-done.10 = bf16[1,8,32,1024]{3,2,1,0:T(8,128)(2,1)S(1)} collective-permute-done((bf16[1,8,32,1024]{3,2,1,0:T(8,128)(2,1)}, bf16[1,8,32,1024]{3,2,1,0:T(8,128)(2,1)S(1)}, u32[]{:S(2)}, u32[]{:S(2)}) %collective-permute-start.10) | collective-permute-done | bytes 524320 | tf_op jit(solution)/shard_map/ppermute | solution.py:40
  183.8 10.5 %collective-permute-done.11 = bf16[1,8,32,1024]{3,2,1,0:T(8,128)(2,1)S(1)} collective-permute-done((bf16[1,8,32,1024]{3,2,1,0:T(8,128)(2,1)S(1)}, bf16[1,8,32,1024]{3,2,1,0:T(8,128)(2,1)S(1)}, u32[]{:S(2)}, u32[]{:S(2)}) %collective-permute-start.11) | collective-permute-done | bytes 524320 | tf_op jit(solution)/shard_map/ppermute | solution.py:40
  197.1 63.3 %while.17 = (s32[]{:T(128)}, f32[8,40,1024]{2,1,0:T(8,128)S(1)}, s32[8,3]{0,1:T(4,128)S(1)}, f32[8,32,1024]{2,1,0:T(8,128)}, s32[]{:T(128)}, /*index=5*/s32[3]{0:T(128)S(1)}, s32[]{:T(128)}) while((s32[]{:T(128)}, f32[8,40,1024]{2,1,0:T(8,128)S(1)}, s32[8,3]{0,1:T(4,128)S(1)}, f32[8,32,1024]{2,1,0:T(8,128)}, s32[]{:T(128)}, ...), condition=%wide.while_cond.1, body=%wide.while_body.1.sunk | while | flops 32787 | bytes 655531 | solution.py:212
  200.4 2.8 dynamic-slice_select_fusion.2
  232.1 2.8 dynamic-slice_select_fusion.2
  240.0 2.8 dynamic-slice_select_fusion.2
  260.6 11.7 %collective-permute-start.12 = (f32[8,8,1024]{2,1,0:T(8,128)S(1)}, f32[8,8,1024]{2,1,0:T(8,128)}, u32[]{:S(2)}, u32[]{:S(2)}) collective-permute-start(f32[8,8,1024]{2,1,0:T(8,128)S(1)} %get-tuple-element.639), channel_id=1, source_target_pairs={{7,0},{0,1},{1,2},{2,3},{3,4},{4,5},{5,6},{6,7},{15,8},{8,9},{9,10... | collective-permute-start | bytes 786440 | tf_op jit(solution)/shard_map/ppermute | solution.py:40
  273.4 5.2 collective-permute-start.15
  282.5 4.0 pad_maximum_fusion
  286.5 26.4 %conditional.1 = (f32[96,8,1024]{2,1,0:T(8,128)}) conditional(s32[]{:T(128)} %convert_element_type.330, () %tuple.33, (bf16[96,8,1024]{2,1,0:T(8,128)(2,1)S(1)}, s32[]{:T(128)}, s32[96]{0:T(128)S(1)}, bf16[96,20,1024]{2,1,0:T(8,128)(2,1)}, f32[8,1024]{1,0:T(8,128)S(1)}) %tuple.162), branch_computations={%region_0.1_spmd, %region_1.2_spmd} | conditional | flops 89253272 | bytes 23799024 | solution.py:129
  287.4 25.5 %fusion.19 = f32[96,8,1024]{2,1,0:T(8,128)} fusion(bf16[96,8,1024]{2,1,0:T(8,128)(2,1)S(1)} %get-tuple-element.299, f32[8,1024]{1,0:T(8,128)S(1)} %get-tuple-element.335, f32[1024]{0:T(1024)S(1)} %get-tuple-element.616, bf16[96,20,1024]{2,1,0:T(8,128)(2,1)} %get-tuple-element.302, f32[96,8]{1,0:T(8,128)S(1)} %get-tuple-element.603, ...), kind=kLoop, calls=%fused_computation.59 | loop fusion | flops 88866816 | bytes 23711744 | tf_op jit(solution)/shard_map/cond/branch_1_fun/add | solution.py:124
  324.6 633.1 %all-reduce.7.cloned.1.call-done = f32[96,8,1024]{2,1,0:T(8,128)} async-done(((f32[96,8,1024]{2,1,0:T(8,128)}), f32[96,8,1024]{2,1,0:T(8,128)}) %all-reduce.7.cloned.1.call-update) | async-done | bytes 3145744 | tf_op jit(solution)/shard_map/psum | solution.py:224
  957.7 4.0 copy.133
  (229 shorter events, 142.7 us)
Async XLA Ops:
  6.5 15.6 %copy-start.1 = (bf16[96,8,1024]{2,1,0:T(8,128)(2,1)S(1)}, bf16[96,8,1024]{2,1,0:T(8,128)(2,1)}, u32[]{:S(2)}) copy-start(bf16[96,8,1024]{2,1,0:T(8,128)(2,1)} %param.23) | copy-start | bytes 4718596
  6.5 951.2 %all-reduce.7.cloned.1.call-start = ((), (), s32[]{:S(2)}) async-start(), calls=%async_computation | async-start | bytes 6291456 | tf_op jit(solution)/shard_map/psum | solution.py:224
  12.8 42.0 %collective-permute-start.2 = (bf16[24,8,1024]{2,1,0:T(8,128)(2,1)}, bf16[24,8,1024]{2,1,0:T(8,128)(2,1)}, u32[]{:S(2)}, u32[]{:S(2)}) collective-permute-start(bf16[24,8,1024]{2,1,0:T(8,128)(2,1)} %broadcast_select_fusion.5), channel_id=1, source_target_pairs={{1,0},{2,1},{3,2},{4,3},{5,4},{6,5},{7,6},{0,7},{9,8},{10,9},{11,1... | collective-permute-start | bytes 1179656 | tf_op jit(solution)/shard_map/ppermute | solution.py:40
  21.7 38.1 %collective-permute-start.3 = (bf16[24,8,1024]{2,1,0:T(8,128)(2,1)}, bf16[24,8,1024]{2,1,0:T(8,128)(2,1)}, u32[]{:S(2)}, u32[]{:S(2)}) collective-permute-start(bf16[24,8,1024]{2,1,0:T(8,128)(2,1)} %broadcast_select_fusion.4), channel_id=1, source_target_pairs={{2,0},{3,1},{4,2},{5,3},{6,4},{7,5},{0,6},{1,7},{10,8},{11,9},{12,... | collective-permute-start | bytes 1179656 | tf_op jit(solution)/shard_map/ppermute | solution.py:40
  23.6 38.0 %collective-permute-start.4 = (bf16[24,8,1024]{2,1,0:T(8,128)(2,1)}, bf16[24,8,1024]{2,1,0:T(8,128)(2,1)}, u32[]{:S(2)}, u32[]{:S(2)}) collective-permute-start(bf16[24,8,1024]{2,1,0:T(8,128)(2,1)} %broadcast_select_fusion.3), channel_id=1, source_target_pairs={{3,0},{4,1},{5,2},{6,3},{7,4},{0,5},{1,6},{2,7},{11,8},{12,9},{13,... | collective-permute-start | bytes 1179656 | tf_op jit(solution)/shard_map/ppermute | solution.py:40
  25.1 45.7 %collective-permute-start.5 = (bf16[24,8,1024]{2,1,0:T(8,128)(2,1)}, bf16[24,8,1024]{2,1,0:T(8,128)(2,1)}, u32[]{:S(2)}, u32[]{:S(2)}) collective-permute-start(bf16[24,8,1024]{2,1,0:T(8,128)(2,1)} %broadcast_select_fusion.2), channel_id=1, source_target_pairs={{4,0},{5,1},{6,2},{7,3},{0,4},{1,5},{2,6},{3,7},{12,8},{13,9},{14,... | collective-permute-start | bytes 1179656 | tf_op jit(solution)/shard_map/ppermute | solution.py:40
  30.2 243.1 %collective-permute-start = (bf16[96,6,1024]{2,0,1:T(8,128)(2,1)}, bf16[96,6,1024]{2,0,1:T(8,128)(2,1)}, u32[]{:S(2)}, u32[]{:S(2)}) collective-permute-start(bf16[96,6,1024]{2,0,1:T(8,128)(2,1)} %copy.76), channel_id=1, source_target_pairs={{0,1},{1,2},{2,3},{3,4},{4,5},{5,6},{6,7},{7,0},{8,9},{9,10},{10,1... | collective-permute-start | bytes 3538952 | tf_op jit(solution)/shard_map/ppermute | solution.py:31
  54.8 225.7 %collective-permute-start.1 = (bf16[96,6,1024]{2,0,1:T(8,128)(2,1)}, bf16[96,6,1024]{2,0,1:T(8,128)(2,1)}, u32[]{:S(2)}, u32[]{:S(2)}) collective-permute-start(bf16[96,6,1024]{2,0,1:T(8,128)(2,1)} %copy.77), channel_id=1, source_target_pairs={{1,0},{2,1},{3,2},{4,3},{5,4},{6,5},{7,6},{0,7},{9,8},{10,9},{11,1... | collective-permute-start | bytes 3538952 | tf_op jit(solution)/shard_map/ppermute | solution.py:32
  91.4 70.2 %collective-permute-start.8 = (bf16[1,8,32,1024]{3,2,1,0:T(8,128)(2,1)}, bf16[1,8,32,1024]{3,2,1,0:T(8,128)(2,1)S(1)}, u32[]{:S(2)}, u32[]{:S(2)}) collective-permute-start(bf16[1,8,32,1024]{3,2,1,0:T(8,128)(2,1)} %bitcast_select_fusion.4), channel_id=1, source_target_pairs={{7,0},{0,1},{1,2},{2,3},{3,4},{4,5},{5,6},{6,7},{15,8},{8,9},{9,10... | collective-permute-start | bytes 1572872 | tf_op jit(solution)/shard_map/ppermute | solution.py:40
  105.2 55.0 %collective-permute-start.7 = (bf16[1,8,32,1024]{3,2,1,0:T(8,128)(2,1)}, bf16[1,8,32,1024]{3,2,1,0:T(8,128)(2,1)S(1)}, u32[]{:S(2)}, u32[]{:S(2)}) collective-permute-start(bf16[1,8,32,1024]{3,2,1,0:T(8,128)(2,1)} %bitcast_select_fusion.5), channel_id=1, source_target_pairs={{6,0},{7,1},{0,2},{1,3},{2,4},{3,5},{4,6},{5,7},{14,8},{15,9},{8,1... | collective-permute-start | bytes 1572872 | tf_op jit(solution)/shard_map/ppermute | solution.py:40
  122.9 37.3 %collective-permute-start.6 = (bf16[1,8,32,1024]{3,2,1,0:T(8,128)(2,1)}, bf16[1,8,32,1024]{3,2,1,0:T(8,128)(2,1)S(1)}, u32[]{:S(2)}, u32[]{:S(2)}) collective-permute-start(bf16[1,8,32,1024]{3,2,1,0:T(8,128)(2,1)} %bitcast_select_fusion.6), channel_id=1, source_target_pairs={{5,0},{6,1},{7,2},{0,3},{1,4},{2,5},{3,6},{4,7},{13,8},{14,9},{15,... | collective-permute-start | bytes 1572872 | tf_op jit(solution)/shard_map/ppermute | solution.py:40
  160.1 13.8 %collective-permute-start.9 = (bf16[1,8,32,1024]{3,2,1,0:T(8,128)(2,1)S(1)}, bf16[1,8,32,1024]{3,2,1,0:T(8,128)(2,1)S(1)}, u32[]{:S(2)}, u32[]{:S(2)}) collective-permute-start(bf16[1,8,32,1024]{3,2,1,0:T(8,128)(2,1)S(1)} %bitcast_select_fusion.2), channel_id=1, source_target_pairs={{1,0},{2,1},{3,2},{4,3},{5,4},{6,5},{7,6},{0,7},{9,8},{10,9},{11,1... | collective-permute-start | bytes 1572872 | tf_op jit(solution)/shard_map/ppermute | solution.py:40
  160.2 23.6 %collective-permute-start.10 = (bf16[1,8,32,1024]{3,2,1,0:T(8,128)(2,1)}, bf16[1,8,32,1024]{3,2,1,0:T(8,128)(2,1)S(1)}, u32[]{:S(2)}, u32[]{:S(2)}) collective-permute-start(bf16[1,8,32,1024]{3,2,1,0:T(8,128)(2,1)} %bitcast_select_fusion.1), channel_id=1, source_target_pairs={{2,0},{3,1},{4,2},{5,3},{6,4},{7,5},{0,6},{1,7},{10,8},{11,9},{12,... | collective-permute-start | bytes 1572872 | tf_op jit(solution)/shard_map/ppermute | solution.py:40
  161.6 34.9 %copy-start = (s32[96]{0:T(128)S(1)}, s32[96]{0:T(128)}, u32[]{:S(2)}) copy-start(s32[96]{0:T(128)} %param.25) | copy-start | bytes 1156
  161.6 32.7 %collective-permute-start.11 = (bf16[1,8,32,1024]{3,2,1,0:T(8,128)(2,1)S(1)}, bf16[1,8,32,1024]{3,2,1,0:T(8,128)(2,1)S(1)}, u32[]{:S(2)}, u32[]{:S(2)}) collective-permute-start(bf16[1,8,32,1024]{3,2,1,0:T(8,128)(2,1)S(1)} %bitcast_select_fusion), channel_id=1, source_target_pairs={{3,0},{4,1},{5,2},{6,3},{7,4},{0,5},{1,6},{2,7},{11,8},{12,9},{13,... | collective-permute-start | bytes 1572872 | tf_op jit(solution)/shard_map/ppermute | solution.py:40
  260.6 21.9 %copy-start.2 = (bf16[96,8,1024]{2,1,0:T(8,128)(2,1)S(1)}, bf16[96,8,1024]{2,1,0:T(8,128)(2,1)}, u32[]{:S(2)}) copy-start(bf16[96,8,1024]{2,1,0:T(8,128)(2,1)} %param.23) | copy-start | bytes 4718596
  260.6 54.6 %collective-permute-start.12 = (f32[8,8,1024]{2,1,0:T(8,128)S(1)}, f32[8,8,1024]{2,1,0:T(8,128)}, u32[]{:S(2)}, u32[]{:S(2)}) collective-permute-start(f32[8,8,1024]{2,1,0:T(8,128)S(1)} %get-tuple-element.639), channel_id=1, source_target_pairs={{7,0},{0,1},{1,2},{2,3},{3,4},{4,5},{5,6},{6,7},{15,8},{8,9},{9,10... | collective-permute-start | bytes 786440 | tf_op jit(solution)/shard_map/ppermute | solution.py:40
  272.3 45.3 %collective-permute-start.13 = (f32[8,8,1024]{2,1,0:T(8,128)S(1)}, f32[8,8,1024]{2,1,0:T(8,128)}, u32[]{:S(2)}, u32[]{:S(2)}) collective-permute-start(f32[8,8,1024]{2,1,0:T(8,128)S(1)} %get-tuple-element.638), channel_id=1, source_target_pairs={{6,0},{7,1},{0,2},{1,3},{2,4},{3,5},{4,6},{5,7},{14,8},{15,9},{8,1... | collective-permute-start | bytes 786440 | tf_op jit(solution)/shard_map/ppermute | solution.py:40
  273.4 46.8 %collective-permute-start.14 = (f32[8,8,1024]{2,1,0:T(8,128)S(1)}, f32[8,8,1024]{2,1,0:T(8,128)S(1)}, u32[]{:S(2)}, u32[]{:S(2)}) collective-permute-start(f32[8,8,1024]{2,1,0:T(8,128)S(1)} %get-tuple-element.637), channel_id=1, source_target_pairs={{5,0},{6,1},{7,2},{0,3},{1,4},{2,5},{3,6},{4,7},{13,8},{14,9},{15,... | collective-permute-start | bytes 786440 | tf_op jit(solution)/shard_map/ppermute | solution.py:40
  273.4 49.0 %collective-permute-start.15 = (f32[8,8,1024]{2,1,0:T(8,128)S(1)}, f32[8,8,1024]{2,1,0:T(8,128)S(1)}, u32[]{:S(2)}, u32[]{:S(2)}) collective-permute-start(f32[8,8,1024]{2,1,0:T(8,128)S(1)} %get-tuple-element.636), channel_id=1, source_target_pairs={{4,0},{5,1},{6,2},{7,3},{0,4},{1,5},{2,6},{3,7},{12,8},{13,9},{14,... | collective-permute-start | bytes 786440 | tf_op jit(solution)/shard_map/ppermute | solution.py:40
  286.5 26.4 %copy-start.9 = (s32[8]{0:T(128)S(1)}, s32[8]{0:T(128)}, u32[]{:S(2)}) copy-start(s32[8]{0:T(128)} %copy-done.8) | copy-start | bytes 100
  286.5 28.7 %copy-start.14 = (s32[8]{0:T(128)S(1)}, s32[8]{0:T(128)}, u32[]{:S(2)}) copy-start(s32[8]{0:T(128)} %compare_select_fusion.32) | copy-start | bytes 100
  286.5 31.2 %copy-start.13 = (s32[8]{0:T(128)S(1)}, s32[8]{0:T(128)}, u32[]{:S(2)}) copy-start(s32[8]{0:T(128)} %compare_select_fusion.31) | copy-start | bytes 100
  286.5 33.6 %copy-start.12 = (s32[8]{0:T(128)S(1)}, s32[8]{0:T(128)}, u32[]{:S(2)}) copy-start(s32[8]{0:T(128)} %compare_select_fusion.30) | copy-start | bytes 100
  (8 other events, 41.5 us)
Sparse Core Ops, SparseCore 0:
  324.8 632.9 all-reduce.6
where the time goes:
time: 982 us; the launch traced here: 969 us
  waiting for transfers between devices  698 us (71%)
  other arithmetic  105 us (11%)
  local copies, waits for them, and re-layouts  85.9 us (9%)
  starting transfers between devices  64.1 us (7%)
  between operations  14.7 us (1%)
    psum x1, waiting for transfers between devices, body(): group_total = lax.psum(slab_sum, 'group')  633 us
    ppermute x14, waiting for transfers between devices, from_behind(): return lax.ppermute(block, axis, route)  65 us
    ppermute x14, starting transfers between devices, from_behind(): return lax.ppermute(block, axis, route)  59.3 us
    scatter x16, other arithmetic  43.1 us
    add x1, other arithmetic, grid_part(): return -0.5 * summed + potential[None] * centre  25.5 us
    scatter x24, local copies, waits for them, and re-layouts  20 us
  transfers between devices with their start and end apart: 17, of which 6 were waited for; matrix products, arithmetic and copies ran while one was open for 18% of the time, Pallas kernels for 0%

commit v1 on v0

v1 whole, which is shorter than its diff:
```python
import functools
import math

import jax
import jax.numpy as jnp
import numpy as np
from jax import lax
from jax.experimental import pallas as pl
from jax.experimental.pallas import tpu as pltpu
from jax.sharding import PartitionSpec as P

lap_weights = (
    -5369.0 / 1800.0,
    12.0 / 7.0,
    -15.0 / 56.0,
    10.0 / 189.0,
    -1.0 / 112.0,
    2.0 / 1925.0,
    -1.0 / 16632.0,
)
stencil_reach = 6
mixing = 0.25
f32, bf16, i32 = jnp.float32, jnp.bfloat16, jnp.int32
kin_colors = 8
EMPTY = -(1 << 20)


def split_np(values):
    head = np.asarray(values, np.float32).astype(bf16)
    rest = (values - head.astype(np.float64)).astype(np.float32).astype(bf16)
    return np.stack([head, rest])


def split2(x):
    head = x.astype(bf16)
    return head, (x - head.astype(f32)).astype(bf16)


def dot(a, b):
    return jnp.dot(a, b, preferred_element_type=f32)


def dot3(a, b):
    return dot(a[0], b[0]) + (dot(a[0], b[1]) + dot(a[1], b[0]))


class Sizes:
    def __init__(self, orbitals, pair_partner, groups, slabs):
        self.colors, self.rows, self.cells = orbitals.shape
        self.groups, self.slabs = groups, slabs
        self.box = math.isqrt(self.cells)
        self.width = self.box // self.rows
        self.span = self.width + 1
        self.mid = self.width // 2
        self.home = self.colors // self.width
        self.blocks = pair_partner.shape[0] // slabs
        self.members = self.home // self.blocks
        self.slots = pair_partner.shape[1]
        self.grid = slabs * self.rows
        self.per = self.grid // self.box
        self.part = self.colors // groups
        self.own = self.home // groups
        self.frame = self.span * self.rows
        self.batch = max(1, 256 // self.frame)
        self.cap = -(-self.blocks * self.slots // self.batch) * self.batch + self.batch


def butterfly_order(groups):
    order, step = [0], groups // 2
    while step:
        order += [o ^ step for o in order]
        step //= 2
    return order


def sine_matrix(box):
    count = np.arange(1, box + 1)
    return np.sqrt(2.0 / (box + 1)) * np.sin(np.pi * np.outer(count, count) / (box + 1))


def pair_tables(z):
    box, half = z.box, z.box // 2
    sine = sine_matrix(box)
    side = [np.arange(half), box - 1 - np.arange(half)]
    order = np.concatenate([(y[:, None] * box + x[None, :]).reshape(-1) for y in side for x in side])
    regroup = np.zeros((z.cells, z.cells))
    regroup[order, np.arange(z.cells)] = 1.0
    halves = [sine[0::2, :half], sine[1::2, :half]]
    forward = np.stack([np.kron(a, b).T for a in halves for b in halves])
    backward = np.stack([m.T for m in forward])
    single = 2.0 - 2.0 * np.cos(np.pi * np.arange(1, box + 1) / (box + 1))
    modes = [(single[py::2][:, None] + single[pz::2][None, :]).reshape(-1) for py in (0, 1) for pz in (0, 1)]
    scale = -mixing / (single[:, None] + np.concatenate(modes)[None, :])
    into = np.zeros((z.rows, box, z.batch * z.frame))
    back = np.zeros((z.rows, z.frame, z.batch * box))
    for sub in range(z.rows):
        for i in range(z.batch):
            into[sub, :, i * z.frame + sub : i * z.frame + sub + box] = sine
            back[sub, sub : sub + box, i * box : (i + 1) * box] = sine.T
    return dict(
        regroup=regroup.astype(bf16),
        ungroup=regroup.T.astype(bf16),
        forward=split_np(forward),
        backward=split_np(backward),
        scale=scale.astype(np.float32),
        into=into.astype(np.float32),
        back=back.astype(np.float32),
    )


def stencil_tables(z):
    box, rows = z.box, z.rows
    band = np.zeros((box, box))
    for off in range(1, stencil_reach + 1):
        band += lap_weights[off] * (np.eye(box, k=off) + np.eye(box, k=-off))
    eye = np.eye(box)
    plane = -0.5 * (3.0 * lap_weights[0] * np.eye(z.cells) + np.kron(band, eye) + np.kron(eye, band))
    along = np.zeros((box, rows, 3 * kin_colors * rows))
    for start in range(box):
        for x in range(rows):
            for y in range(-rows, 2 * rows):
                off = abs(y - x)
                if off and off <= stencil_reach and (x - start) // box == (y - start) // box:
                    for i in range(kin_colors):
                        at = ((y + rows) // rows) * kin_colors * rows + i * rows + y % rows
                        along[start, x, at] = -0.5 * lap_weights[off]
    return split_np(plane), along.astype(np.float32)


def plan_kernel(z, ids, shift, partner, member, count_ref, slot_ref, mine_ref, src_ref, order, filled):
    q, g = ids[0], ids[1]
    o = lax.rem(q + z.slabs - z.mid, z.slabs)
    for c in range(z.width):
        filled[c] = 0

    def color_step(c, _):
        cls = shift[c] // z.rows
        n = filled[cls]
        filled[cls] = n + 1
        order[cls, n] = c
        back = lax.rem(q - cls + z.slabs * z.width, z.width)
        src_ref[c] = lax.rem(n, z.groups) * z.width * z.own + back * z.own + n // z.groups
        return 0

    lax.fori_loop(0, z.colors, color_step, 0)
    home_class = lax.rem(o, z.width)
    for m in range(z.own):
        c = order[home_class, m * z.groups + g]
        mine_ref[0, m] = c
        mine_ref[1, m] = lax.rem(shift[c], z.rows)
    total = jnp.int32(0)
    for t in range(z.blocks):

        def slot_step(p, total, t=t):
            j = partner[o * z.blocks + t, p]
            n = t * z.members + member[o * z.blocks + t, p]
            live = jnp.logical_and(j >= 0, lax.rem(n, z.groups) == g)
            j = jnp.maximum(j, 0)
            cj = j // z.per
            sub = lax.rem(shift[order[home_class, n]], z.rows)
            there = (j - cj * z.per) * z.box + shift[cj]
            d = there - (o * z.rows + sub) + z.grid // 2
            d = lax.rem(d + z.grid, z.grid) - z.grid // 2
            slot_ref[0, total] = n // z.groups
            slot_ref[1, total] = cj
            slot_ref[2, total] = sub + d
            slot_ref[3, total] = sub
            return total + live.astype(i32)

        total = lax.fori_loop(0, z.slots, slot_step, total)
    count_ref[0] = total
    for i in range(z.batch):
        slot_ref[0, total + i] = 0
        slot_ref[1, total + i] = 0
        slot_ref[2, total + i] = EMPTY
        slot_ref[3, total + i] = 0


def plan(z, ids, shift, partner, member):
    smem = pl.BlockSpec(memory_space=pltpu.SMEM)
    return pl.pallas_call(
        functools.partial(plan_kernel, z),
        out_shape=(
            jax.ShapeDtypeStruct((1,), i32),
            jax.ShapeDtypeStruct((4, z.cap), i32),
            jax.ShapeDtypeStruct((2, z.own), i32),
            jax.ShapeDtypeStruct((z.colors,), i32),
        ),
        in_specs=[smem] * 4,
        out_specs=(smem,) * 4,
        scratch_shapes=[pltpu.SMEM((z.width, z.colors), i32), pltpu.SMEM((z.width,), i32)],
        name="plan",
    )(ids, shift, partner, member)


def pair_kernel(z, ids, count, slots, mine, here, *rest):
    pieces, rest = rest[: (z.span - 1) * z.groups], rest[(z.span - 1) * z.groups :]
    (regroup, ungroup, forward, backward, scale, into, back), rest = rest[:7], rest[7:]
    outs, rest = rest[: z.span], rest[z.span :]
    window, raw, own, held, acc, sems = rest
    g = ids[1]
    order = butterfly_order(z.groups)
    copies = [pltpu.make_async_copy(here, window.at[z.mid], sems.at[0])]
    for k in range(z.span - 1):
        slab = k if k < z.mid else k + 1
        for p in range(z.groups):
            at = (g ^ order[p]) * z.part
            copies.append(
                pltpu.make_async_copy(
                    pieces[k * z.groups + p], window.at[slab, pl.ds(at, z.part)], sems.at[len(copies)]
                )
            )
    for c in copies:
        c.start()
    acc[...] = jnp.zeros_like(acc)
    for c in copies:
        c.wait()
    frame, box, batch, quad = z.frame, z.box, z.batch, z.cells // 4
    rows = lax.broadcasted_iota(i32, (z.rows, z.cells), 0)

    def regrouped():
        return dot(raw[...].astype(bf16), regroup[...])

    for first in range(0, z.own, batch):
        todo = min(batch, z.own - first)
        for i in range(batch):
            for k in range(z.span):
                at = i * frame + k * z.rows
                if i < todo:
                    raw[at : at + z.rows, :] = window[k, mine[0, first + i]].astype(f32)
                else:
                    raw[at : at + z.rows, :] = jnp.zeros((z.rows, z.cells), f32)
        done = regrouped()
        for i in range(todo):
            own[first + i] = done[i * frame : (i + 1) * frame]

    lane_in = lax.broadcasted_iota(i32, (box, batch * frame), 1)
    lane_back = lax.broadcasted_iota(i32, (frame, batch * box), 1)

    def step(b, _):
        first = b * batch
        for i in range(batch):
            color, start = slots[1, first + i], slots[2, first + i]
            for k in range(z.span):
                at = i * frame + k * z.rows
                r = rows + (k * z.rows - start)
                inside = (r >= 0) & (r < box)
                raw[at : at + z.rows, :] = jnp.where(inside, window[k, color].astype(f32), 0.0)
        held[...] = regrouped()
        lhs_in, lhs_back, density = [], [], []
        for i in range(batch):
            m, sub = slots[0, first + i], slots[3, first + i]
            lo = i * frame
            lhs_in.append(jnp.where((lane_in >= lo) & (lane_in < lo + frame), into[sub], 0.0))
            lo = i * box
            lhs_back.append(jnp.where((lane_back >= lo) & (lane_back < lo + box), back[sub], 0.0))
            density.append(own[m] * held[i * frame : (i + 1) * frame])
        x = dot3(split2(jnp.concatenate(lhs_in, 0)), split2(jnp.concatenate(density, 0)))
        q = [x[:, i * quad : (i + 1) * quad] for i in range(4)]
        a, b_, c, d = q[0] + q[2], q[0] - q[2], q[1] + q[3], q[1] - q[3]
        folded = (a + c, a - c, b_ + d, b_ - d)
        solved = []
        for i in range(4):
            y = dot3(split2(folded[i]), (forward[0, i], forward[1, i]))
            factor = scale[:, i * quad : (i + 1) * quad]
            y = (y.reshape(batch, box, quad) * factor[None]).reshape(batch * box, quad)
            solved.append(dot3(split2(y), (backward[0, i], backward[1, i])))
        ee, eo, oe, oo = solved
        a, b_, c, d = ee + oe, ee - oe, eo + oo, eo - oo
        field = jnp.concatenate([a + c, a - c, b_ + d, b_ - d], axis=1)
        v = dot3(split2(jnp.concatenate(lhs_back, 0)), split2(field))
        for i in range(batch):
            m = slots[0, first + i]
            lo = i * frame
            acc[m] = acc[m] + v[lo : lo + frame] * held[lo : lo + frame]
        return 0

    lax.fori_loop(0, (count[0] + batch - 1) // batch, step, 0)
    for m in range(z.own):
        x = acc[m]
        one = x.astype(bf16)
        left = x - one.astype(f32)
        two, three = split2(left)
        res = dot(one, ungroup[...]) + (dot(two, ungroup[...]) + dot(three, ungroup[...]))
        for k in range(z.span):
            outs[k][m] = res[k * z.rows : (k + 1) * z.rows]


def pair_part(z, ids, count, slots, mine, here, pieces):
    tables = pair_tables(z)
    smem = pl.BlockSpec(memory_space=pltpu.SMEM)
    vmem = pl.BlockSpec(memory_space=pltpu.VMEM)
    hbm = pl.BlockSpec(memory_space=pl.ANY)
    names = ("regroup", "ungroup", "forward", "backward", "scale", "into", "back")
    wide = z.batch * z.frame
    return pl.pallas_call(
        functools.partial(pair_kernel, z),
        out_shape=[jax.ShapeDtypeStruct((z.own, z.rows, z.cells), f32)] * z.span,
        in_specs=[smem] * 4 + [hbm] * (1 + len(pieces)) + [vmem] * len(names),
        out_specs=[vmem] * z.span,
        scratch_shapes=[
            pltpu.VMEM((z.span, z.colors, z.rows, z.cells), bf16),
            pltpu.VMEM((wide, z.cells), f32),
            pltpu.VMEM((z.own, z.frame, z.cells), f32),
            pltpu.VMEM((wide, z.cells), f32),
            pltpu.VMEM((z.own, z.frame, z.cells), f32),
            pltpu.SemaphoreType.DMA((1 + len(pieces),)),
        ],
        compiler_params=pltpu.CompilerParams(vmem_limit_bytes=56 << 20),
        cost_estimate=pl.CostEstimate(flops=20_000_000_000, bytes_accessed=16_000_000, transcendentals=0),
        name="pair_solves",
    )(ids, count, slots, mine, here, *pieces, *[jnp.asarray(tables[n]) for n in names])


def local_kernel(z, per_step, ids, shift, here, potential, *rest):
    pieces, rest = rest[: 2 * z.groups], rest[2 * z.groups :]
    plane, along, out, near, lhs, sems = rest
    q, g = ids[0], ids[1]
    order = butterfly_order(z.groups)
    step = pl.program_id(0)

    @pl.when(step == 0)
    def _():
        copies = []
        for s in range(2):
            for p in range(z.groups):
                at = (g ^ order[p]) * z.part
                copies.append(
                    pltpu.make_async_copy(
                        pieces[s * z.groups + p], near.at[s, pl.ds(at, z.part)], sems.at[len(copies)]
                    )
                )
        for c in copies:
            c.start()
        for c in copies:
            c.wait()

    rows, cells, kc = z.rows, z.cells, kin_colors
    lane = lax.broadcasted_iota(i32, (rows, 3 * kc * rows), 1)
    centre = here[...].reshape(per_step * rows, cells)
    tile = 256
    cols = []
    for j in range(0, cells, tile):
        lo, hi = max(0, j - stencil_reach * z.box), min(cells, j + tile + stencil_reach * z.box)
        lo, hi = lo // tile * tile, -(-hi // tile) * tile
        u = centre[:, lo:hi]
        cols.append(dot(u, plane[0, lo:hi, j : j + tile]) + dot(u, plane[1, lo:hi, j : j + tile]))
    flat = jnp.concatenate(cols, axis=1)
    pot = potential[...]
    for s in range(per_step // kc):
        first = step * per_step + s * kc
        for i in range(kc):
            start = lax.rem(shift[first + i] - q * rows + z.grid, z.box)
            lhs[i * rows : (i + 1) * rows, :] = jnp.where(lane // rows % kc == i, along[start], 0.0)
        mid = centre[s * kc * rows : (s + 1) * kc * rows]
        before = near[0, pl.ds(first, kc)].reshape(kc * rows, cells)
        after = near[1, pl.ds(first, kc)].reshape(kc * rows, cells)
        stack = jnp.concatenate([before, mid, after], axis=0)
        head, low = split2(lhs[...])
        kin = dot(head, stack) + dot(low, stack) + flat[s * kc * rows : (s + 1) * kc * rows]
        value = kin.reshape(kc, rows, cells) + pot[None] * mid.astype(f32).reshape(kc, rows, cells)
        out[s * kc : (s + 1) * kc] = value


def local_part(z, ids, shift, here, potential, pieces):
    plane, along = stencil_tables(z)
    per_step = kin_colors * max(d for d in (1, 2, 3, 4) if z.colors // kin_colors % d == 0)
    smem = pl.BlockSpec(memory_space=pltpu.SMEM)
    hbm = pl.BlockSpec(memory_space=pl.ANY)
    block = pl.BlockSpec((per_step, z.rows, z.cells), lambda i: (i, 0, 0))
    vmem = pl.BlockSpec(memory_space=pltpu.VMEM)
    return pl.pallas_call(
        functools.partial(local_kernel, z, per_step),
        grid=(z.colors // per_step,),
        out_shape=jax.ShapeDtypeStruct((z.colors, z.rows, z.cells), f32),
        in_specs=[smem, smem, block, vmem] + [hbm] * len(pieces) + [vmem] * 2,
        out_specs=block,
        scratch_shapes=[
            pltpu.VMEM((2, z.colors, z.rows, z.cells), bf16),
            pltpu.VMEM((kin_colors * z.rows, 3 * kin_colors * z.rows), f32),
            pltpu.SemaphoreType.DMA((len(pieces),)),
        ],
        compiler_params=pltpu.CompilerParams(
            vmem_limit_bytes=40 << 20, dimension_semantics=("arbitrary",)
        ),
        cost_estimate=pl.CostEstimate(flops=6_000_000_000, bytes_accessed=12_000_000, transcendentals=0),
        name="local",
    )(ids, shift, here, potential, *pieces, jnp.asarray(plane), jnp.asarray(along))


def finish_kernel(z, per_step, ids, src, local, *rest):
    pieces, out, gathered, sems = rest[: z.groups], rest[z.groups], rest[z.groups + 1], rest[z.groups + 2]
    order = butterfly_order(z.groups)
    step = pl.program_id(0)
    size = z.width * z.own

    @pl.when(step == 0)
    def _():
        copies = [
            pltpu.make_async_copy(pieces[p], gathered.at[pl.ds((ids[1] ^ order[p]) * size, size)], sems.at[p])
            for p in range(z.groups)
        ]
        for c in copies:
            c.start()
        for c in copies:
            c.wait()

    for i in range(per_step):
        out[i] = local[i] + gathered[src[step * per_step + i]]


def finish(z, ids, src, local, pieces):
    per_step = z.colors // 8 if z.colors % 8 == 0 else 1
    smem = pl.BlockSpec(memory_space=pltpu.SMEM)
    hbm = pl.BlockSpec(memory_space=pl.ANY)
    block = pl.BlockSpec((per_step, z.rows, z.cells), lambda i: (i, 0, 0))
    return pl.pallas_call(
        functools.partial(finish_kernel, z, per_step),
        grid=(z.colors // per_step,),
        out_shape=jax.ShapeDtypeStruct(local.shape, f32),
        in_specs=[smem, smem, block] + [hbm] * len(pieces),
        out_specs=block,
        scratch_shapes=[
            pltpu.VMEM((z.groups * z.width * z.own, z.rows, z.cells), f32),
            pltpu.SemaphoreType.DMA((z.groups,)),
        ],
        compiler_params=pltpu.CompilerParams(
            vmem_limit_bytes=24 << 20, dimension_semantics=("arbitrary",)
        ),
        name="finish",
    )(ids, src, local, *pieces)


def from_slab(x, away, slabs):
    return lax.ppermute(x, "orb", [((i + away) % slabs, i) for i in range(slabs)])


def swapped(x, bit, groups):
    return lax.ppermute(x, "group", [(i, i ^ bit) for i in range(groups)])


def shared(piece, groups):
    have, step = [piece], groups // 2
    while step:
        have += [swapped(x, step, groups) for x in have]
        step //= 2
    return have


def body(orbitals, potential, box_shift, pair_partner, pair_member):
    slabs, groups = lax.axis_size("orb"), lax.axis_size("group")
    z = Sizes(orbitals, pair_partner, groups, slabs)
    q, g = lax.axis_index("orb"), lax.axis_index("group")
    ids = jnp.stack([q, g]).astype(i32)
    mine = lax.dynamic_slice_in_dim(orbitals, g * z.part, z.part, 0)
    pieces = []
    for k in range(z.span):
        if k != z.mid:
            pieces.append(shared(from_slab(mine, k - z.mid, slabs), groups))
    count, slots, home, src = plan(z, ids, box_shift, pair_partner, pair_member)
    local = local_part(
        z, ids, box_shift, orbitals, potential, pieces[z.mid - 1] + pieces[z.mid]
    )
    spread = pair_part(z, ids, count, slots, home, orbitals, [x for p in pieces for x in p])
    parts = [
        spread[k] if k == z.mid else from_slab(spread[k], z.mid - k, slabs) for k in range(z.span)
    ]
    parts = [parts[0] + parts[-1]] + parts[1:-1]
    return finish(z, ids, src, local, shared(jnp.concatenate(parts, axis=0), groups))


def solution(mesh):
    placed = (P(None, "orb", None), P("orb", None), P(), P(), P())
    return jax.shard_map(
        body, mesh=mesh, in_specs=placed, out_specs=P(None, "orb", None), check_vma=False
    )
```

time: 982 us -> 150 us (0.15); the launches traced: 969 us -> 148 us
  waiting for transfers between devices: 698 us -> 65.4 us
  other arithmetic: 105 us -> 1.71 us
  local copies, waits for them, and re-layouts: 85.9 us -> 8.96 us
  Pallas kernels: 0 us -> 37.8 us
  starting transfers between devices: 64.1 us -> 33.3 us
  between operations: 14.7 us -> 0.34 us
    psum x1 -> x0, waiting for transfers between devices: 633 us -> none  [body(): group_total = lax.psum(slab_sum, 'group')]
    scatter x17 -> x0, other arithmetic: 43.7 us -> none
    pallas_call x0 -> x4, Pallas kernels: none -> 37.8 us  [the longest x1 18.4 us: pair_part(): pl.pallas_call(functools.partial(pair_kernel, z), out_shape=[jax.ShapeDty...]
    gather x27 -> x0, local copies, waits for them, and re-layouts: 37.2 us -> none  [the longest x12 15.8 us: body(): outgoing = jnp.take(home_boxes, jnp.take(class_rank, wanted), axis=0)]
    ppermute x16 -> x23, starting transfers between devices: 64.1 us -> 33.3 us  [the longest x8 21.9 us: from_slab(): lax.ppermute(x, 'orb', [((i + away) % slabs, i) for i in range(slabs)])]
    add x11 -> x1, other arithmetic: 27.1 us -> 0.02 us  [body(): parts = [parts[0] + parts[-1]] + parts[1:-1]]
    scatter x24 -> x0, local copies, waits for them, and re-layouts: 20 us -> none
    scatter-add x5 -> x0, other arithmetic: 11.7 us -> none  [the longest x4 9.42 us: body(): slab_sum = slab_sum.at[sender_colors].add(arrived)]
  transfers between devices with their start and end apart: 17 -> 23, of which waited for: 6 -> 10; matrix products, arithmetic and copies ran while one was open for 18% -> 0% of each run, Pallas kernels for 0% -> 10%
where the time goes in v1:
time: 150 us; the launch traced here: 148 us
  waiting for transfers between devices  65.4 us (44%)
  Pallas kernels  37.8 us (25%)
  starting transfers between devices  33.3 us (22%)
  local copies, waits for them, and re-layouts  8.96 us (6%)
  other arithmetic  1.71 us (1%)
    ppermute x15, waiting for transfers between devices, swapped(): return lax.ppermute(x, 'group', [(i, i ^ bit) for i in range(groups)])  37.5 us
    ppermute x8, waiting for transfers between devices, from_slab(): lax.ppermute(x, 'orb', [((i + away) % slabs, i) for i in range(slabs)])  27.9 us
    ppermute x8, starting transfers between devices, from_slab(): lax.ppermute(x, 'orb', [((i + away) % slabs, i) for i in range(slabs)])  21.9 us
    pallas_call x1, Pallas kernels, pair_part(): pl.pallas_call(functools.partial(pair_kernel, z), out_shape=[jax.ShapeDty...  18.4 us
    ppermute x15, starting transfers between devices, swapped(): return lax.ppermute(x, 'group', [(i, i ^ bit) for i in range(groups)])  11.4 us
    pallas_call x1, Pallas kernels, plan(): pl.pallas_call(functools.partial(plan_kernel, z), out_shape=(jax.ShapeDty...  8.8 us
    unnamed x52, local copies, waits for them, and re-layouts  7.94 us
    pallas_call x1, Pallas kernels, local_part(): pl.pallas_call(functools.partial(local_kernel, z, per_step), grid=(z.colo...  6.5 us
  transfers between devices with their start and end apart: 23, of which 10 were waited for; matrix products, arithmetic and copies ran while one was open for 0% of the time, Pallas kernels for 10%

profile of v1, /device:TPU:0, one launch (start us, length us, event | category | flops | bytes accessed | tf_op | source)
XLA Modules:
  0.0 147.5 jit_solution(17075156564454341178)
XLA Ops:
  0.0 1.0 constant_dynamic-slice_fusion
  1.0 5.1 %collective-permute-start.12 = (bf16[24,8,1024]{2,1,0:T(8,128)(2,1)S(1)}, bf16[24,8,1024]{2,1,0:T(8,128)(2,1)S(1)}, u32[]{:S(2)}, u32[]{:S(2)}) collective-permute-start(bf16[24,8,1024]{2,1,0:T(8,128)(2,1)S(1)} %constant_dynamic-slice_fusion), channel_id=1, source_target_pairs={{2,0},{3,1},{4,2},{5,3},{6,4},{7,5},{0,6},{1,7},{10,8},{11,9},{12,... | collective-permute-start | bytes 1179656 | tf_op jit(solution)/shard_map/ppermute | solution.py:435
  6.1 4.8 %collective-permute-start.4 = (bf16[24,8,1024]{2,1,0:T(8,128)(2,1)S(1)}, bf16[24,8,1024]{2,1,0:T(8,128)(2,1)S(1)}, u32[]{:S(2)}, u32[]{:S(2)}) collective-permute-start(bf16[24,8,1024]{2,1,0:T(8,128)(2,1)S(1)} %constant_dynamic-slice_fusion), channel_id=1, source_target_pairs={{1,0},{2,1},{3,2},{4,3},{5,4},{6,5},{7,6},{0,7},{9,8},{10,9},{11,1... | collective-permute-start | bytes 1179656 | tf_op jit(solution)/shard_map/ppermute | solution.py:435
  10.9 4.7 %collective-permute-done.12.rest_12_ = bf16[24,8,1024]{2,1,0:T(8,128)(2,1)S(1)} collective-permute-done((bf16[24,8,1024]{2,1,0:T(8,128)(2,1)S(1)}, bf16[24,8,1024]{2,1,0:T(8,128)(2,1)S(1)}, u32[]{:S(2)}, u32[]{:S(2)}) %collective-permute-start.12) | collective-permute-done | bytes 393248 | tf_op jit(solution)/shard_map/ppermute | solution.py:435
  15.7 1.5 %collective-permute-start.13 = (bf16[24,8,1024]{2,1,0:T(8,128)(2,1)S(1)}, bf16[24,8,1024]{2,1,0:T(8,128)(2,1)}, u32[]{:S(2)}, u32[]{:S(2)}) collective-permute-start(bf16[24,8,1024]{2,1,0:T(8,128)(2,1)S(1)} %collective-permute-done.12.rest_12_), channel_id=1, source_target_pairs={{0,16},{8,24},{16,0},{24,8},{1,17},{9,25},{17,1},{25,9},{2,18},{10... | collective-permute-start | bytes 1179656 | tf_op jit(solution)/shard_map/ppermute | solution.py:439
  17.1 7.9 %collective-permute-done.8.rest_0_ = bf16[24,8,1024]{2,1,0:T(8,128)(2,1)S(1)} collective-permute-done((bf16[24,8,1024]{2,1,0:T(8,128)(2,1)S(1)}, bf16[24,8,1024]{2,1,0:T(8,128)(2,1)S(1)}, u32[]{:S(2)}, u32[]{:S(2)}) %collective-permute-start.8) | collective-permute-done | bytes 393248 | tf_op jit(solution)/shard_map/ppermute | solution.py:435
  25.0 6.4 %collective-permute-done.4.rest_4_.rest_8_ = bf16[24,8,1024]{2,1,0:T(8,128)(2,1)S(1)} collective-permute-done((bf16[24,8,1024]{2,1,0:T(8,128)(2,1)S(1)}, bf16[24,8,1024]{2,1,0:T(8,128)(2,1)S(1)}, u32[]{:S(2)}, u32[]{:S(2)}) %collective-permute-start.4) | collective-permute-done | bytes 393248 | tf_op jit(solution)/shard_map/ppermute | solution.py:435
  31.4 1.5 %collective-permute-start.9 = (bf16[24,8,1024]{2,1,0:T(8,128)(2,1)S(1)}, bf16[24,8,1024]{2,1,0:T(8,128)(2,1)}, u32[]{:S(2)}, u32[]{:S(2)}) collective-permute-start(bf16[24,8,1024]{2,1,0:T(8,128)(2,1)S(1)} %collective-permute-done.8.rest_0_), channel_id=1, source_target_pairs={{0,16},{8,24},{16,0},{24,8},{1,17},{9,25},{17,1},{25,9},{2,18},{10... | collective-permute-start | bytes 1179656 | tf_op jit(solution)/shard_map/ppermute | solution.py:439
  33.2 1.6 %collective-permute-start.5 = (bf16[24,8,1024]{2,1,0:T(8,128)(2,1)S(1)}, bf16[24,8,1024]{2,1,0:T(8,128)(2,1)S(1)}, u32[]{:S(2)}, u32[]{:S(2)}) collective-permute-start(bf16[24,8,1024]{2,1,0:T(8,128)(2,1)S(1)} %collective-permute-done.4.rest_4_.rest_8_), channel_id=1, source_target_pairs={{0,16},{8,24},{16,0},{24,8},{1,17},{9,25},{17,1},{25,9},{2,18},{10... | collective-permute-start | bytes 1179656 | tf_op jit(solution)/shard_map/ppermute | solution.py:439
  35.3 8.2 %collective-permute-done.9.rest_1_ = bf16[24,8,1024]{2,1,0:T(8,128)(2,1)} collective-permute-done((bf16[24,8,1024]{2,1,0:T(8,128)(2,1)S(1)}, bf16[24,8,1024]{2,1,0:T(8,128)(2,1)}, u32[]{:S(2)}, u32[]{:S(2)}) %collective-permute-start.9) | collective-permute-done | bytes 393248 | tf_op jit(solution)/shard_map/ppermute | solution.py:439
  44.1 7.8 %collective-permute-done.5.rest_5_.rest_9_ = bf16[24,8,1024]{2,1,0:T(8,128)(2,1)S(1)} collective-permute-done((bf16[24,8,1024]{2,1,0:T(8,128)(2,1)S(1)}, bf16[24,8,1024]{2,1,0:T(8,128)(2,1)S(1)}, u32[]{:S(2)}, u32[]{:S(2)}) %collective-permute-start.5) | collective-permute-done | bytes 393248 | tf_op jit(solution)/shard_map/ppermute | solution.py:439
  51.9 6.4 %collective-permute-done.1.rest_1_.rest_5_ = bf16[24,8,1024]{2,1,0:T(8,128)(2,1)S(1)} collective-permute-done((bf16[24,8,1024]{2,1,0:T(8,128)(2,1)S(1)}, bf16[24,8,1024]{2,1,0:T(8,128)(2,1)S(1)}, u32[]{:S(2)}, u32[]{:S(2)}) %collective-permute-start.1) | collective-permute-done | bytes 393248 | tf_op jit(solution)/shard_map/ppermute | solution.py:439
  59.0 8.8 %plan.1 = (s32[1]{0:T(128)}, s32[4,174]{1,0:T(4,128)}, s32[2,6]{1,0:T(2,128)}, s32[96]{0:T(128)}) custom-call(s32[2]{0:T(128)} %pad_add_fusion.ids, s32[96]{0:T(128)} %shift.3, s32[24,56]{1,0:T(8,128)} %partner.1, s32[24,56]{1,0:T(8,128)} %member.1), custom_call_target="tpu_custom_call" | custom-call | tf_op jit(solution)/shard_map/plan/pallas_call | solution.py:181
  68.8 18.4 %pair_solves.1 = (f32[6,8,1024]{2,1,0:T(8,128)}, f32[6,8,1024]{2,1,0:T(8,128)}, f32[6,8,1024]{2,1,0:T(8,128)}, f32[6,8,1024]{2,1,0:T(8,128)}, f32[6,8,1024]{2,1,0:T(8,128)}) custom-call(s32[2]{0:T(128)} %pad_add_fusion.ids, s32[1]{0:T(128)} %get-tuple-element.15.count, s32[4,174]{1,0:T(4,128)} %get-tuple-element.16.slots, s32[2,6]{1,0:T(2,128)} %get-tuple-element.17.mine, ...), custom_call_target="tpu_custom_call" | custom-call | flops 20000000000 | bytes 16000000 | tf_op jit(solution)/shard_map/pair_solves/pallas_call | solution.py:296
  87.3 3.1 %collective-permute-start.16 = (f32[6,8,1024]{2,1,0:T(8,128)}, f32[6,8,1024]{2,1,0:T(8,128)S(1)}, u32[]{:S(2)}, u32[]{:S(2)}) collective-permute-start(f32[6,8,1024]{2,1,0:T(8,128)} %get-tuple-element.18), channel_id=1, source_target_pairs={{2,0},{3,1},{4,2},{5,3},{6,4},{7,5},{0,6},{1,7},{10,8},{11,9},{12,... | collective-permute-start | bytes 589832 | tf_op jit(solution)/shard_map/ppermute | solution.py:435
  90.3 6.9 %collective-permute-start.17 = (f32[6,8,1024]{2,1,0:T(8,128)}, f32[6,8,1024]{2,1,0:T(8,128)S(1)}, u32[]{:S(2)}, u32[]{:S(2)}) collective-permute-start(f32[6,8,1024]{2,1,0:T(8,128)} %get-tuple-element.19), channel_id=1, source_target_pairs={{6,0},{7,1},{0,2},{1,3},{2,4},{3,5},{4,6},{5,7},{14,8},{15,9},{8,1... | collective-permute-start | bytes 589832 | tf_op jit(solution)/shard_map/ppermute | solution.py:435
  97.2 2.0 %collective-permute-start.19 = (f32[6,8,1024]{2,1,0:T(8,128)}, f32[6,8,1024]{2,1,0:T(8,128)S(1)}, u32[]{:S(2)}, u32[]{:S(2)}) collective-permute-start(f32[6,8,1024]{2,1,0:T(8,128)} %get-tuple-element.22), channel_id=1, source_target_pairs={{7,0},{0,1},{1,2},{2,3},{3,4},{4,5},{5,6},{6,7},{15,8},{8,9},{9,10... | collective-permute-start | bytes 589832 | tf_op jit(solution)/shard_map/ppermute | solution.py:435
  99.3 5.1 %collective-permute-done.16 = f32[6,8,1024]{2,1,0:T(8,128)S(1)} collective-permute-done((f32[6,8,1024]{2,1,0:T(8,128)}, f32[6,8,1024]{2,1,0:T(8,128)S(1)}, u32[]{:S(2)}, u32[]{:S(2)}) %collective-permute-start.16) | collective-permute-done | bytes 196640 | tf_op jit(solution)/shard_map/ppermute | solution.py:435
  104.4 3.4 %collective-permute-done.17 = f32[6,8,1024]{2,1,0:T(8,128)S(1)} collective-permute-done((f32[6,8,1024]{2,1,0:T(8,128)}, f32[6,8,1024]{2,1,0:T(8,128)S(1)}, u32[]{:S(2)}, u32[]{:S(2)}) %collective-permute-start.17) | collective-permute-done | bytes 196640 | tf_op jit(solution)/shard_map/ppermute | solution.py:435
  108.9 5.8 %collective-permute-start.20 = (f32[24,8,1024]{2,1,0:T(8,128)S(1)}, f32[24,8,1024]{2,1,0:T(8,128)S(1)}, u32[]{:S(2)}, u32[]{:S(2)}) collective-permute-start(f32[24,8,1024]{2,1,0:T(8,128)S(1)} %pad_maximum_fusion.rest_0_), channel_id=1, source_target_pairs={{0,16},{8,24},{16,0},{24,8},{1,17},{9,25},{17,1},{25,9},{2,18},{10... | collective-permute-start | bytes 2359304 | tf_op jit(solution)/shard_map/ppermute | solution.py:439
  114.7 15.1 %collective-permute-done.20.rest_1_ = f32[24,8,1024]{2,1,0:T(8,128)S(1)} collective-permute-done((f32[24,8,1024]{2,1,0:T(8,128)S(1)}, f32[24,8,1024]{2,1,0:T(8,128)S(1)}, u32[]{:S(2)}, u32[]{:S(2)}) %collective-permute-start.20) | collective-permute-done | bytes 786464 | tf_op jit(solution)/shard_map/ppermute | solution.py:439
  132.8 1.0 copy-done.13
  136.8 6.5 %local.1 = f32[96,8,1024]{2,1,0:T(8,128)S(1)} custom-call(s32[2]{0:T(128)S(1)} %copy-done.1, s32[96]{0:T(128)S(1)} %copy-done.3, bf16[96,8,1024]{2,1,0:T(8,128)(2,1)S(1)} %copy-done, f32[8,1024]{1,0:T(8,128)S(1)} %copy-done.20, bf16[24,8,1024]{2,1,0:T(8,128)(2,1)S(1)} %copy-done.7, bf16[24,8,1024]{2,1,0:T(8,128)(2,1)S(1)} %copy-done.13, ...), custom_call_target="tpu_custom_call" | custom-call | flops 6000000000 | bytes 12000000 | tf_op jit(solution)/shard_map/local/pallas_call | solution.py:372
  143.4 4.2 %finish.1 = f32[96,8,1024]{2,1,0:T(8,128)} custom-call(s32[2]{0:T(128)S(1)} %copy-done.1, s32[96]{0:T(128)S(1)} %copy-done.2, f32[96,8,1024]{2,1,0:T(8,128)S(1)} %local.1, f32[24,8,1024]{2,1,0:T(8,128)S(1)} %pad_maximum_fusion.rest_0_, f32[24,8,1024]{2,1,0:T(8,128)S(1)} %collective-permute-done.20.rest_1_, ...), custom_call_target="tpu_custom_call" | custom-call | tf_op jit(solution)/shard_map/finish/pallas_call | solution.py:417
  (82 shorter events, 10.1 us)
Async XLA Ops:
  1.0 14.6 %collective-permute-start.12 = (bf16[24,8,1024]{2,1,0:T(8,128)(2,1)S(1)}, bf16[24,8,1024]{2,1,0:T(8,128)(2,1)S(1)}, u32[]{:S(2)}, u32[]{:S(2)}) collective-permute-start(bf16[24,8,1024]{2,1,0:T(8,128)(2,1)S(1)} %constant_dynamic-slice_fusion), channel_id=1, source_target_pairs={{2,0},{3,1},{4,2},{5,3},{6,4},{7,5},{0,6},{1,7},{10,8},{11,9},{12,... | collective-permute-start | bytes 1179656 | tf_op jit(solution)/shard_map/ppermute | solution.py:435
  6.1 18.9 %collective-permute-start.8 = (bf16[24,8,1024]{2,1,0:T(8,128)(2,1)S(1)}, bf16[24,8,1024]{2,1,0:T(8,128)(2,1)S(1)}, u32[]{:S(2)}, u32[]{:S(2)}) collective-permute-start(bf16[24,8,1024]{2,1,0:T(8,128)(2,1)S(1)} %constant_dynamic-slice_fusion), channel_id=1, source_target_pairs={{6,0},{7,1},{0,2},{1,3},{2,4},{3,5},{4,6},{5,7},{14,8},{15,9},{8,1... | collective-permute-start | bytes 1179656 | tf_op jit(solution)/shard_map/ppermute | solution.py:435
  6.1 25.3 %collective-permute-start.4 = (bf16[24,8,1024]{2,1,0:T(8,128)(2,1)S(1)}, bf16[24,8,1024]{2,1,0:T(8,128)(2,1)S(1)}, u32[]{:S(2)}, u32[]{:S(2)}) collective-permute-start(bf16[24,8,1024]{2,1,0:T(8,128)(2,1)S(1)} %constant_dynamic-slice_fusion), channel_id=1, source_target_pairs={{1,0},{2,1},{3,2},{4,3},{5,4},{6,5},{7,6},{0,7},{9,8},{10,9},{11,1... | collective-permute-start | bytes 1179656 | tf_op jit(solution)/shard_map/ppermute | solution.py:435
  10.9 22.3 %collective-permute-start = (bf16[24,8,1024]{2,1,0:T(8,128)(2,1)S(1)}, bf16[24,8,1024]{2,1,0:T(8,128)(2,1)S(1)}, u32[]{:S(2)}, u32[]{:S(2)}) collective-permute-start(bf16[24,8,1024]{2,1,0:T(8,128)(2,1)S(1)} %constant_dynamic-slice_fusion), channel_id=1, source_target_pairs={{7,0},{0,1},{1,2},{2,3},{3,4},{4,5},{5,6},{6,7},{15,8},{8,9},{9,10... | collective-permute-start | bytes 1179656 | tf_op jit(solution)/shard_map/ppermute | solution.py:435
  15.7 17.6 %collective-permute-start.14 = (bf16[24,8,1024]{2,1,0:T(8,128)(2,1)S(1)}, bf16[24,8,1024]{2,1,0:T(8,128)(2,1)S(1)}, u32[]{:S(2)}, u32[]{:S(2)}) collective-permute-start(bf16[24,8,1024]{2,1,0:T(8,128)(2,1)S(1)} %collective-permute-done.12.rest_12_), channel_id=1, source_target_pairs={{0,8},{8,0},{16,24},{24,16},{1,9},{9,1},{17,25},{25,17},{2,10},{10... | collective-permute-start | bytes 1179656 | tf_op jit(solution)/shard_map/ppermute | solution.py:439
  15.7 19.1 %collective-permute-start.13 = (bf16[24,8,1024]{2,1,0:T(8,128)(2,1)S(1)}, bf16[24,8,1024]{2,1,0:T(8,128)(2,1)}, u32[]{:S(2)}, u32[]{:S(2)}) collective-permute-start(bf16[24,8,1024]{2,1,0:T(8,128)(2,1)S(1)} %collective-permute-done.12.rest_12_), channel_id=1, source_target_pairs={{0,16},{8,24},{16,0},{24,8},{1,17},{9,25},{17,1},{25,9},{2,18},{10... | collective-permute-start | bytes 1179656 | tf_op jit(solution)/shard_map/ppermute | solution.py:439
  25.0 10.3 %collective-permute-start.10 = (bf16[24,8,1024]{2,1,0:T(8,128)(2,1)S(1)}, bf16[24,8,1024]{2,1,0:T(8,128)(2,1)}, u32[]{:S(2)}, u32[]{:S(2)}) collective-permute-start(bf16[24,8,1024]{2,1,0:T(8,128)(2,1)S(1)} %collective-permute-done.8.rest_0_), channel_id=1, source_target_pairs={{0,8},{8,0},{16,24},{24,16},{1,9},{9,1},{17,25},{25,17},{2,10},{10... | collective-permute-start | bytes 1179656 | tf_op jit(solution)/shard_map/ppermute | solution.py:439
  31.4 12.2 %collective-permute-start.9 = (bf16[24,8,1024]{2,1,0:T(8,128)(2,1)S(1)}, bf16[24,8,1024]{2,1,0:T(8,128)(2,1)}, u32[]{:S(2)}, u32[]{:S(2)}) collective-permute-start(bf16[24,8,1024]{2,1,0:T(8,128)(2,1)S(1)} %collective-permute-done.8.rest_0_), channel_id=1, source_target_pairs={{0,16},{8,24},{16,0},{24,8},{1,17},{9,25},{17,1},{25,9},{2,18},{10... | collective-permute-start | bytes 1179656 | tf_op jit(solution)/shard_map/ppermute | solution.py:439
  33.2 10.3 %collective-permute-start.6 = (bf16[24,8,1024]{2,1,0:T(8,128)(2,1)S(1)}, bf16[24,8,1024]{2,1,0:T(8,128)(2,1)S(1)}, u32[]{:S(2)}, u32[]{:S(2)}) collective-permute-start(bf16[24,8,1024]{2,1,0:T(8,128)(2,1)S(1)} %collective-permute-done.4.rest_4_.rest_8_), channel_id=1, source_target_pairs={{0,8},{8,0},{16,24},{24,16},{1,9},{9,1},{17,25},{25,17},{2,10},{10... | collective-permute-start | bytes 1179656 | tf_op jit(solution)/shard_map/ppermute | solution.py:439
  33.2 18.6 %collective-permute-start.5 = (bf16[24,8,1024]{2,1,0:T(8,128)(2,1)S(1)}, bf16[24,8,1024]{2,1,0:T(8,128)(2,1)S(1)}, u32[]{:S(2)}, u32[]{:S(2)}) collective-permute-start(bf16[24,8,1024]{2,1,0:T(8,128)(2,1)S(1)} %collective-permute-done.4.rest_4_.rest_8_), channel_id=1, source_target_pairs={{0,16},{8,24},{16,0},{24,8},{1,17},{9,25},{17,1},{25,9},{2,18},{10... | collective-permute-start | bytes 1179656 | tf_op jit(solution)/shard_map/ppermute | solution.py:439
  34.8 23.5 %collective-permute-start.1 = (bf16[24,8,1024]{2,1,0:T(8,128)(2,1)S(1)}, bf16[24,8,1024]{2,1,0:T(8,128)(2,1)S(1)}, u32[]{:S(2)}, u32[]{:S(2)}) collective-permute-start(bf16[24,8,1024]{2,1,0:T(8,128)(2,1)S(1)} %collective-permute-done.rest_0_.rest_4_), channel_id=1, source_target_pairs={{0,16},{8,24},{16,0},{24,8},{1,17},{9,25},{17,1},{25,9},{2,18},{10... | collective-permute-start | bytes 1179656 | tf_op jit(solution)/shard_map/ppermute | solution.py:439
  35.3 32.5 %collective-permute-start.2 = (bf16[24,8,1024]{2,1,0:T(8,128)(2,1)S(1)}, bf16[24,8,1024]{2,1,0:T(8,128)(2,1)S(1)}, u32[]{:S(2)}, u32[]{:S(2)}) collective-permute-start(bf16[24,8,1024]{2,1,0:T(8,128)(2,1)S(1)} %collective-permute-done.rest_0_.rest_4_), channel_id=1, source_target_pairs={{0,8},{8,0},{16,24},{24,16},{1,9},{9,1},{17,25},{25,17},{2,10},{10... | collective-permute-start | bytes 1179656 | tf_op jit(solution)/shard_map/ppermute | solution.py:439
  43.6 24.3 %collective-permute-start.15 = (bf16[24,8,1024]{2,1,0:T(8,128)(2,1)}, bf16[24,8,1024]{2,1,0:T(8,128)(2,1)}, u32[]{:S(2)}, u32[]{:S(2)}) collective-permute-start(bf16[24,8,1024]{2,1,0:T(8,128)(2,1)} %collective-permute-done.13.rest_13_), channel_id=1, source_target_pairs={{0,8},{8,0},{16,24},{24,16},{1,9},{9,1},{17,25},{25,17},{2,10},{10... | collective-permute-start | bytes 1179656 | tf_op jit(solution)/shard_map/ppermute | solution.py:439
  43.6 24.3 %collective-permute-start.11 = (bf16[24,8,1024]{2,1,0:T(8,128)(2,1)}, bf16[24,8,1024]{2,1,0:T(8,128)(2,1)}, u32[]{:S(2)}, u32[]{:S(2)}) collective-permute-start(bf16[24,8,1024]{2,1,0:T(8,128)(2,1)} %collective-permute-done.9.rest_1_), channel_id=1, source_target_pairs={{0,8},{8,0},{16,24},{24,16},{1,9},{9,1},{17,25},{25,17},{2,10},{10... | collective-permute-start | bytes 1179656 | tf_op jit(solution)/shard_map/ppermute | solution.py:439
  51.9 16.0 %collective-permute-start.7 = (bf16[24,8,1024]{2,1,0:T(8,128)(2,1)S(1)}, bf16[24,8,1024]{2,1,0:T(8,128)(2,1)S(1)}, u32[]{:S(2)}, u32[]{:S(2)}) collective-permute-start(bf16[24,8,1024]{2,1,0:T(8,128)(2,1)S(1)} %collective-permute-done.5.rest_5_.rest_9_), channel_id=1, source_target_pairs={{0,8},{8,0},{16,24},{24,16},{1,9},{9,1},{17,25},{25,17},{2,10},{10... | collective-permute-start | bytes 1179656 | tf_op jit(solution)/shard_map/ppermute | solution.py:439
  58.3 9.6 %collective-permute-start.3 = (bf16[24,8,1024]{2,1,0:T(8,128)(2,1)S(1)}, bf16[24,8,1024]{2,1,0:T(8,128)(2,1)S(1)}, u32[]{:S(2)}, u32[]{:S(2)}) collective-permute-start(bf16[24,8,1024]{2,1,0:T(8,128)(2,1)S(1)} %collective-permute-done.1.rest_1_.rest_5_), channel_id=1, source_target_pairs={{0,8},{8,0},{16,24},{24,16},{1,9},{9,1},{17,25},{25,17},{2,10},{10... | collective-permute-start | bytes 1179656 | tf_op jit(solution)/shard_map/ppermute | solution.py:439
  68.8 60.9 %copy-start.22 = (f32[32,8,192]{2,1,0:T(8,128)S(1)}, f32[32,8,192]{2,1,0:T(8,128)}, u32[]{:S(2)}) copy-start(f32[32,8,192]{2,1,0:T(8,128)} %constant.33.clone.rest_9_) | copy-start | bytes 589828
  87.3 17.1 %collective-permute-start.16 = (f32[6,8,1024]{2,1,0:T(8,128)}, f32[6,8,1024]{2,1,0:T(8,128)S(1)}, u32[]{:S(2)}, u32[]{:S(2)}) collective-permute-start(f32[6,8,1024]{2,1,0:T(8,128)} %get-tuple-element.18), channel_id=1, source_target_pairs={{2,0},{3,1},{4,2},{5,3},{6,4},{7,5},{0,6},{1,7},{10,8},{11,9},{12,... | collective-permute-start | bytes 589832 | tf_op jit(solution)/shard_map/ppermute | solution.py:435
  90.3 17.5 %collective-permute-start.17 = (f32[6,8,1024]{2,1,0:T(8,128)}, f32[6,8,1024]{2,1,0:T(8,128)S(1)}, u32[]{:S(2)}, u32[]{:S(2)}) collective-permute-start(f32[6,8,1024]{2,1,0:T(8,128)} %get-tuple-element.19), channel_id=1, source_target_pairs={{6,0},{7,1},{0,2},{1,3},{2,4},{3,5},{4,6},{5,7},{14,8},{15,9},{8,1... | collective-permute-start | bytes 589832 | tf_op jit(solution)/shard_map/ppermute | solution.py:435
  97.2 10.6 %collective-permute-start.18 = (f32[6,8,1024]{2,1,0:T(8,128)}, f32[6,8,1024]{2,1,0:T(8,128)S(1)}, u32[]{:S(2)}, u32[]{:S(2)}) collective-permute-start(f32[6,8,1024]{2,1,0:T(8,128)} %get-tuple-element.20), channel_id=1, source_target_pairs={{1,0},{2,1},{3,2},{4,3},{5,4},{6,5},{7,6},{0,7},{9,8},{10,9},{11,1... | collective-permute-start | bytes 589832 | tf_op jit(solution)/shard_map/ppermute | solution.py:435
  97.2 10.6 %collective-permute-start.19 = (f32[6,8,1024]{2,1,0:T(8,128)}, f32[6,8,1024]{2,1,0:T(8,128)S(1)}, u32[]{:S(2)}, u32[]{:S(2)}) collective-permute-start(f32[6,8,1024]{2,1,0:T(8,128)} %get-tuple-element.22), channel_id=1, source_target_pairs={{7,0},{0,1},{1,2},{2,3},{3,4},{4,5},{5,6},{6,7},{15,8},{8,9},{9,10... | collective-permute-start | bytes 589832 | tf_op jit(solution)/shard_map/ppermute | solution.py:435
  108.9 20.9 %collective-permute-start.20 = (f32[24,8,1024]{2,1,0:T(8,128)S(1)}, f32[24,8,1024]{2,1,0:T(8,128)S(1)}, u32[]{:S(2)}, u32[]{:S(2)}) collective-permute-start(f32[24,8,1024]{2,1,0:T(8,128)S(1)} %pad_maximum_fusion.rest_0_), channel_id=1, source_target_pairs={{0,16},{8,24},{16,0},{24,8},{1,17},{9,25},{17,1},{25,9},{2,18},{10... | collective-permute-start | bytes 2359304 | tf_op jit(solution)/shard_map/ppermute | solution.py:439
  114.7 28.6 %collective-permute-start.21 = (f32[24,8,1024]{2,1,0:T(8,128)S(1)}, f32[24,8,1024]{2,1,0:T(8,128)S(1)}, u32[]{:S(2)}, u32[]{:S(2)}) collective-permute-start(f32[24,8,1024]{2,1,0:T(8,128)S(1)} %pad_maximum_fusion.rest_0_), channel_id=1, source_target_pairs={{0,8},{8,0},{16,24},{24,16},{1,9},{9,1},{17,25},{25,17},{2,10},{10... | collective-permute-start | bytes 2359304 | tf_op jit(solution)/shard_map/ppermute | solution.py:439
  129.8 13.6 %collective-permute-start.22 = (f32[24,8,1024]{2,1,0:T(8,128)S(1)}, f32[24,8,1024]{2,1,0:T(8,128)S(1)}, u32[]{:S(2)}, u32[]{:S(2)}) collective-permute-start(f32[24,8,1024]{2,1,0:T(8,128)S(1)} %collective-permute-done.20.rest_1_), channel_id=1, source_target_pairs={{0,8},{8,0},{16,24},{24,16},{1,9},{9,1},{17,25},{25,17},{2,10},{10... | collective-permute-start | bytes 2359304 | tf_op jit(solution)/shard_map/ppermute | solution.py:439
  (25 other events, 529.1 us)

commit v2 on v1

--- a/solution.py
+++ b/solution.py
@@ -1,5 +1,6 @@
 import functools
 import math
+from typing import NamedTuple
 
 import jax
 import jax.numpy as jnp
@@ -20,9 +21,12 @@
 )
 stencil_reach = 6
 mixing = 0.25
-f32, bf16, i32 = jnp.float32, jnp.bfloat16, jnp.int32
+f32, bf16, i32, i16 = jnp.float32, jnp.bfloat16, jnp.int32, jnp.int16
 kin_colors = 8
 EMPTY = -(1 << 20)
+LANES = 128
+TOP = 32767.0
+STEPS = 256.0
 
 
 def split_np(values):
@@ -62,6 +66,7 @@
         self.own = self.home // groups
         self.frame = self.span * self.rows
         self.batch = max(1, 256 // self.frame)
+        self.planes = self.own + -(-self.own * LANES // self.cells)
         self.cap = -(-self.blocks * self.slots // self.batch) * self.batch + self.batch
 
 
@@ -139,7 +144,8 @@
         filled[cls] = n + 1
         order[cls, n] = c
         back = lax.rem(q - cls + z.slabs * z.width, z.width)
-        src_ref[c] = lax.rem(n, z.groups) * z.width * z.own + back * z.own + n // z.groups
+        src_ref[0, c] = (lax.rem(n, z.groups) * z.width + back) * z.planes
+        src_ref[1, c] = n // z.groups
         return 0
 
     lax.fori_loop(0, z.colors, color_step, 0)
@@ -184,32 +190,55 @@
             jax.ShapeDtypeStruct((1,), i32),
             jax.ShapeDtypeStruct((4, z.cap), i32),
             jax.ShapeDtypeStruct((2, z.own), i32),
-            jax.ShapeDtypeStruct((z.colors,), i32),
+            jax.ShapeDtypeStruct((2, z.colors), i32),
         ),
         in_specs=[smem] * 4,
         out_specs=(smem,) * 4,
         scratch_shapes=[pltpu.SMEM((z.width, z.colors), i32), pltpu.SMEM((z.width,), i32)],
+        cost_estimate=pl.CostEstimate(flops=10_000_000_000, bytes_accessed=100_000, transcendentals=0),
         name="plan",
     )(ids, shift, partner, member)
 
 
-def pair_kernel(z, ids, count, slots, mine, here, *rest):
-    pieces, rest = rest[: (z.span - 1) * z.groups], rest[(z.span - 1) * z.groups :]
+class Piece(NamedTuple):
+    even: int
+    odd: int
+    flip: int
+    parts: int
+    unit: int
+    add: int
+    size: int
+
+    def slab(self, q):
+        return jnp.where(lax.rem(q, 2) == 0, self.even, self.odd)
+
+    def colors(self, g):
+        return pl.ds(lax.rem(g ^ self.flip, self.parts) * self.unit + self.add, self.size)
+
+
+def scale_of(code):
+    return jnp.exp2(code.astype(f32) * (1.0 / STEPS)) * (1.0 / TOP)
+
+
+def coded(x):
+    groups = [x[:, i : i + LANES] for i in range(0, x.shape[1], LANES)]
+    top = functools.reduce(jnp.maximum, [jnp.abs(v) for v in groups])
+    code = jnp.ceil(jnp.log2(jnp.clip(top, 2.0**-100, 2.0**100)) * STEPS) + 1.0
+    factor = 1.0 / scale_of(code)
+    whole = [jnp.clip(jnp.round(v * factor), -TOP, TOP).astype(i32) for v in groups]
+    return jnp.concatenate(whole, axis=1), jnp.where(top > 0, code, 0.0).astype(i32)
+
+
+def pair_kernel(z, layout, ids, count, slots, mine, here, *rest):
+    pieces, rest = rest[: len(layout)], rest[len(layout) :]
     (regroup, ungroup, forward, backward, scale, into, back), rest = rest[:7], rest[7:]
     outs, rest = rest[: z.span], rest[z.span :]
     window, raw, own, held, acc, sems = rest
-    g = ids[1]
-    order = butterfly_order(z.groups)
+    q, g = ids[0], ids[1]
     copies = [pltpu.make_async_copy(here, window.at[z.mid], sems.at[0])]
-    for k in range(z.span - 1):
-        slab = k if k < z.mid else k + 1
-        for p in range(z.groups):
-            at = (g ^ order[p]) * z.part
-            copies.append(
-                pltpu.make_async_copy(
-                    pieces[k * z.groups + p], window.at[slab, pl.ds(at, z.part)], sems.at[len(copies)]
-                )
-            )
+    for piece, ref in zip(layout, pieces):
+        to = window.at[piece.slab(q), piece.colors(g)]
+        copies.append(pltpu.make_async_copy(ref, to, sems.at[len(copies)]))
     for c in copies:
         c.start()
     acc[...] = jnp.zeros_like(acc)
@@ -270,23 +299,24 @@
         field = jnp.concatenate([a + c, a - c, b_ + d, b_ - d], axis=1)
         v = dot3(split2(jnp.concatenate(lhs_back, 0)), split2(field))
         for i in range(batch):
-            m = slots[0, first + i]
+            at = pl.ds(slots[0, first + i] * frame, frame)
             lo = i * frame
-            acc[m] = acc[m] + v[lo : lo + frame] * held[lo : lo + frame]
+            acc[at, :] = acc[at, :] + v[lo : lo + frame] * held[lo : lo + frame]
         return 0
 
     lax.fori_loop(0, (count[0] + batch - 1) // batch, step, 0)
+    head, low = split2(acc[...])
+    res = dot(head, ungroup[...]) + dot(low, ungroup[...])
+    values, codes = coded(res)
     for m in range(z.own):
-        x = acc[m]
-        one = x.astype(bf16)
-        left = x - one.astype(f32)
-        two, three = split2(left)
-        res = dot(one, ungroup[...]) + (dot(two, ungroup[...]) + dot(three, ungroup[...]))
         for k in range(z.span):
-            outs[k][m] = res[k * z.rows : (k + 1) * z.rows]
-
-
-def pair_part(z, ids, count, slots, mine, here, pieces):
+            at = m * frame + k * z.rows
+            outs[k][m] = values[at : at + z.rows].astype(i16)
+            plane, lane = z.own + m * LANES // z.cells, m * LANES % z.cells
+            outs[k][plane, :, lane : lane + LANES] = codes[at : at + z.rows].astype(i16)
+
+
+def pair_part(z, ids, count, slots, mine, here, layout, pieces):
     tables = pair_tables(z)
     smem = pl.BlockSpec(memory_space=pltpu.SMEM)
     vmem = pl.BlockSpec(memory_space=pltpu.VMEM)
@@ -294,8 +324,8 @@
     names = ("regroup", "ungroup", "forward", "backward", "scale", "into", "back")
     wide = z.batch * z.frame
     return pl.pallas_call(
-        functools.partial(pair_kernel, z),
-        out_shape=[jax.ShapeDtypeStruct((z.own, z.rows, z.cells), f32)] * z.span,
+        functools.partial(pair_kernel, z, layout),
+        out_shape=[jax.ShapeDtypeStruct((z.planes, z.rows, z.cells), i16)] * z.span,
         in_specs=[smem] * 4 + [hbm] * (1 + len(pieces)) + [vmem] * len(names),
         out_specs=[vmem] * z.span,
         scratch_shapes=[
@@ -303,33 +333,57 @@
             pltpu.VMEM((wide, z.cells), f32),
             pltpu.VMEM((z.own, z.frame, z.cells), f32),
             pltpu.VMEM((wide, z.cells), f32),
-            pltpu.VMEM((z.own, z.frame, z.cells), f32),
+            pltpu.VMEM((z.own * z.frame, z.cells), f32),
             pltpu.SemaphoreType.DMA((1 + len(pieces),)),
         ],
-        compiler_params=pltpu.CompilerParams(vmem_limit_bytes=56 << 20),
+        compiler_params=pltpu.CompilerParams(vmem_limit_bytes=34 << 20),
         cost_estimate=pl.CostEstimate(flops=20_000_000_000, bytes_accessed=16_000_000, transcendentals=0),
         name="pair_solves",
     )(ids, count, slots, mine, here, *pieces, *[jnp.asarray(tables[n]) for n in names])
 
 
-def local_kernel(z, per_step, ids, shift, here, potential, *rest):
-    pieces, rest = rest[: 2 * z.groups], rest[2 * z.groups :]
-    plane, along, out, near, lhs, sems = rest
+def plane_kernel(z, per_step, here, potential, plane, out):
+    centre = here[...].reshape(per_step * z.rows, z.cells)
+    tile, reach = 256, stencil_reach * z.box
+    cols = []
+    for j in range(0, z.cells, tile):
+        lo, hi = max(0, j - reach) // tile * tile, -(-min(z.cells, j + tile + reach) // tile) * tile
+        u = centre[:, lo:hi]
+        cols.append(dot(u, plane[0, lo:hi, j : j + tile]) + dot(u, plane[1, lo:hi, j : j + tile]))
+    flat = jnp.concatenate(cols, axis=1).reshape(per_step, z.rows, z.cells)
+    out[...] = flat + potential[...][None] * here[...].astype(f32)
+
+
+def plane_part(z, here, potential, plane):
+    per_step = kin_colors * max(d for d in (1, 2, 3, 4) if z.colors // kin_colors % d == 0)
+    block = pl.BlockSpec((per_step, z.rows, z.cells), lambda i: (i, 0, 0))
+    vmem = pl.BlockSpec(memory_space=pltpu.VMEM)
+    return pl.pallas_call(
+        functools.partial(plane_kernel, z, per_step),
+        grid=(z.colors // per_step,),
+        out_shape=jax.ShapeDtypeStruct((z.colors, z.rows, z.cells), f32),
+        in_specs=[block, vmem, vmem],
+        out_specs=block,
+        compiler_params=pltpu.CompilerParams(
+            vmem_limit_bytes=16 << 20, dimension_semantics=("arbitrary",)
+        ),
+        cost_estimate=pl.CostEstimate(flops=6_000_000_000, bytes_accessed=12_000_000, transcendentals=0),
+        name="plane",
+    )(here, potential, plane)
+
+
+def along_kernel(z, per_step, layout, ids, shift, here, flat, *rest):
+    pieces, rest = rest[: len(layout)], rest[len(layout) :]
+    along, out, near, lhs, sems = rest
     q, g = ids[0], ids[1]
-    order = butterfly_order(z.groups)
     step = pl.program_id(0)
 
     @pl.when(step == 0)
     def _():
         copies = []
-        for s in range(2):
-            for p in range(z.groups):
-                at = (g ^ order[p]) * z.part
-                copies.append(
-                    pltpu.make_async_copy(
-                        pieces[s * z.groups + p], near.at[s, pl.ds(at, z.part)], sems.at[len(copies)]
-                    )
-                )
+        for piece, ref in zip(layout, pieces):
+            to = near.at[(piece.slab(q) > z.mid).astype(i32), piece.colors(g)]
+            copies.append(pltpu.make_async_copy(ref, to, sems.at[len(copies)]))
         for c in copies:
             c.start()
         for c in copies:
@@ -337,43 +391,31 @@
 
     rows, cells, kc = z.rows, z.cells, kin_colors
     lane = lax.broadcasted_iota(i32, (rows, 3 * kc * rows), 1)
-    centre = here[...].reshape(per_step * rows, cells)
-    tile = 256
-    cols = []
-    for j in range(0, cells, tile):
-        lo, hi = max(0, j - stencil_reach * z.box), min(cells, j + tile + stencil_reach * z.box)
-        lo, hi = lo // tile * tile, -(-hi // tile) * tile
-        u = centre[:, lo:hi]
-        cols.append(dot(u, plane[0, lo:hi, j : j + tile]) + dot(u, plane[1, lo:hi, j : j + tile]))
-    flat = jnp.concatenate(cols, axis=1)
-    pot = potential[...]
     for s in range(per_step // kc):
         first = step * per_step + s * kc
         for i in range(kc):
             start = lax.rem(shift[first + i] - q * rows + z.grid, z.box)
             lhs[i * rows : (i + 1) * rows, :] = jnp.where(lane // rows % kc == i, along[start], 0.0)
-        mid = centre[s * kc * rows : (s + 1) * kc * rows]
+        mid = here[s * kc : (s + 1) * kc].reshape(kc * rows, cells)
         before = near[0, pl.ds(first, kc)].reshape(kc * rows, cells)
         after = near[1, pl.ds(first, kc)].reshape(kc * rows, cells)
         stack = jnp.concatenate([before, mid, after], axis=0)
         head, low = split2(lhs[...])
-        kin = dot(head, stack) + dot(low, stack) + flat[s * kc * rows : (s + 1) * kc * rows]
-        value = kin.reshape(kc, rows, cells) + pot[None] * mid.astype(f32).reshape(kc, rows, cells)
-        out[s * kc : (s + 1) * kc] = value
-
-
-def local_part(z, ids, shift, here, potential, pieces):
-    plane, along = stencil_tables(z)
+        kin = (dot(head, stack) + dot(low, stack)).reshape(kc, rows, cells)
+        out[s * kc : (s + 1) * kc] = flat[s * kc : (s + 1) * kc] + kin
+
+
+def along_part(z, ids, shift, here, flat, layout, pieces, along):
     per_step = kin_colors * max(d for d in (1, 2, 3, 4) if z.colors // kin_colors % d == 0)
     smem = pl.BlockSpec(memory_space=pltpu.SMEM)
     hbm = pl.BlockSpec(memory_space=pl.ANY)
     block = pl.BlockSpec((per_step, z.rows, z.cells), lambda i: (i, 0, 0))
     vmem = pl.BlockSpec(memory_space=pltpu.VMEM)
     return pl.pallas_call(
-        functools.partial(local_kernel, z, per_step),
+        functools.partial(along_kernel, z, per_step, layout),
         grid=(z.colors // per_step,),
         out_shape=jax.ShapeDtypeStruct((z.colors, z.rows, z.cells), f32),
-        in_specs=[smem, smem, block, vmem] + [hbm] * len(pieces) + [vmem] * 2,
+        in_specs=[smem, smem, block, block] + [hbm] * len(pieces) + [vmem],
         out_specs=block,
         scratch_shapes=[
             pltpu.VMEM((2, z.colors, z.rows, z.cells), bf16),
@@ -381,18 +423,18 @@
             pltpu.SemaphoreType.DMA((len(pieces),)),
         ],
         compiler_params=pltpu.CompilerParams(
-            vmem_limit_bytes=40 << 20, dimension_semantics=("arbitrary",)
+            vmem_limit_bytes=16 << 20, dimension_semantics=("arbitrary",)
         ),
-        cost_estimate=pl.CostEstimate(flops=6_000_000_000, bytes_accessed=12_000_000, transcendentals=0),
-        name="local",
-    )(ids, shift, here, potential, *pieces, jnp.asarray(plane), jnp.asarray(along))
+        cost_estimate=pl.CostEstimate(flops=5_000_000_000, bytes_accessed=12_000_000, transcendentals=0),
+        name="along",
+    )(ids, shift, here, flat, *pieces, along)
 
 
 def finish_kernel(z, per_step, ids, src, local, *rest):
     pieces, out, gathered, sems = rest[: z.groups], rest[z.groups], rest[z.groups + 1], rest[z.groups + 2]
     order = butterfly_order(z.groups)
     step = pl.program_id(0)
-    size = z.width * z.own
+    size = z.width * z.planes
 
     @pl.when(step == 0)
     def _():
@@ -406,7 +448,12 @@
             c.wait()
 
     for i in range(per_step):
-        out[i] = local[i] + gathered[src[step * per_step + i]]
+        first, m = src[0, step * per_step + i], src[1, step * per_step + i]
+        at = m * LANES
+        lane = pl.multiple_of(lax.rem(at, z.cells), LANES)
+        scale = scale_of(gathered[first + z.own + at // z.cells, :, pl.ds(lane, LANES)])
+        value = gathered[first + m].astype(f32)
+        out[i] = local[i] + value * jnp.concatenate([scale] * (z.cells // LANES), axis=1)
 
 
 def finish(z, ids, src, local, pieces):
@@ -421,18 +468,22 @@
         in_specs=[smem, smem, block] + [hbm] * len(pieces),
         out_specs=block,
         scratch_shapes=[
-            pltpu.VMEM((z.groups * z.width * z.own, z.rows, z.cells), f32),
+            pltpu.VMEM((z.groups * z.width * z.planes, z.rows, z.cells), i16),
             pltpu.SemaphoreType.DMA((z.groups,)),
         ],
         compiler_params=pltpu.CompilerParams(
-            vmem_limit_bytes=24 << 20, dimension_semantics=("arbitrary",)
+            vmem_limit_bytes=12 << 20, dimension_semantics=("arbitrary",)
         ),
         name="finish",
     )(ids, src, local, *pieces)
 
 
+def moved(x, source, slabs):
+    return lax.ppermute(x, "orb", [(source(i) % slabs, i) for i in range(slabs)])
+
+
 def from_slab(x, away, slabs):
-    return lax.ppermute(x, "orb", [((i + away) % slabs, i) for i in range(slabs)])
+    return moved(x, lambda i: i + away, slabs)
 
 
 def swapped(x, bit, groups):
@@ -447,26 +498,74 @@
     return have
 
 
+def after(x, *others):
+    return lax.optimization_barrier((x, *others))[0]
+
+
+def fetch(z, orbitals, g, early_work, late_work):
+    quarter = lax.dynamic_slice_in_dim(orbitals, g * z.part, z.part, 0)
+    slabs, groups = z.slabs, z.groups
+    layout, pieces = [], []
+
+    def keep(even, odd, flips, have):
+        for flip, x in zip(flips, have):
+            layout.append(Piece(even, odd, flip, groups, z.part, 0, z.part))
+            pieces.append(x)
+
+    quarters = butterfly_order(groups)
+    if z.mid != 2 or slabs % 2 or groups < 2:
+        done = *early_work(), late_work()
+        for k in range(z.span):
+            if k != z.mid:
+                keep(k, k, quarters, shared(from_slab(quarter, k - z.mid, slabs), groups))
+        return layout, pieces, done
+    half, lo, hi = z.colors // 2, z.mid - 2, z.mid + 2
+    chunk = half // 2
+    firsts = [
+        lax.dynamic_slice_in_dim(orbitals, lax.rem(g, 2) * half + i * chunk, chunk, 0) for i in range(2)
+    ]
+    side = [moved(x, lambda i: i + 2 if i % 2 == 0 else i - 2, slabs) for x in firsts]
+    near = moved(quarter, lambda i: i ^ 1, slabs)
+    rest = moved(quarter, lambda i: i - 2 if i % 2 == 0 else i + 2, slabs)
+    done = early_work()
+    flat = late_work()
+    side = [after(x, *done, flat) for x in side]
+    far = [moved(x, lambda i: i ^ 1, slabs) for x in side]
+    keep(lo + 3, lo + 1, quarters, shared(after(near, *done, flat), groups))
+    for i in range(2):
+        for x, even, odd in ((side[i], hi, lo), (far[i], lo + 1, lo + 3)):
+            for flip, y in enumerate((x, swapped(x, 1, groups))):
+                layout.append(Piece(even, odd, flip, 2, half, i * chunk, chunk))
+                pieces.append(y)
+    keep(lo, hi, quarters, shared(after(rest, flat), groups))
+    return layout, pieces, (*done, flat)
+
+
 def body(orbitals, potential, box_shift, pair_partner, pair_member):
     slabs, groups = lax.axis_size("orb"), lax.axis_size("group")
     z = Sizes(orbitals, pair_partner, groups, slabs)
     q, g = lax.axis_index("orb"), lax.axis_index("group")
     ids = jnp.stack([q, g]).astype(i32)
-    mine = lax.dynamic_slice_in_dim(orbitals, g * z.part, z.part, 0)
-    pieces = []
-    for k in range(z.span):
-        if k != z.mid:
-            pieces.append(shared(from_slab(mine, k - z.mid, slabs), groups))
-    count, slots, home, src = plan(z, ids, box_shift, pair_partner, pair_member)
-    local = local_part(
-        z, ids, box_shift, orbitals, potential, pieces[z.mid - 1] + pieces[z.mid]
+    plane, along = [jnp.asarray(t) for t in stencil_tables(z)]
+    layout, pieces, done = fetch(
+        z,
+        orbitals,
+        g,
+        lambda: plan(z, ids, box_shift, pair_partner, pair_member),
+        lambda: plane_part(z, orbitals, potential, plane),
     )
-    spread = pair_part(z, ids, count, slots, home, orbitals, [x for p in pieces for x in p])
+    count, slots, home, src, flat = done
+    beside = [i for i, p in enumerate(layout) if {p.even, p.odd} <= {z.mid - 1, z.mid + 1}]
+    local = along_part(
+        z, ids, box_shift, orbitals, flat, [layout[i] for i in beside], [pieces[i] for i in beside], along
+    )
+    spread = pair_part(z, ids, count, slots, home, orbitals, layout, pieces)
     parts = [
         spread[k] if k == z.mid else from_slab(spread[k], z.mid - k, slabs) for k in range(z.span)
     ]
     parts = [parts[0] + parts[-1]] + parts[1:-1]
-    return finish(z, ids, src, local, shared(jnp.concatenate(parts, axis=0), groups))
+    joined = after(jnp.concatenate(parts, axis=0), local)
+    return finish(z, ids, src, local, shared(joined, groups))
 
 
 def solution(mesh):

time: 150 us -> 107 us (0.71)
  waiting for transfers between devices: 65.4 us -> 40.2 us
  starting transfers between devices: 33.3 us -> 25.7 us
  local copies, waits for them, and re-layouts: 8.96 us -> 4.52 us
  Pallas kernels: 37.8 us -> 33.8 us
    ppermute x15 -> x13, waiting for transfers between devices: 37.5 us -> 23.6 us  [swapped(): return lax.ppermute(x, 'group', [(i, i ^ bit) for i in range(groups)])]
    ppermute x8 -> x10, waiting for transfers between devices: 27.9 us -> 16.6 us  [moved(): lax.ppermute(x, 'orb', [(source(i) % slabs, i) for i in range(slabs)])]
    ppermute x15 -> x13, starting transfers between devices: 11.4 us -> 3.71 us  [swapped(): return lax.ppermute(x, 'group', [(i, i ^ bit) for i in range(groups)])]
    unnamed x52 -> x32, local copies, waits for them, and re-layouts: 7.94 us -> 2.25 us
    pallas_call x2 -> x3, Pallas kernels: 24.9 us -> 19.2 us  [the longest x1 12.2 us: pair_part(): pl.pallas_call(functools.partial(pair_kernel, z, layout), out_shape=[jax....]
    ppermute x8 -> x10, starting transfers between devices: 21.9 us -> 21.9 us  [moved(): lax.ppermute(x, 'orb', [(source(i) % slabs, i) for i in range(slabs)])]
  transfers between devices with their start and end apart: 23 -> 23, of which waited for: 10 -> 12; matrix products, arithmetic and copies ran while one was open for 0% -> 1% of each run, Pallas kernels for 10% -> 15%
where the time goes in v2:
time: 107 us; the launch traced here: 105 us
  waiting for transfers between devices  40.2 us (38%)
  Pallas kernels  33.8 us (32%)
  starting transfers between devices  25.7 us (24%)
  local copies, waits for them, and re-layouts  4.52 us (4%)
    ppermute x13, waiting for transfers between devices, swapped(): return lax.ppermute(x, 'group', [(i, i ^ bit) for i in range(groups)])  23.6 us
    ppermute x10, starting transfers between devices, moved(): lax.ppermute(x, 'orb', [(source(i) % slabs, i) for i in range(slabs)])  21.9 us
    ppermute x10, waiting for transfers between devices, moved(): lax.ppermute(x, 'orb', [(source(i) % slabs, i) for i in range(slabs)])  16.6 us
    pallas_call x1, Pallas kernels, pair_part(): pl.pallas_call(functools.partial(pair_kernel, z, layout), out_shape=[jax....  12.2 us
    pallas_call x1, Pallas kernels, plan(): pl.pallas_call(functools.partial(plan_kernel, z), out_shape=(jax.ShapeDty...  9 us
    pallas_call x1, Pallas kernels, finish(): pl.pallas_call(functools.partial(finish_kernel, z, per_step), grid=(z.col...  5.57 us
    pallas_call x1, Pallas kernels, along_part(): pl.pallas_call(functools.partial(along_kernel, z, per_step, layout), grid...  4.41 us
    ppermute x13, starting transfers between devices, swapped(): return lax.ppermute(x, 'group', [(i, i ^ bit) for i in range(groups)])  3.71 us
  transfers between devices with their start and end apart: 23, of which 12 were waited for; matrix products, arithmetic and copies ran while one was open for 1% of the time, Pallas kernels for 15%

profile of v2, /device:TPU:0, one launch (start us, length us, event | category | flops | bytes accessed | tf_op | source)
XLA Modules:
  0.0 105.1 jit_solution(4214982873610227149)
XLA Ops:
  0.0 2.3 %constant_dynamic-slice_fusion = (bf16[24,8,1024]{2,1,0:T(8,128)(2,1)}, bf16[24,8,1024]{2,1,0:T(8,128)(2,1)}, bf16[24,8,1024]{2,1,0:T(8,128)(2,1)}) fusion(bf16[96,8,1024]{2,1,0:T(8,128)(2,1)} %here.5, s32[]{:T(128)S(6)} %select_n.11, s32[]{:T(128)S(6)} %select_n.10, s32[]{:T(128)S(6)} %select_n.9), kind=kLoop, calls=%fused_computation.1 | loop fusion | bytes 2359308 | tf_op jit(solution)/shard_map/dynamic_slice | solution.py:525
  2.3 3.0 %collective-permute-start.12 = (bf16[24,8,1024]{2,1,0:T(8,128)(2,1)}, bf16[24,8,1024]{2,1,0:T(8,128)(2,1)S(1)}, u32[]{:S(2)}, u32[]{:S(2)}) collective-permute-start(bf16[24,8,1024]{2,1,0:T(8,128)(2,1)} %get-tuple-element.35), channel_id=1, source_target_pairs={{6,0},{3,1},{0,2},{5,3},{2,4},{7,5},{4,6},{1,7},{14,8},{11,9},{8,1... | collective-permute-start | bytes 1179656 | tf_op jit(solution)/shard_map/ppermute | solution.py:482
  5.3 3.5 %collective-permute-start = (bf16[24,8,1024]{2,1,0:T(8,128)(2,1)}, bf16[24,8,1024]{2,1,0:T(8,128)(2,1)S(1)}, u32[]{:S(2)}, u32[]{:S(2)}) collective-permute-start(bf16[24,8,1024]{2,1,0:T(8,128)(2,1)} %get-tuple-element.35), channel_id=1, source_target_pairs={{1,0},{0,1},{3,2},{2,3},{5,4},{4,5},{7,6},{6,7},{9,8},{8,9},{11,10... | collective-permute-start | bytes 1179656 | tf_op jit(solution)/shard_map/ppermute | solution.py:482
  10.4 9.0 %plan.1 = (s32[1]{0:T(128)}, s32[4,174]{1,0:T(4,128)}, s32[2,6]{1,0:T(2,128)}, s32[2,96]{1,0:T(2,128)}) custom-call(s32[2]{0:T(128)} %pad_add_fusion.1.ids, s32[96]{0:T(128)} %shift.3, s32[24,56]{1,0:T(8,128)} %partner.1, s32[24,56]{1,0:T(8,128)} %member.1), custom_call_target="tpu_custom_call" | custom-call | flops 10000000000 | bytes 100000 | tf_op jit(solution)/shard_map/plan/pallas_call | solution.py:187
  19.4 2.2 %copy-done.5 = bf16[2,1024,1024]{2,1,0:T(8,128)(2,1)S(1)} copy-done((bf16[2,1024,1024]{2,1,0:T(8,128)(2,1)S(1)}, bf16[2,1024,1024]{2,1,0:T(8,128)(2,1)}, u32[]{:S(2)}) %copy-start.5) | copy-done | bytes 4194328
  21.7 2.6 %plane.2.flat = f32[96,8,1024]{2,1,0:T(8,128)S(1)} custom-call(bf16[96,8,1024]{2,1,0:T(8,128)(2,1)S(1)} %copy-done, f32[8,1024]{1,0:T(8,128)S(1)} %copy-done.3, bf16[2,1024,1024]{2,1,0:T(8,128)(2,1)S(1)} %copy-done.5), custom_call_target="tpu_custom_call" | custom-call | flops 6000000000 | bytes 12000000 | tf_op jit(solution)/shard_map/plane/pallas_call | solution.py:361
  24.2 1.0 collective-permute-done.4.rest_4_
  25.3 2.6 %collective-permute-start.5 = (bf16[24,8,1024]{2,1,0:T(8,128)(2,1)S(1)}, bf16[24,8,1024]{2,1,0:T(8,128)(2,1)S(1)}, u32[]{:S(2)}, u32[]{:S(2)}) collective-permute-start(bf16[24,8,1024]{2,1,0:T(8,128)(2,1)S(1)} %collective-permute-done.4.rest_4_), channel_id=1, source_target_pairs={{1,0},{0,1},{3,2},{2,3},{5,4},{4,5},{7,6},{6,7},{9,8},{8,9},{11,10... | collective-permute-start | bytes 1179656 | tf_op jit(solution)/shard_map/ppermute | solution.py:482
  27.9 5.7 %collective-permute-done.7.rest_8_ = bf16[24,8,1024]{2,1,0:T(8,128)(2,1)S(1)} collective-permute-done((bf16[24,8,1024]{2,1,0:T(8,128)(2,1)}, bf16[24,8,1024]{2,1,0:T(8,128)(2,1)S(1)}, u32[]{:S(2)}, u32[]{:S(2)}) %collective-permute-start.7) | collective-permute-done | bytes 393248 | tf_op jit(solution)/shard_map/ppermute | solution.py:482
  33.6 1.6 %collective-permute-start.8 = (bf16[24,8,1024]{2,1,0:T(8,128)(2,1)S(1)}, bf16[24,8,1024]{2,1,0:T(8,128)(2,1)S(1)}, u32[]{:S(2)}, u32[]{:S(2)}) collective-permute-start(bf16[24,8,1024]{2,1,0:T(8,128)(2,1)S(1)} %collective-permute-done.7.rest_8_), channel_id=1, source_target_pairs={{1,0},{0,1},{3,2},{2,3},{5,4},{4,5},{7,6},{6,7},{9,8},{8,9},{11,10... | collective-permute-start | bytes 1179656 | tf_op jit(solution)/shard_map/ppermute | solution.py:482
  35.2 1.5 %collective-permute-start.13 = (bf16[24,8,1024]{2,1,0:T(8,128)(2,1)S(1)}, bf16[24,8,1024]{2,1,0:T(8,128)(2,1)S(1)}, u32[]{:S(2)}, u32[]{:S(2)}) collective-permute-start(bf16[24,8,1024]{2,1,0:T(8,128)(2,1)S(1)} %collective-permute-done.12.rest_12_), channel_id=1, source_target_pairs={{0,16},{8,24},{16,0},{24,8},{1,17},{9,25},{17,1},{25,9},{2,18},{10... | collective-permute-start | bytes 1179656 | tf_op jit(solution)/shard_map/ppermute | solution.py:490
  37.7 6.9 %collective-permute-done.8.rest_6_.rest_10_ = bf16[24,8,1024]{2,1,0:T(8,128)(2,1)S(1)} collective-permute-done((bf16[24,8,1024]{2,1,0:T(8,128)(2,1)S(1)}, bf16[24,8,1024]{2,1,0:T(8,128)(2,1)S(1)}, u32[]{:S(2)}, u32[]{:S(2)}) %collective-permute-start.8) | collective-permute-done | bytes 393248 | tf_op jit(solution)/shard_map/ppermute | solution.py:482
  44.6 2.6 %collective-permute-done.13.rest_13_ = bf16[24,8,1024]{2,1,0:T(8,128)(2,1)S(1)} collective-permute-done((bf16[24,8,1024]{2,1,0:T(8,128)(2,1)S(1)}, bf16[24,8,1024]{2,1,0:T(8,128)(2,1)S(1)}, u32[]{:S(2)}, u32[]{:S(2)}) %collective-permute-start.13) | collective-permute-done | bytes 393248 | tf_op jit(solution)/shard_map/ppermute | solution.py:490
  47.2 6.1 %collective-permute-done.1.rest_1_ = bf16[24,8,1024]{2,1,0:T(8,128)(2,1)S(1)} collective-permute-done((bf16[24,8,1024]{2,1,0:T(8,128)(2,1)S(1)}, bf16[24,8,1024]{2,1,0:T(8,128)(2,1)S(1)}, u32[]{:S(2)}, u32[]{:S(2)}) %collective-permute-start.1) | collective-permute-done | bytes 393248 | tf_op jit(solution)/shard_map/ppermute | solution.py:490
  54.4 0.7 collective-permute-done.6.rest_5_.rest_7_
  56.8 12.2 %pair_solves.1 = (s16[7,8,1024]{2,1,0:T(8,128)(2,1)S(1)}, s16[7,8,1024]{2,1,0:T(8,128)(2,1)S(1)}, s16[7,8,1024]{2,1,0:T(8,128)(2,1)S(1)}, s16[7,8,1024]{2,1,0:T(8,128)(2,1)S(1)}, s16[7,8,1024]{2,1,0:T(8,128)(2,1)S(1)}) custom-call(s32[2]{0:T(128)S(1)} %copy-done.2, s32[1]{0:T(128)} %get-tuple-element.20.count, s32[4,174]{1,0:T(4,128)S(1)} %copy-done.14, ...), custom_call_target="tpu_custom_call" | custom-call | flops 20000000000 | bytes 16000000 | tf_op jit(solution)/shard_map/pair_solves/pallas_call | solution.py:326
  69.0 1.6 %collective-permute-start.16 = (s16[7,8,1024]{2,1,0:T(8,128)(2,1)S(1)}, s16[7,8,1024]{2,1,0:T(8,128)(2,1)S(1)}, u32[]{:S(2)}, u32[]{:S(2)}) collective-permute-start(s16[7,8,1024]{2,1,0:T(8,128)(2,1)S(1)} %get-tuple-element.27), channel_id=1, source_target_pairs={{2,0},{3,1},{4,2},{5,3},{6,4},{7,5},{0,6},{1,7},{10,8},{11,9},{12,... | collective-permute-start | bytes 344072 | tf_op jit(solution)/shard_map/ppermute | solution.py:482
  70.6 5.6 %collective-permute-start.17 = (s16[7,8,1024]{2,1,0:T(8,128)(2,1)S(1)}, s16[7,8,1024]{2,1,0:T(8,128)(2,1)S(1)}, u32[]{:S(2)}, u32[]{:S(2)}) collective-permute-start(s16[7,8,1024]{2,1,0:T(8,128)(2,1)S(1)} %get-tuple-element.28), channel_id=1, source_target_pairs={{6,0},{7,1},{0,2},{1,3},{2,4},{3,5},{4,6},{5,7},{14,8},{15,9},{8,1... | collective-permute-start | bytes 344072 | tf_op jit(solution)/shard_map/ppermute | solution.py:482
  76.2 3.1 %collective-permute-start.18 = (s16[7,8,1024]{2,1,0:T(8,128)(2,1)S(1)}, s16[7,8,1024]{2,1,0:T(8,128)(2,1)S(1)}, u32[]{:S(2)}, u32[]{:S(2)}) collective-permute-start(s16[7,8,1024]{2,1,0:T(8,128)(2,1)S(1)} %get-tuple-element.29), channel_id=1, source_target_pairs={{1,0},{2,1},{3,2},{4,3},{5,4},{6,5},{7,6},{0,7},{9,8},{10,9},{11,1... | collective-permute-start | bytes 344072 | tf_op jit(solution)/shard_map/ppermute | solution.py:482
  79.3 4.4 %along.1.local = f32[96,8,1024]{2,1,0:T(8,128)S(1)} custom-call(s32[2]{0:T(128)S(1)} %copy-done.2, s32[96]{0:T(128)S(1)} %copy-done.4, bf16[96,8,1024]{2,1,0:T(8,128)(2,1)S(1)} %copy-done, f32[96,8,1024]{2,1,0:T(8,128)S(1)} %plane.2.flat, bf16[24,8,1024]{2,1,0:T(8,128)(2,1)S(1)} %collective-permute-done.rest_0_, ...), custom_call_target="tpu_custom_call" | custom-call | flops 5000000000 | bytes 12000000 | tf_op jit(solution)/shard_map/along/pallas_call | solution.py:414
  83.8 3.0 %collective-permute-done.19 = s16[7,8,1024]{2,1,0:T(8,128)(2,1)S(1)} collective-permute-done((s16[7,8,1024]{2,1,0:T(8,128)(2,1)S(1)}, s16[7,8,1024]{2,1,0:T(8,128)(2,1)S(1)}, u32[]{:S(2)}, u32[]{:S(2)}) %collective-permute-start.19) | collective-permute-done | bytes 114720 | tf_op jit(solution)/shard_map/ppermute | solution.py:482
  87.0 10.7 %collective-permute-done.20.rest_1_ = s16[28,8,1024]{2,1,0:T(8,128)(2,1)S(1)} collective-permute-done((s16[28,8,1024]{2,1,0:T(8,128)(2,1)S(1)}, s16[28,8,1024]{2,1,0:T(8,128)(2,1)S(1)}, u32[]{:S(2)}, u32[]{:S(2)}) %collective-permute-start.20) | collective-permute-done | bytes 458784 | tf_op jit(solution)/shard_map/ppermute | solution.py:490
  97.7 1.8 %collective-permute-done.22.rest_3_ = s16[28,8,1024]{2,1,0:T(8,128)(2,1)S(1)} collective-permute-done((s16[28,8,1024]{2,1,0:T(8,128)(2,1)S(1)}, s16[28,8,1024]{2,1,0:T(8,128)(2,1)S(1)}, u32[]{:S(2)}, u32[]{:S(2)}) %collective-permute-start.22) | collective-permute-done | bytes 458784 | tf_op jit(solution)/shard_map/ppermute | solution.py:490
  99.5 5.6 %finish.1 = f32[96,8,1024]{2,1,0:T(8,128)} custom-call(s32[2]{0:T(128)S(1)} %copy-done.2, s32[2,96]{1,0:T(2,128)S(1)} %copy-done.1, f32[96,8,1024]{2,1,0:T(8,128)S(1)} %along.1.local, s16[28,8,1024]{2,1,0:T(8,128)(2,1)S(1)} %pad_add_fusion.rest_0_, s16[28,8,1024]{2,1,0:T(8,128)(2,1)S(1)} %collective-permute-done.20.rest_1_, ...), custom_call_target="tpu_custom_call" | custom-call | tf_op jit(solution)/shard_map/finish/pallas_call | solution.py:464
  (63 shorter events, 5.6 us)
Async XLA Ops:
  2.3 32.9 %collective-permute-start.12 = (bf16[24,8,1024]{2,1,0:T(8,128)(2,1)}, bf16[24,8,1024]{2,1,0:T(8,128)(2,1)S(1)}, u32[]{:S(2)}, u32[]{:S(2)}) collective-permute-start(bf16[24,8,1024]{2,1,0:T(8,128)(2,1)} %get-tuple-element.35), channel_id=1, source_target_pairs={{6,0},{3,1},{0,2},{5,3},{2,4},{7,5},{4,6},{1,7},{14,8},{11,9},{8,1... | collective-permute-start | bytes 1179656 | tf_op jit(solution)/shard_map/ppermute | solution.py:482
  5.3 31.4 %collective-permute-start = (bf16[24,8,1024]{2,1,0:T(8,128)(2,1)}, bf16[24,8,1024]{2,1,0:T(8,128)(2,1)S(1)}, u32[]{:S(2)}, u32[]{:S(2)}) collective-permute-start(bf16[24,8,1024]{2,1,0:T(8,128)(2,1)} %get-tuple-element.35), channel_id=1, source_target_pairs={{1,0},{0,1},{3,2},{2,3},{5,4},{4,5},{7,6},{6,7},{9,8},{8,9},{11,10... | collective-permute-start | bytes 1179656 | tf_op jit(solution)/shard_map/ppermute | solution.py:482
  8.8 16.4 %collective-permute-start.4 = (bf16[24,8,1024]{2,1,0:T(8,128)(2,1)}, bf16[24,8,1024]{2,1,0:T(8,128)(2,1)S(1)}, u32[]{:S(2)}, u32[]{:S(2)}) collective-permute-start(bf16[24,8,1024]{2,1,0:T(8,128)(2,1)} %get-tuple-element.34), channel_id=1, source_target_pairs={{2,0},{7,1},{4,2},{1,3},{6,4},{3,5},{0,6},{5,7},{10,8},{15,9},{12,... | collective-permute-start | bytes 1179656 | tf_op jit(solution)/shard_map/ppermute | solution.py:482
  9.3 24.3 %collective-permute-start.7 = (bf16[24,8,1024]{2,1,0:T(8,128)(2,1)}, bf16[24,8,1024]{2,1,0:T(8,128)(2,1)S(1)}, u32[]{:S(2)}, u32[]{:S(2)}) collective-permute-start(bf16[24,8,1024]{2,1,0:T(8,128)(2,1)} %get-tuple-element.33), channel_id=1, source_target_pairs={{2,0},{7,1},{4,2},{1,3},{6,4},{3,5},{0,6},{5,7},{10,8},{15,9},{12,... | collective-permute-start | bytes 1179656 | tf_op jit(solution)/shard_map/ppermute | solution.py:482
  25.3 54.0 %copy-start.11 = (f32[32,8,192]{2,1,0:T(8,128)S(1)}, f32[32,8,192]{2,1,0:T(8,128)}, u32[]{:S(2)}) copy-start(f32[32,8,192]{2,1,0:T(8,128)} %constant.41.clone.rest_8_) | copy-start | bytes 589828
  25.3 12.0 %collective-permute-start.5 = (bf16[24,8,1024]{2,1,0:T(8,128)(2,1)S(1)}, bf16[24,8,1024]{2,1,0:T(8,128)(2,1)S(1)}, u32[]{:S(2)}, u32[]{:S(2)}) collective-permute-start(bf16[24,8,1024]{2,1,0:T(8,128)(2,1)S(1)} %collective-permute-done.4.rest_4_), channel_id=1, source_target_pairs={{1,0},{0,1},{3,2},{2,3},{5,4},{4,5},{7,6},{6,7},{9,8},{8,9},{11,10... | collective-permute-start | bytes 1179656 | tf_op jit(solution)/shard_map/ppermute | solution.py:482
  33.6 11.0 %collective-permute-start.8 = (bf16[24,8,1024]{2,1,0:T(8,128)(2,1)S(1)}, bf16[24,8,1024]{2,1,0:T(8,128)(2,1)S(1)}, u32[]{:S(2)}, u32[]{:S(2)}) collective-permute-start(bf16[24,8,1024]{2,1,0:T(8,128)(2,1)S(1)} %collective-permute-done.7.rest_8_), channel_id=1, source_target_pairs={{1,0},{0,1},{3,2},{2,3},{5,4},{4,5},{7,6},{6,7},{9,8},{8,9},{11,10... | collective-permute-start | bytes 1179656 | tf_op jit(solution)/shard_map/ppermute | solution.py:482
  35.2 12.1 %collective-permute-start.13 = (bf16[24,8,1024]{2,1,0:T(8,128)(2,1)S(1)}, bf16[24,8,1024]{2,1,0:T(8,128)(2,1)S(1)}, u32[]{:S(2)}, u32[]{:S(2)}) collective-permute-start(bf16[24,8,1024]{2,1,0:T(8,128)(2,1)S(1)} %collective-permute-done.12.rest_12_), channel_id=1, source_target_pairs={{0,16},{8,24},{16,0},{24,8},{1,17},{9,25},{17,1},{25,9},{2,18},{10... | collective-permute-start | bytes 1179656 | tf_op jit(solution)/shard_map/ppermute | solution.py:490
  36.7 16.6 %collective-permute-start.1 = (bf16[24,8,1024]{2,1,0:T(8,128)(2,1)S(1)}, bf16[24,8,1024]{2,1,0:T(8,128)(2,1)S(1)}, u32[]{:S(2)}, u32[]{:S(2)}) collective-permute-start(bf16[24,8,1024]{2,1,0:T(8,128)(2,1)S(1)} %collective-permute-done.rest_0_), channel_id=1, source_target_pairs={{0,16},{8,24},{16,0},{24,8},{1,17},{9,25},{17,1},{25,9},{2,18},{10... | collective-permute-start | bytes 1179656 | tf_op jit(solution)/shard_map/ppermute | solution.py:490
  37.2 16.1 %collective-permute-start.10 = (bf16[24,8,1024]{2,1,0:T(8,128)(2,1)S(1)}, bf16[24,8,1024]{2,1,0:T(8,128)(2,1)S(1)}, u32[]{:S(2)}, u32[]{:S(2)}) collective-permute-start(bf16[24,8,1024]{2,1,0:T(8,128)(2,1)S(1)} %collective-permute-done.4.rest_4_), channel_id=1, source_target_pairs={{0,8},{8,0},{16,24},{24,16},{1,9},{9,1},{17,25},{25,17},{2,10},{10... | collective-permute-start | bytes 1179656 | tf_op jit(solution)/shard_map/ppermute | solution.py:490
  37.2 16.6 %collective-permute-start.11 = (bf16[24,8,1024]{2,1,0:T(8,128)(2,1)S(1)}, bf16[24,8,1024]{2,1,0:T(8,128)(2,1)S(1)}, u32[]{:S(2)}, u32[]{:S(2)}) collective-permute-start(bf16[24,8,1024]{2,1,0:T(8,128)(2,1)S(1)} %collective-permute-done.7.rest_8_), channel_id=1, source_target_pairs={{0,8},{8,0},{16,24},{24,16},{1,9},{9,1},{17,25},{25,17},{2,10},{10... | collective-permute-start | bytes 1179656 | tf_op jit(solution)/shard_map/ppermute | solution.py:490
  44.6 9.3 %collective-permute-start.14 = (bf16[24,8,1024]{2,1,0:T(8,128)(2,1)S(1)}, bf16[24,8,1024]{2,1,0:T(8,128)(2,1)S(1)}, u32[]{:S(2)}, u32[]{:S(2)}) collective-permute-start(bf16[24,8,1024]{2,1,0:T(8,128)(2,1)S(1)} %collective-permute-done.12.rest_12_), channel_id=1, source_target_pairs={{0,8},{8,0},{16,24},{24,16},{1,9},{9,1},{17,25},{25,17},{2,10},{10... | collective-permute-start | bytes 1179656 | tf_op jit(solution)/shard_map/ppermute | solution.py:490
  47.2 7.1 %collective-permute-start.2 = (bf16[24,8,1024]{2,1,0:T(8,128)(2,1)S(1)}, bf16[24,8,1024]{2,1,0:T(8,128)(2,1)S(1)}, u32[]{:S(2)}, u32[]{:S(2)}) collective-permute-start(bf16[24,8,1024]{2,1,0:T(8,128)(2,1)S(1)} %collective-permute-done.rest_0_), channel_id=1, source_target_pairs={{0,8},{8,0},{16,24},{24,16},{1,9},{9,1},{17,25},{25,17},{2,10},{10... | collective-permute-start | bytes 1179656 | tf_op jit(solution)/shard_map/ppermute | solution.py:490
  53.3 1.7 %collective-permute-start.6 = (bf16[24,8,1024]{2,1,0:T(8,128)(2,1)S(1)}, bf16[24,8,1024]{2,1,0:T(8,128)(2,1)S(1)}, u32[]{:S(2)}, u32[]{:S(2)}) collective-permute-start(bf16[24,8,1024]{2,1,0:T(8,128)(2,1)S(1)} %collective-permute-done.5.rest_4_.rest_6_), channel_id=1, source_target_pairs={{0,8},{8,0},{16,24},{24,16},{1,9},{9,1},{17,25},{25,17},{2,10},{10... | collective-permute-start | bytes 1179656 | tf_op jit(solution)/shard_map/ppermute | solution.py:490
  53.3 2.3 %collective-permute-start.9 = (bf16[24,8,1024]{2,1,0:T(8,128)(2,1)S(1)}, bf16[24,8,1024]{2,1,0:T(8,128)(2,1)S(1)}, u32[]{:S(2)}, u32[]{:S(2)}) collective-permute-start(bf16[24,8,1024]{2,1,0:T(8,128)(2,1)S(1)} %collective-permute-done.8.rest_6_.rest_10_), channel_id=1, source_target_pairs={{0,8},{8,0},{16,24},{24,16},{1,9},{9,1},{17,25},{25,17},{2,10},{10... | collective-permute-start | bytes 1179656 | tf_op jit(solution)/shard_map/ppermute | solution.py:490
  53.8 2.3 %collective-permute-start.15 = (bf16[24,8,1024]{2,1,0:T(8,128)(2,1)S(1)}, bf16[24,8,1024]{2,1,0:T(8,128)(2,1)S(1)}, u32[]{:S(2)}, u32[]{:S(2)}) collective-permute-start(bf16[24,8,1024]{2,1,0:T(8,128)(2,1)S(1)} %collective-permute-done.13.rest_13_), channel_id=1, source_target_pairs={{0,8},{8,0},{16,24},{24,16},{1,9},{9,1},{17,25},{25,17},{2,10},{10... | collective-permute-start | bytes 1179656 | tf_op jit(solution)/shard_map/ppermute | solution.py:490
  53.9 2.8 %collective-permute-start.3 = (bf16[24,8,1024]{2,1,0:T(8,128)(2,1)S(1)}, bf16[24,8,1024]{2,1,0:T(8,128)(2,1)S(1)}, u32[]{:S(2)}, u32[]{:S(2)}) collective-permute-start(bf16[24,8,1024]{2,1,0:T(8,128)(2,1)S(1)} %collective-permute-done.1.rest_1_), channel_id=1, source_target_pairs={{0,8},{8,0},{16,24},{24,16},{1,9},{9,1},{17,25},{25,17},{2,10},{10... | collective-permute-start | bytes 1179656 | tf_op jit(solution)/shard_map/ppermute | solution.py:490
  69.0 14.7 %collective-permute-start.16 = (s16[7,8,1024]{2,1,0:T(8,128)(2,1)S(1)}, s16[7,8,1024]{2,1,0:T(8,128)(2,1)S(1)}, u32[]{:S(2)}, u32[]{:S(2)}) collective-permute-start(s16[7,8,1024]{2,1,0:T(8,128)(2,1)S(1)} %get-tuple-element.27), channel_id=1, source_target_pairs={{2,0},{3,1},{4,2},{5,3},{6,4},{7,5},{0,6},{1,7},{10,8},{11,9},{12,... | collective-permute-start | bytes 344072 | tf_op jit(solution)/shard_map/ppermute | solution.py:482
  70.6 13.1 %collective-permute-start.17 = (s16[7,8,1024]{2,1,0:T(8,128)(2,1)S(1)}, s16[7,8,1024]{2,1,0:T(8,128)(2,1)S(1)}, u32[]{:S(2)}, u32[]{:S(2)}) collective-permute-start(s16[7,8,1024]{2,1,0:T(8,128)(2,1)S(1)} %get-tuple-element.28), channel_id=1, source_target_pairs={{6,0},{7,1},{0,2},{1,3},{2,4},{3,5},{4,6},{5,7},{14,8},{15,9},{8,1... | collective-permute-start | bytes 344072 | tf_op jit(solution)/shard_map/ppermute | solution.py:482
  76.2 7.6 %collective-permute-start.18 = (s16[7,8,1024]{2,1,0:T(8,128)(2,1)S(1)}, s16[7,8,1024]{2,1,0:T(8,128)(2,1)S(1)}, u32[]{:S(2)}, u32[]{:S(2)}) collective-permute-start(s16[7,8,1024]{2,1,0:T(8,128)(2,1)S(1)} %get-tuple-element.29), channel_id=1, source_target_pairs={{1,0},{2,1},{3,2},{4,3},{5,4},{6,5},{7,6},{0,7},{9,8},{10,9},{11,1... | collective-permute-start | bytes 344072 | tf_op jit(solution)/shard_map/ppermute | solution.py:482
  79.3 7.5 %collective-permute-start.19 = (s16[7,8,1024]{2,1,0:T(8,128)(2,1)S(1)}, s16[7,8,1024]{2,1,0:T(8,128)(2,1)S(1)}, u32[]{:S(2)}, u32[]{:S(2)}) collective-permute-start(s16[7,8,1024]{2,1,0:T(8,128)(2,1)S(1)} %get-tuple-element.31), channel_id=1, source_target_pairs={{7,0},{0,1},{1,2},{2,3},{3,4},{4,5},{5,6},{6,7},{15,8},{8,9},{9,10... | collective-permute-start | bytes 344072 | tf_op jit(solution)/shard_map/ppermute | solution.py:482
  86.8 10.9 %collective-permute-start.20 = (s16[28,8,1024]{2,1,0:T(8,128)(2,1)S(1)}, s16[28,8,1024]{2,1,0:T(8,128)(2,1)S(1)}, u32[]{:S(2)}, u32[]{:S(2)}) collective-permute-start(s16[28,8,1024]{2,1,0:T(8,128)(2,1)S(1)} %pad_add_fusion.rest_0_), channel_id=1, source_target_pairs={{0,16},{8,24},{16,0},{24,8},{1,17},{9,25},{17,1},{25,9},{2,18},{10... | collective-permute-start | bytes 1376264 | tf_op jit(solution)/shard_map/ppermute | solution.py:490
  86.9 10.8 %collective-permute-start.21 = (s16[28,8,1024]{2,1,0:T(8,128)(2,1)S(1)}, s16[28,8,1024]{2,1,0:T(8,128)(2,1)S(1)}, u32[]{:S(2)}, u32[]{:S(2)}) collective-permute-start(s16[28,8,1024]{2,1,0:T(8,128)(2,1)S(1)} %pad_add_fusion.rest_0_), channel_id=1, source_target_pairs={{0,8},{8,0},{16,24},{24,16},{1,9},{9,1},{17,25},{25,17},{2,10},{10... | collective-permute-start | bytes 1376264 | tf_op jit(solution)/shard_map/ppermute | solution.py:490
  97.7 1.8 %collective-permute-start.22 = (s16[28,8,1024]{2,1,0:T(8,128)(2,1)S(1)}, s16[28,8,1024]{2,1,0:T(8,128)(2,1)S(1)}, u32[]{:S(2)}, u32[]{:S(2)}) collective-permute-start(s16[28,8,1024]{2,1,0:T(8,128)(2,1)S(1)} %collective-permute-done.20.rest_1_), channel_id=1, source_target_pairs={{0,8},{8,0},{16,24},{24,16},{1,9},{9,1},{17,25},{25,17},{2,10},{10... | collective-permute-start | bytes 1376264 | tf_op jit(solution)/shard_map/ppermute | solution.py:490
  (15 other events, 446.0 us)

commit v3 on v2

--- a/solution.py
+++ b/solution.py
@@ -45,7 +45,9 @@
 
 
 def dot3(a, b):
-    return dot(a[0], b[0]) + (dot(a[0], b[1]) + dot(a[1], b[0]))
+    rows = a[0].shape[0]
+    both = dot(jnp.concatenate(a, axis=0), b[0])
+    return both[:rows] + (dot(a[0], b[1]) + both[rows:])
 
 
 class Sizes:
@@ -132,7 +134,7 @@
     return split_np(plane), along.astype(np.float32)
 
 
-def plan_kernel(z, ids, shift, partner, member, count_ref, slot_ref, mine_ref, src_ref, order, filled):
+def plan_kernel(z, ids, shift, partner, member, count_ref, slot_ref, mine_ref, dst_ref, order, filled):
     q, g = ids[0], ids[1]
     o = lax.rem(q + z.slabs - z.mid, z.slabs)
     for c in range(z.width):
@@ -144,8 +146,7 @@
         filled[cls] = n + 1
         order[cls, n] = c
         back = lax.rem(q - cls + z.slabs * z.width, z.width)
-        src_ref[0, c] = (lax.rem(n, z.groups) * z.width + back) * z.planes
-        src_ref[1, c] = n // z.groups
+        dst_ref[(lax.rem(n, z.groups) * z.width + back) * z.own + n // z.groups] = c
         return 0
 
     lax.fori_loop(0, z.colors, color_step, 0)
@@ -190,7 +191,7 @@
             jax.ShapeDtypeStruct((1,), i32),
             jax.ShapeDtypeStruct((4, z.cap), i32),
             jax.ShapeDtypeStruct((2, z.own), i32),
-            jax.ShapeDtypeStruct((2, z.colors), i32),
+            jax.ShapeDtypeStruct((z.colors,), i32),
         ),
         in_specs=[smem] * 4,
         out_specs=(smem,) * 4,
@@ -430,52 +431,37 @@
     )(ids, shift, here, flat, *pieces, along)
 
 
-def finish_kernel(z, per_step, ids, src, local, *rest):
-    pieces, out, gathered, sems = rest[: z.groups], rest[z.groups], rest[z.groups + 1], rest[z.groups + 2]
+def finish_kernel(z, spans, ids, dst, local, *rest):
+    parts, (out, total, sem) = rest[:-3], rest[-3:]
     order = butterfly_order(z.groups)
-    step = pl.program_id(0)
-    size = z.width * z.planes
-
-    @pl.when(step == 0)
-    def _():
-        copies = [
-            pltpu.make_async_copy(pieces[p], gathered.at[pl.ds((ids[1] ^ order[p]) * size, size)], sems.at[p])
-            for p in range(z.groups)
-        ]
-        for c in copies:
-            c.start()
-        for c in copies:
-            c.wait()
-
-    for i in range(per_step):
-        first, m = src[0, step * per_step + i], src[1, step * per_step + i]
-        at = m * LANES
-        lane = pl.multiple_of(lax.rem(at, z.cells), LANES)
-        scale = scale_of(gathered[first + z.own + at // z.cells, :, pl.ds(lane, LANES)])
-        value = gathered[first + m].astype(f32)
-        out[i] = local[i] + value * jnp.concatenate([scale] * (z.cells // LANES), axis=1)
-
-
-def finish(z, ids, src, local, pieces):
-    per_step = z.colors // 8 if z.colors % 8 == 0 else 1
+    at = 0
+    for backs in spans:
+        for p in range(z.groups):
+            ref, at = parts[at], at + 1
+            for b, back in enumerate(backs):
+                for m in range(z.own):
+                    c = dst[((ids[1] ^ order[p]) * z.width + back) * z.own + m]
+                    plane, lane = z.own + m * LANES // z.cells, m * LANES % z.cells
+                    scale = scale_of(ref[b * z.planes + plane, :, lane : lane + LANES])
+                    value = ref[b * z.planes + m].astype(f32)
+                    wide = jnp.concatenate([scale] * (z.cells // LANES), axis=1)
+                    total[c] = local[c] + value * wide
+                    pltpu.make_async_copy(total.at[c], out.at[c], sem).start()
+    pltpu.make_async_copy(total, out, sem).wait()
+
+
+def finish(z, ids, dst, local, spans, parts):
     smem = pl.BlockSpec(memory_space=pltpu.SMEM)
-    hbm = pl.BlockSpec(memory_space=pl.ANY)
-    block = pl.BlockSpec((per_step, z.rows, z.cells), lambda i: (i, 0, 0))
+    vmem = pl.BlockSpec(memory_space=pltpu.VMEM)
     return pl.pallas_call(
-        functools.partial(finish_kernel, z, per_step),
-        grid=(z.colors // per_step,),
+        functools.partial(finish_kernel, z, spans),
         out_shape=jax.ShapeDtypeStruct(local.shape, f32),
-        in_specs=[smem, smem, block] + [hbm] * len(pieces),
-        out_specs=block,
-        scratch_shapes=[
-            pltpu.VMEM((z.groups * z.width * z.planes, z.rows, z.cells), i16),
-            pltpu.SemaphoreType.DMA((z.groups,)),
-        ],
-        compiler_params=pltpu.CompilerParams(
-            vmem_limit_bytes=12 << 20, dimension_semantics=("arbitrary",)
-        ),
+        in_specs=[smem, smem, vmem] + [vmem] * len(parts),
+        out_specs=pl.BlockSpec(memory_space=pl.ANY),
+        scratch_shapes=[pltpu.VMEM(local.shape, f32), pltpu.SemaphoreType.DMA],
+        compiler_params=pltpu.CompilerParams(vmem_limit_bytes=16 << 20),
         name="finish",
-    )(ids, src, local, *pieces)
+    )(ids, dst, local, *parts)
 
 
 def moved(x, source, slabs):
@@ -503,41 +489,31 @@
 
 
 def fetch(z, orbitals, g, early_work, late_work):
-    quarter = lax.dynamic_slice_in_dim(orbitals, g * z.part, z.part, 0)
     slabs, groups = z.slabs, z.groups
     layout, pieces = [], []
 
-    def keep(even, odd, flips, have):
-        for flip, x in zip(flips, have):
-            layout.append(Piece(even, odd, flip, groups, z.part, 0, z.part))
-            pieces.append(x)
-
-    quarters = butterfly_order(groups)
     if z.mid != 2 or slabs % 2 or groups < 2:
-        done = *early_work(), late_work()
+        done = *early_work(), late_work(orbitals)
+        quarter = lax.dynamic_slice_in_dim(orbitals, g * z.part, z.part, 0)
         for k in range(z.span):
             if k != z.mid:
-                keep(k, k, quarters, shared(from_slab(quarter, k - z.mid, slabs), groups))
+                pieces += shared(from_slab(quarter, k - z.mid, slabs), groups)
+                layout += [Piece(k, k, flip, groups, z.part, 0, z.part) for flip in butterfly_order(groups)]
         return layout, pieces, done
     half, lo, hi = z.colors // 2, z.mid - 2, z.mid + 2
-    chunk = half // 2
-    firsts = [
-        lax.dynamic_slice_in_dim(orbitals, lax.rem(g, 2) * half + i * chunk, chunk, 0) for i in range(2)
-    ]
-    side = [moved(x, lambda i: i + 2 if i % 2 == 0 else i - 2, slabs) for x in firsts]
-    near = moved(quarter, lambda i: i ^ 1, slabs)
-    rest = moved(quarter, lambda i: i - 2 if i % 2 == 0 else i + 2, slabs)
+    mine = lax.dynamic_slice_in_dim(orbitals, lax.rem(g, 2) * half, half, 0)
+    side = moved(mine, lambda i: i + 2 if i % 2 == 0 else i - 2, slabs)
+    near = moved(mine, lambda i: i ^ 1, slabs)
     done = early_work()
-    flat = late_work()
-    side = [after(x, *done, flat) for x in side]
-    far = [moved(x, lambda i: i ^ 1, slabs) for x in side]
-    keep(lo + 3, lo + 1, quarters, shared(after(near, *done, flat), groups))
-    for i in range(2):
-        for x, even, odd in ((side[i], hi, lo), (far[i], lo + 1, lo + 3)):
-            for flip, y in enumerate((x, swapped(x, 1, groups))):
-                layout.append(Piece(even, odd, flip, 2, half, i * chunk, chunk))
-                pieces.append(y)
-    keep(lo, hi, quarters, shared(after(rest, flat), groups))
+    side = after(side, *done)
+    far = moved(side, lambda i: i ^ 1, slabs)
+    rest = moved(after(mine, side), lambda i: i - 2 if i % 2 == 0 else i + 2, slabs)
+    flat = late_work(after(orbitals, side))
+    far = after(far, flat)
+    for x, even, odd in ((near, lo + 3, lo + 1), (side, hi, lo), (far, lo + 1, lo + 3), (rest, lo, hi)):
+        for flip, y in enumerate((x, swapped(x, 1, groups))):
+            layout.append(Piece(even, odd, flip, 2, half, 0, half))
+            pieces.append(y)
     return layout, pieces, (*done, flat)
 
 
@@ -552,9 +528,9 @@
         orbitals,
         g,
         lambda: plan(z, ids, box_shift, pair_partner, pair_member),
-        lambda: plane_part(z, orbitals, potential, plane),
+        lambda x: plane_part(z, x, potential, plane),
     )
-    count, slots, home, src, flat = done
+    count, slots, home, dst, flat = done
     beside = [i for i, p in enumerate(layout) if {p.even, p.odd} <= {z.mid - 1, z.mid + 1}]
     local = along_part(
         z, ids, box_shift, orbitals, flat, [layout[i] for i in beside], [pieces[i] for i in beside], along
@@ -563,9 +539,12 @@
     parts = [
         spread[k] if k == z.mid else from_slab(spread[k], z.mid - k, slabs) for k in range(z.span)
     ]
-    parts = [parts[0] + parts[-1]] + parts[1:-1]
-    joined = after(jnp.concatenate(parts, axis=0), local)
-    return finish(z, ids, src, local, shared(joined, groups))
+    parts[0] = parts[0] + parts[-1]
+    spans = [(0, z.mid)] + [tuple(k for k in range(1, z.width) if k != z.mid)]
+    shares = [
+        y for ks in spans for y in shared(after(jnp.concatenate([parts[k] for k in ks], axis=0), local), groups)
+    ]
+    return finish(z, ids, dst, local, spans, shares)
 
 
 def solution(mesh):

time: 107 us -> 93.9 us (0.88); the launches traced: 105 us -> 94.8 us
  Pallas kernels: 33.8 us -> 26 us
  waiting for transfers between devices: 40.2 us -> 36.4 us
  starting transfers between devices: 25.7 us -> 27.1 us
    ppermute x13 -> x10, waiting for transfers between devices: 23.6 us -> 10.3 us  [swapped(): return lax.ppermute(x, 'group', [(i, i ^ bit) for i in range(groups)])]
    ppermute x10 -> x8, waiting for transfers between devices: 16.6 us -> 26.1 us  [moved(): lax.ppermute(x, 'orb', [(source(i) % slabs, i) for i in range(slabs)])]
    pallas_call x1, Pallas kernels: 5.57 us -> 2.18 us  [finish(): pl.pallas_call(functools.partial(finish_kernel, z, spans), out_shape=jax....]
    pallas_call x1, Pallas kernels: 12.2 us -> 9.04 us  [pair_part(): pl.pallas_call(functools.partial(pair_kernel, z, layout), out_shape=[jax....]
    ppermute x10 -> x8, starting transfers between devices: 21.9 us -> 23.4 us  [moved(): lax.ppermute(x, 'orb', [(source(i) % slabs, i) for i in range(slabs)])]
    pallas_call x1, Pallas kernels: 4.41 us -> 3.03 us  [along_part(): pl.pallas_call(functools.partial(along_kernel, z, per_step, layout), grid...]
    ppermute x13 -> x10, starting transfers between devices: 3.71 us -> 3.62 us  [swapped(): return lax.ppermute(x, 'group', [(i, i ^ bit) for i in range(groups)])]
  transfers between devices with their start and end apart: 23 -> 18, of which waited for: 12 -> 9; matrix products, arithmetic and copies ran while one was open for 1% -> 1% of each run, Pallas kernels for 15% -> 16%
where the time goes in v3:
time: 93.9 us; the launch traced here: 94.8 us
  waiting for transfers between devices  36.4 us (39%)
  starting transfers between devices  27.1 us (29%)
  Pallas kernels  26 us (28%)
  local copies, waits for them, and re-layouts  4.32 us (5%)
    ppermute x8, waiting for transfers between devices, moved(): lax.ppermute(x, 'orb', [(source(i) % slabs, i) for i in range(slabs)])  26.1 us
    ppermute x8, starting transfers between devices, moved(): lax.ppermute(x, 'orb', [(source(i) % slabs, i) for i in range(slabs)])  23.4 us
    ppermute x10, waiting for transfers between devices, swapped(): return lax.ppermute(x, 'group', [(i, i ^ bit) for i in range(groups)])  10.3 us
    pallas_call x1, Pallas kernels, plan(): pl.pallas_call(functools.partial(plan_kernel, z), out_shape=(jax.ShapeDty...  9.18 us
    pallas_call x1, Pallas kernels, pair_part(): pl.pallas_call(functools.partial(pair_kernel, z, layout), out_shape=[jax....  9.04 us
    ppermute x10, starting transfers between devices, swapped(): return lax.ppermute(x, 'group', [(i, i ^ bit) for i in range(groups)])  3.62 us
    pallas_call x1, Pallas kernels, along_part(): pl.pallas_call(functools.partial(along_kernel, z, per_step, layout), grid...  3.03 us
    pallas_call x1, Pallas kernels, plane_part(): pl.pallas_call(functools.partial(plane_kernel, z, per_step), grid=(z.colo...  2.59 us
  transfers between devices with their start and end apart: 18, of which 9 were waited for; matrix products, arithmetic and copies ran while one was open for 1% of the time, Pallas kernels for 16%

profile of v3, /device:TPU:0, one launch (start us, length us, event | category | flops | bytes accessed | tf_op | source)
XLA Modules:
  0.0 94.8 jit_solution(3587297294487602755)
XLA Ops:
  0.0 2.1 %constant_dynamic-slice_fusion = bf16[48,8,1024]{2,1,0:T(8,128)(2,1)} fusion(bf16[96,8,1024]{2,1,0:T(8,128)(2,1)} %here.4, s32[]{:T(128)S(6)} %select_n.3), kind=kLoop, calls=%fused_computation.3 | loop fusion | bytes 1572868 | tf_op jit(solution)/shard_map/dynamic_slice | solution.py:504
  2.1 3.0 %collective-permute-start.1 = (bf16[48,8,1024]{2,1,0:T(8,128)(2,1)}, bf16[48,8,1024]{2,1,0:T(8,128)(2,1)S(1)}, u32[]{:S(2)}, u32[]{:S(2)}) collective-permute-start(bf16[48,8,1024]{2,1,0:T(8,128)(2,1)} %constant_dynamic-slice_fusion), channel_id=1, source_target_pairs={{1,0},{0,1},{3,2},{2,3},{5,4},{4,5},{7,6},{6,7},{9,8},{8,9},{11,10... | collective-permute-start | bytes 2359304 | tf_op jit(solution)/shard_map/ppermute | solution.py:468
  5.0 3.6 %collective-permute-start = (bf16[48,8,1024]{2,1,0:T(8,128)(2,1)}, bf16[48,8,1024]{2,1,0:T(8,128)(2,1)S(1)}, u32[]{:S(2)}, u32[]{:S(2)}) collective-permute-start(bf16[48,8,1024]{2,1,0:T(8,128)(2,1)} %constant_dynamic-slice_fusion), channel_id=1, source_target_pairs={{2,0},{7,1},{4,2},{1,3},{6,4},{3,5},{0,6},{5,7},{10,8},{15,9},{12,... | collective-permute-start | bytes 2359304 | tf_op jit(solution)/shard_map/ppermute | solution.py:468
  8.6 0.7 pad_add_fusion.2.ids
  9.3 9.2 %plan.1 = (s32[1]{0:T(128)}, s32[4,174]{1,0:T(4,128)}, s32[2,6]{1,0:T(2,128)}, s32[96]{0:T(128)}) custom-call(s32[2]{0:T(128)} %pad_add_fusion.2.ids, s32[96]{0:T(128)} %shift.3, s32[24,56]{1,0:T(8,128)} %partner.1, s32[24,56]{1,0:T(8,128)} %member.1), custom_call_target="tpu_custom_call" | custom-call | flops 10000000000 | bytes 100000 | tf_op jit(solution)/shard_map/plan/pallas_call | solution.py:188
  18.5 7.0 %collective-permute-done.rest_2_ = bf16[48,8,1024]{2,1,0:T(8,128)(2,1)S(1)} collective-permute-done((bf16[48,8,1024]{2,1,0:T(8,128)(2,1)}, bf16[48,8,1024]{2,1,0:T(8,128)(2,1)S(1)}, u32[]{:S(2)}, u32[]{:S(2)}) %collective-permute-start) | collective-permute-done | bytes 786464 | tf_op jit(solution)/shard_map/ppermute | solution.py:468
  25.5 1.2 %collective-permute-start.3 = (bf16[48,8,1024]{2,1,0:T(8,128)(2,1)S(1)}, bf16[48,8,1024]{2,1,0:T(8,128)(2,1)S(1)}, u32[]{:S(2)}, u32[]{:S(2)}) collective-permute-start(bf16[48,8,1024]{2,1,0:T(8,128)(2,1)S(1)} %collective-permute-done.rest_2_), channel_id=1, source_target_pairs={{1,0},{0,1},{3,2},{2,3},{5,4},{4,5},{7,6},{6,7},{9,8},{8,9},{11,10... | collective-permute-start | bytes 2359304 | tf_op jit(solution)/shard_map/ppermute | solution.py:468
  27.2 2.2 %copy-done.5 = bf16[2,1024,1024]{2,1,0:T(8,128)(2,1)S(1)} copy-done((bf16[2,1024,1024]{2,1,0:T(8,128)(2,1)S(1)}, bf16[2,1024,1024]{2,1,0:T(8,128)(2,1)}, u32[]{:S(2)}) %copy-start.5) | copy-done | bytes 4194328
  29.4 2.6 %plane.2.flat = f32[96,8,1024]{2,1,0:T(8,128)S(1)} custom-call(bf16[96,8,1024]{2,1,0:T(8,128)(2,1)S(1)} %copy-done, f32[8,1024]{1,0:T(8,128)S(1)} %copy-done.3, bf16[2,1024,1024]{2,1,0:T(8,128)(2,1)S(1)} %copy-done.5), custom_call_target="tpu_custom_call" | custom-call | flops 6000000000 | bytes 12000000 | tf_op jit(solution)/shard_map/plane/pallas_call | solution.py:362
  32.0 11.5 %collective-permute-done.3.rest_2_.rest_4_ = bf16[48,8,1024]{2,1,0:T(8,128)(2,1)S(1)} collective-permute-done((bf16[48,8,1024]{2,1,0:T(8,128)(2,1)S(1)}, bf16[48,8,1024]{2,1,0:T(8,128)(2,1)S(1)}, u32[]{:S(2)}, u32[]{:S(2)}) %collective-permute-start.3) | collective-permute-done | bytes 786464 | tf_op jit(solution)/shard_map/ppermute | solution.py:468
  43.6 3.2 %collective-permute-done.6.rest_6_ = bf16[48,8,1024]{2,1,0:T(8,128)(2,1)S(1)} collective-permute-done((bf16[48,8,1024]{2,1,0:T(8,128)(2,1)}, bf16[48,8,1024]{2,1,0:T(8,128)(2,1)S(1)}, u32[]{:S(2)}, u32[]{:S(2)}) %collective-permute-start.6) | collective-permute-done | bytes 786464 | tf_op jit(solution)/shard_map/ppermute | solution.py:468
  47.3 1.8 %collective-permute-done.7.rest_7_ = bf16[48,8,1024]{2,1,0:T(8,128)(2,1)S(1)} collective-permute-done((bf16[48,8,1024]{2,1,0:T(8,128)(2,1)S(1)}, bf16[48,8,1024]{2,1,0:T(8,128)(2,1)S(1)}, u32[]{:S(2)}, u32[]{:S(2)}) %collective-permute-start.7) | collective-permute-done | bytes 786464 | tf_op jit(solution)/shard_map/ppermute | solution.py:476
  49.1 1.1 %collective-permute-done.4.rest_3_.rest_5_ = bf16[48,8,1024]{2,1,0:T(8,128)(2,1)S(1)} collective-permute-done((bf16[48,8,1024]{2,1,0:T(8,128)(2,1)S(1)}, bf16[48,8,1024]{2,1,0:T(8,128)(2,1)S(1)}, u32[]{:S(2)}, u32[]{:S(2)}) %collective-permute-start.4) | collective-permute-done | bytes 786464 | tf_op jit(solution)/shard_map/ppermute | solution.py:476
  50.3 9.0 %pair_solves.1 = (s16[7,8,1024]{2,1,0:T(8,128)(2,1)S(1)}, s16[7,8,1024]{2,1,0:T(8,128)(2,1)S(1)}, s16[7,8,1024]{2,1,0:T(8,128)(2,1)S(1)}, s16[7,8,1024]{2,1,0:T(8,128)(2,1)S(1)}, s16[7,8,1024]{2,1,0:T(8,128)(2,1)S(1)}) custom-call(s32[2]{0:T(128)S(1)} %copy-done.1, s32[1]{0:T(128)} %get-tuple-element.21.count, s32[4,174]{1,0:T(4,128)S(1)} %copy-done.14, ...), custom_call_target="tpu_custom_call" | custom-call | flops 20000000000 | bytes 16000000 | tf_op jit(solution)/shard_map/pair_solves/pallas_call | solution.py:327
  59.3 9.0 %collective-permute-start.8 = (s16[7,8,1024]{2,1,0:T(8,128)(2,1)S(1)}, s16[7,8,1024]{2,1,0:T(8,128)(2,1)S(1)}, u32[]{:S(2)}, u32[]{:S(2)}) collective-permute-start(s16[7,8,1024]{2,1,0:T(8,128)(2,1)S(1)} %get-tuple-element.28), channel_id=1, source_target_pairs={{2,0},{3,1},{4,2},{5,3},{6,4},{7,5},{0,6},{1,7},{10,8},{11,9},{12,... | collective-permute-start | bytes 344072 | tf_op jit(solution)/shard_map/ppermute | solution.py:468
  68.3 6.7 %collective-permute-start.13 = (s16[7,8,1024]{2,1,0:T(8,128)(2,1)S(1)}, s16[7,8,1024]{2,1,0:T(8,128)(2,1)S(1)}, u32[]{:S(2)}, u32[]{:S(2)}) collective-permute-start(s16[7,8,1024]{2,1,0:T(8,128)(2,1)S(1)} %get-tuple-element.32), channel_id=1, source_target_pairs={{1,0},{2,1},{3,2},{4,3},{5,4},{6,5},{7,6},{0,7},{9,8},{10,9},{11,1... | collective-permute-start | bytes 344072 | tf_op jit(solution)/shard_map/ppermute | solution.py:468
  75.0 3.0 %along.1.local = f32[96,8,1024]{2,1,0:T(8,128)S(1)} custom-call(s32[2]{0:T(128)S(1)} %copy-done.1, s32[96]{0:T(128)S(1)} %copy-done.4, bf16[96,8,1024]{2,1,0:T(8,128)(2,1)S(1)} %copy-done, f32[96,8,1024]{2,1,0:T(8,128)S(1)} %plane.2.flat, bf16[48,8,1024]{2,1,0:T(8,128)(2,1)S(1)} %collective-permute-done.1.rest_0_, ...), custom_call_target="tpu_custom_call" | custom-call | flops 5000000000 | bytes 12000000 | tf_op jit(solution)/shard_map/along/pallas_call | solution.py:415
  78.2 4.3 %collective-permute-done.14 = s16[7,8,1024]{2,1,0:T(8,128)(2,1)S(1)} collective-permute-done((s16[7,8,1024]{2,1,0:T(8,128)(2,1)S(1)}, s16[7,8,1024]{2,1,0:T(8,128)(2,1)S(1)}, u32[]{:S(2)}, u32[]{:S(2)}) %collective-permute-start.14) | collective-permute-done | bytes 114720 | tf_op jit(solution)/shard_map/ppermute | solution.py:468
  82.6 2.0 %collective-permute-start.10 = (s16[14,8,1024]{2,1,0:T(8,128)(2,1)S(1)}, s16[14,8,1024]{2,1,0:T(8,128)(2,1)S(1)}, u32[]{:S(2)}, u32[]{:S(2)}) collective-permute-start(s16[14,8,1024]{2,1,0:T(8,128)(2,1)S(1)} %pad_add_fusion.rest_0_), channel_id=1, source_target_pairs={{0,16},{8,24},{16,0},{24,8},{1,17},{9,25},{17,1},{25,9},{2,18},{10... | collective-permute-start | bytes 688136 | tf_op jit(solution)/shard_map/ppermute | solution.py:476
  84.6 0.5 collective-permute-start.11
  85.1 3.5 %collective-permute-done.15.rest_5_ = s16[14,8,1024]{2,1,0:T(8,128)(2,1)S(1)} collective-permute-done((s16[14,8,1024]{2,1,0:T(8,128)(2,1)S(1)}, s16[14,8,1024]{2,1,0:T(8,128)(2,1)S(1)}, u32[]{:S(2)}, u32[]{:S(2)}) %collective-permute-start.15) | collective-permute-done | bytes 229408 | tf_op jit(solution)/shard_map/ppermute | solution.py:476
  88.6 2.5 %collective-permute-done.10.rest_1_ = s16[14,8,1024]{2,1,0:T(8,128)(2,1)S(1)} collective-permute-done((s16[14,8,1024]{2,1,0:T(8,128)(2,1)S(1)}, s16[14,8,1024]{2,1,0:T(8,128)(2,1)S(1)}, u32[]{:S(2)}, u32[]{:S(2)}) %collective-permute-start.10) | collective-permute-done | bytes 229408 | tf_op jit(solution)/shard_map/ppermute | solution.py:476
  91.1 1.5 %collective-permute-done.12.rest_3_ = s16[14,8,1024]{2,1,0:T(8,128)(2,1)S(1)} collective-permute-done((s16[14,8,1024]{2,1,0:T(8,128)(2,1)S(1)}, s16[14,8,1024]{2,1,0:T(8,128)(2,1)S(1)}, u32[]{:S(2)}, u32[]{:S(2)}) %collective-permute-start.12) | collective-permute-done | bytes 229408 | tf_op jit(solution)/shard_map/ppermute | solution.py:476
  92.6 2.2 %finish.1 = f32[96,8,1024]{2,1,0:T(8,128)} custom-call(s32[2]{0:T(128)S(1)} %copy-done.1, s32[96]{0:T(128)S(1)} %copy-done.2, f32[96,8,1024]{2,1,0:T(8,128)S(1)} %along.1.local, s16[14,8,1024]{2,1,0:T(8,128)(2,1)S(1)} %pad_add_fusion.rest_0_, s16[14,8,1024]{2,1,0:T(8,128)(2,1)S(1)} %collective-permute-done.10.rest_1_, ...), custom_call_target="tpu_custom_call" | custom-call | tf_op jit(solution)/shard_map/finish/pallas_call | solution.py:456
  (54 shorter events, 1.3 us)
Async XLA Ops:
  2.1 24.6 %collective-permute-start.1 = (bf16[48,8,1024]{2,1,0:T(8,128)(2,1)}, bf16[48,8,1024]{2,1,0:T(8,128)(2,1)S(1)}, u32[]{:S(2)}, u32[]{:S(2)}) collective-permute-start(bf16[48,8,1024]{2,1,0:T(8,128)(2,1)} %constant_dynamic-slice_fusion), channel_id=1, source_target_pairs={{1,0},{0,1},{3,2},{2,3},{5,4},{4,5},{7,6},{6,7},{9,8},{8,9},{11,10... | collective-permute-start | bytes 2359304 | tf_op jit(solution)/shard_map/ppermute | solution.py:468
  5.0 20.4 %collective-permute-start = (bf16[48,8,1024]{2,1,0:T(8,128)(2,1)}, bf16[48,8,1024]{2,1,0:T(8,128)(2,1)S(1)}, u32[]{:S(2)}, u32[]{:S(2)}) collective-permute-start(bf16[48,8,1024]{2,1,0:T(8,128)(2,1)} %constant_dynamic-slice_fusion), channel_id=1, source_target_pairs={{2,0},{7,1},{4,2},{1,3},{6,4},{3,5},{0,6},{5,7},{10,8},{15,9},{12,... | collective-permute-start | bytes 2359304 | tf_op jit(solution)/shard_map/ppermute | solution.py:468
  25.5 24.7 %copy-start.14 = (s32[4,174]{1,0:T(4,128)S(1)}, s32[4,174]{1,0:T(4,128)}, u32[]{:S(2)}) copy-start(s32[4,174]{1,0:T(4,128)} %get-tuple-element.22.slots) | copy-start | bytes 8356
  25.5 24.7 %copy-start.15 = (s32[2,6]{1,0:T(2,128)S(1)}, s32[2,6]{1,0:T(2,128)}, u32[]{:S(2)}) copy-start(s32[2,6]{1,0:T(2,128)} %get-tuple-element.23.mine) | copy-start | bytes 148
  25.5 24.7 %copy-start.1 = (s32[2]{0:T(128)S(1)}, s32[2]{0:T(128)}, u32[]{:S(2)}) copy-start(s32[2]{0:T(128)} %pad_add_fusion.2.ids) | copy-start | bytes 28
  25.5 18.1 %collective-permute-start.3 = (bf16[48,8,1024]{2,1,0:T(8,128)(2,1)S(1)}, bf16[48,8,1024]{2,1,0:T(8,128)(2,1)S(1)}, u32[]{:S(2)}, u32[]{:S(2)}) collective-permute-start(bf16[48,8,1024]{2,1,0:T(8,128)(2,1)S(1)} %collective-permute-done.rest_2_), channel_id=1, source_target_pairs={{1,0},{0,1},{3,2},{2,3},{5,4},{4,5},{7,6},{6,7},{9,8},{8,9},{11,10... | collective-permute-start | bytes 2359304 | tf_op jit(solution)/shard_map/ppermute | solution.py:468
  26.6 20.1 %collective-permute-start.6 = (bf16[48,8,1024]{2,1,0:T(8,128)(2,1)}, bf16[48,8,1024]{2,1,0:T(8,128)(2,1)S(1)}, u32[]{:S(2)}, u32[]{:S(2)}) collective-permute-start(bf16[48,8,1024]{2,1,0:T(8,128)(2,1)} %constant_dynamic-slice_fusion), channel_id=1, source_target_pairs={{6,0},{3,1},{0,2},{5,3},{2,4},{7,5},{4,6},{1,7},{14,8},{11,9},{8,1... | collective-permute-start | bytes 2359304 | tf_op jit(solution)/shard_map/ppermute | solution.py:468
  26.6 20.7 %collective-permute-start.5 = (bf16[48,8,1024]{2,1,0:T(8,128)(2,1)S(1)}, bf16[48,8,1024]{2,1,0:T(8,128)(2,1)S(1)}, u32[]{:S(2)}, u32[]{:S(2)}) collective-permute-start(bf16[48,8,1024]{2,1,0:T(8,128)(2,1)S(1)} %collective-permute-done.rest_2_), channel_id=1, source_target_pairs={{0,8},{8,0},{16,24},{24,16},{1,9},{9,1},{17,25},{25,17},{2,10},{10... | collective-permute-start | bytes 2359304 | tf_op jit(solution)/shard_map/ppermute | solution.py:476
  26.7 20.6 %collective-permute-start.2 = (bf16[48,8,1024]{2,1,0:T(8,128)(2,1)S(1)}, bf16[48,8,1024]{2,1,0:T(8,128)(2,1)S(1)}, u32[]{:S(2)}, u32[]{:S(2)}) collective-permute-start(bf16[48,8,1024]{2,1,0:T(8,128)(2,1)S(1)} %collective-permute-done.1.rest_0_), channel_id=1, source_target_pairs={{0,8},{8,0},{16,24},{24,16},{1,9},{9,1},{17,25},{25,17},{2,10},{10... | collective-permute-start | bytes 2359304 | tf_op jit(solution)/shard_map/ppermute | solution.py:476
  29.4 20.9 %copy-start.10 = (f32[8,40,192]{2,1,0:T(8,128)S(1)}, f32[8,40,192]{2,1,0:T(8,128)}, u32[]{:S(2)}) copy-start(f32[8,40,192]{2,1,0:T(8,128)} %constant.44.clone.rest_14_) | copy-start | bytes 737284
  32.0 43.0 %copy-start.4 = (s32[96]{0:T(128)S(1)}, s32[96]{0:T(128)}, u32[]{:S(2)}) copy-start(s32[96]{0:T(128)} %shift.3) | copy-start | bytes 1156
  32.0 43.0 %copy-start.11 = (f32[32,8,192]{2,1,0:T(8,128)S(1)}, f32[32,8,192]{2,1,0:T(8,128)}, u32[]{:S(2)}) copy-start(f32[32,8,192]{2,1,0:T(8,128)} %constant.37.clone.rest_4_) | copy-start | bytes 589828
  46.8 2.3 %collective-permute-start.7 = (bf16[48,8,1024]{2,1,0:T(8,128)(2,1)S(1)}, bf16[48,8,1024]{2,1,0:T(8,128)(2,1)S(1)}, u32[]{:S(2)}, u32[]{:S(2)}) collective-permute-start(bf16[48,8,1024]{2,1,0:T(8,128)(2,1)S(1)} %collective-permute-done.6.rest_6_), channel_id=1, source_target_pairs={{0,8},{8,0},{16,24},{24,16},{1,9},{9,1},{17,25},{25,17},{2,10},{10... | collective-permute-start | bytes 2359304 | tf_op jit(solution)/shard_map/ppermute | solution.py:476
  46.8 3.4 %collective-permute-start.4 = (bf16[48,8,1024]{2,1,0:T(8,128)(2,1)S(1)}, bf16[48,8,1024]{2,1,0:T(8,128)(2,1)S(1)}, u32[]{:S(2)}, u32[]{:S(2)}) collective-permute-start(bf16[48,8,1024]{2,1,0:T(8,128)(2,1)S(1)} %collective-permute-done.3.rest_2_.rest_4_), channel_id=1, source_target_pairs={{0,8},{8,0},{16,24},{24,16},{1,9},{9,1},{17,25},{25,17},{2,10},{10... | collective-permute-start | bytes 2359304 | tf_op jit(solution)/shard_map/ppermute | solution.py:476
  59.3 18.8 %collective-permute-start.8 = (s16[7,8,1024]{2,1,0:T(8,128)(2,1)S(1)}, s16[7,8,1024]{2,1,0:T(8,128)(2,1)S(1)}, u32[]{:S(2)}, u32[]{:S(2)}) collective-permute-start(s16[7,8,1024]{2,1,0:T(8,128)(2,1)S(1)} %get-tuple-element.28), channel_id=1, source_target_pairs={{2,0},{3,1},{4,2},{5,3},{6,4},{7,5},{0,6},{1,7},{10,8},{11,9},{12,... | collective-permute-start | bytes 344072 | tf_op jit(solution)/shard_map/ppermute | solution.py:468
  68.3 9.8 %collective-permute-start.9 = (s16[7,8,1024]{2,1,0:T(8,128)(2,1)S(1)}, s16[7,8,1024]{2,1,0:T(8,128)(2,1)S(1)}, u32[]{:S(2)}, u32[]{:S(2)}) collective-permute-start(s16[7,8,1024]{2,1,0:T(8,128)(2,1)S(1)} %get-tuple-element.29), channel_id=1, source_target_pairs={{6,0},{7,1},{0,2},{1,3},{2,4},{3,5},{4,6},{5,7},{14,8},{15,9},{8,1... | collective-permute-start | bytes 344072 | tf_op jit(solution)/shard_map/ppermute | solution.py:468
  68.3 9.9 %collective-permute-start.13 = (s16[7,8,1024]{2,1,0:T(8,128)(2,1)S(1)}, s16[7,8,1024]{2,1,0:T(8,128)(2,1)S(1)}, u32[]{:S(2)}, u32[]{:S(2)}) collective-permute-start(s16[7,8,1024]{2,1,0:T(8,128)(2,1)S(1)} %get-tuple-element.32), channel_id=1, source_target_pairs={{1,0},{2,1},{3,2},{4,3},{5,4},{6,5},{7,6},{0,7},{9,8},{10,9},{11,1... | collective-permute-start | bytes 344072 | tf_op jit(solution)/shard_map/ppermute | solution.py:468
  75.0 7.5 %collective-permute-start.14 = (s16[7,8,1024]{2,1,0:T(8,128)(2,1)S(1)}, s16[7,8,1024]{2,1,0:T(8,128)(2,1)S(1)}, u32[]{:S(2)}, u32[]{:S(2)}) collective-permute-start(s16[7,8,1024]{2,1,0:T(8,128)(2,1)S(1)} %get-tuple-element.33), channel_id=1, source_target_pairs={{7,0},{0,1},{1,2},{2,3},{3,4},{4,5},{5,6},{6,7},{15,8},{8,9},{9,10... | collective-permute-start | bytes 344072 | tf_op jit(solution)/shard_map/ppermute | solution.py:468
  82.5 6.1 %collective-permute-start.15 = (s16[14,8,1024]{2,1,0:T(8,128)(2,1)S(1)}, s16[14,8,1024]{2,1,0:T(8,128)(2,1)S(1)}, u32[]{:S(2)}, u32[]{:S(2)}) collective-permute-start(s16[14,8,1024]{2,1,0:T(8,128)(2,1)S(1)} %pad_add_fusion.1.rest_4_), channel_id=1, source_target_pairs={{0,16},{8,24},{16,0},{24,8},{1,17},{9,25},{17,1},{25,9},{2,18},{10... | collective-permute-start | bytes 688136 | tf_op jit(solution)/shard_map/ppermute | solution.py:476
  82.6 8.5 %collective-permute-start.10 = (s16[14,8,1024]{2,1,0:T(8,128)(2,1)S(1)}, s16[14,8,1024]{2,1,0:T(8,128)(2,1)S(1)}, u32[]{:S(2)}, u32[]{:S(2)}) collective-permute-start(s16[14,8,1024]{2,1,0:T(8,128)(2,1)S(1)} %pad_add_fusion.rest_0_), channel_id=1, source_target_pairs={{0,16},{8,24},{16,0},{24,8},{1,17},{9,25},{17,1},{25,9},{2,18},{10... | collective-permute-start | bytes 688136 | tf_op jit(solution)/shard_map/ppermute | solution.py:476
  84.6 6.5 %collective-permute-start.16 = (s16[14,8,1024]{2,1,0:T(8,128)(2,1)S(1)}, s16[14,8,1024]{2,1,0:T(8,128)(2,1)S(1)}, u32[]{:S(2)}, u32[]{:S(2)}) collective-permute-start(s16[14,8,1024]{2,1,0:T(8,128)(2,1)S(1)} %pad_add_fusion.1.rest_4_), channel_id=1, source_target_pairs={{0,8},{8,0},{16,24},{24,16},{1,9},{9,1},{17,25},{25,17},{2,10},{10... | collective-permute-start | bytes 688136 | tf_op jit(solution)/shard_map/ppermute | solution.py:476
  84.6 6.5 %collective-permute-start.11 = (s16[14,8,1024]{2,1,0:T(8,128)(2,1)S(1)}, s16[14,8,1024]{2,1,0:T(8,128)(2,1)S(1)}, u32[]{:S(2)}, u32[]{:S(2)}) collective-permute-start(s16[14,8,1024]{2,1,0:T(8,128)(2,1)S(1)} %pad_add_fusion.rest_0_), channel_id=1, source_target_pairs={{0,8},{8,0},{16,24},{24,16},{1,9},{9,1},{17,25},{25,17},{2,10},{10... | collective-permute-start | bytes 688136 | tf_op jit(solution)/shard_map/ppermute | solution.py:476
  88.6 2.5 %collective-permute-start.17 = (s16[14,8,1024]{2,1,0:T(8,128)(2,1)S(1)}, s16[14,8,1024]{2,1,0:T(8,128)(2,1)S(1)}, u32[]{:S(2)}, u32[]{:S(2)}) collective-permute-start(s16[14,8,1024]{2,1,0:T(8,128)(2,1)S(1)} %collective-permute-done.15.rest_5_), channel_id=1, source_target_pairs={{0,8},{8,0},{16,24},{24,16},{1,9},{9,1},{17,25},{25,17},{2,10},{10... | collective-permute-start | bytes 688136 | tf_op jit(solution)/shard_map/ppermute | solution.py:476
  91.1 1.5 %collective-permute-start.12 = (s16[14,8,1024]{2,1,0:T(8,128)(2,1)S(1)}, s16[14,8,1024]{2,1,0:T(8,128)(2,1)S(1)}, u32[]{:S(2)}, u32[]{:S(2)}) collective-permute-start(s16[14,8,1024]{2,1,0:T(8,128)(2,1)S(1)} %collective-permute-done.10.rest_1_), channel_id=1, source_target_pairs={{0,8},{8,0},{16,24},{24,16},{1,9},{9,1},{17,25},{25,17},{2,10},{10... | collective-permute-start | bytes 688136 | tf_op jit(solution)/shard_map/ppermute | solution.py:476
  (10 other events, 180.7 us)

commit v4 on v3

--- a/solution.py
+++ b/solution.py
@@ -69,6 +69,7 @@
         self.frame = self.span * self.rows
         self.batch = max(1, 256 // self.frame)
         self.planes = self.own + -(-self.own * LANES // self.cells)
+        self.staged = self.mid == 2 and slabs % 2 == 0 and groups >= 2
         self.cap = -(-self.blocks * self.slots // self.batch) * self.batch + self.batch
 
 
@@ -155,10 +156,12 @@
         c = order[home_class, m * z.groups + g]
         mine_ref[0, m] = c
         mine_ref[1, m] = lax.rem(shift[c], z.rows)
-    total = jnp.int32(0)
+    reach_slots = z.slots // (2 * z.width - 1)
+    sign = jnp.where(lax.rem(q, 2) == 0, 1, -1)
+    counts = (jnp.int32(0), jnp.int32(0))
     for t in range(z.blocks):
 
-        def slot_step(p, total, t=t):
+        def slot_step(p, counts, t=t):
             j = partner[o * z.blocks + t, p]
             n = t * z.members + member[o * z.blocks + t, p]
             live = jnp.logical_and(j >= 0, lax.rem(n, z.groups) == g)
@@ -168,19 +171,25 @@
             there = (j - cj * z.per) * z.box + shift[cj]
             d = there - (o * z.rows + sub) + z.grid // 2
             d = lax.rem(d + z.grid, z.grid) - z.grid // 2
-            slot_ref[0, total] = n // z.groups
-            slot_ref[1, total] = cj
-            slot_ref[2, total] = sub + d
-            slot_ref[3, total] = sub
-            return total + live.astype(i32)
-
-        total = lax.fori_loop(0, z.slots, slot_step, total)
-    count_ref[0] = total
-    for i in range(z.batch):
-        slot_ref[0, total + i] = 0
-        slot_ref[1, total + i] = 0
-        slot_ref[2, total + i] = EMPTY
-        slot_ref[3, total + i] = 0
+            reach = (p // reach_slots - (z.width - 1)) * sign
+            first = jnp.logical_and(reach >= z.mid, z.staged).astype(i32)
+            at = jnp.where(first == 1, counts[0], counts[1])
+            slot_ref[first, 0, at] = n // z.groups
+            slot_ref[first, 1, at] = cj
+            slot_ref[first, 2, at] = sub + d
+            slot_ref[first, 3, at] = sub
+            one = live.astype(i32)
+            return counts[0] + one * first, counts[1] + one * (1 - first)
+
+        counts = lax.fori_loop(0, z.slots, slot_step, counts)
+    for first in (0, 1):
+        total = counts[1 - first]
+        count_ref[first] = total
+        for i in range(z.batch):
+            slot_ref[first, 0, total + i] = 0
+            slot_ref[first, 1, total + i] = 0
+            slot_ref[first, 2, total + i] = EMPTY
+            slot_ref[first, 3, total + i] = 0
 
 
 def plan(z, ids, shift, partner, member):
@@ -188,8 +197,8 @@
     return pl.pallas_call(
         functools.partial(plan_kernel, z),
         out_shape=(
-            jax.ShapeDtypeStruct((1,), i32),
-            jax.ShapeDtypeStruct((4, z.cap), i32),
+            jax.ShapeDtypeStruct((2,), i32),
+            jax.ShapeDtypeStruct((2, 4, z.cap), i32),
             jax.ShapeDtypeStruct((2, z.own), i32),
             jax.ShapeDtypeStruct((z.colors,), i32),
         ),
@@ -230,11 +239,16 @@
     return jnp.concatenate(whole, axis=1), jnp.where(top > 0, code, 0.0).astype(i32)
 
 
-def pair_kernel(z, layout, ids, count, slots, mine, here, *rest):
+def pair_kernel(z, first, layout, ids, count, slots, mine, here, *rest):
     pieces, rest = rest[: len(layout)], rest[len(layout) :]
-    (regroup, ungroup, forward, backward, scale, into, back), rest = rest[:7], rest[7:]
-    outs, rest = rest[: z.span], rest[z.span :]
-    window, raw, own, held, acc, sems = rest
+    if not first:
+        sums, rest = rest[0], rest[1:]
+    (regroup, forward, backward, scale, into, back), rest = rest[:6], rest[6:]
+    if first:
+        acc, window, raw, own, held, sems = rest
+    else:
+        ungroup, outs, (window, raw, own, held, acc, sems) = rest[0], rest[1 : z.span + 1], rest[z.span + 1 :]
+    which = 1 if first else 0
     q, g = ids[0], ids[1]
     copies = [pltpu.make_async_copy(here, window.at[z.mid], sems.at[0])]
     for piece, ref in zip(layout, pieces):
@@ -242,7 +256,7 @@
         copies.append(pltpu.make_async_copy(ref, to, sems.at[len(copies)]))
     for c in copies:
         c.start()
-    acc[...] = jnp.zeros_like(acc)
+    acc[...] = jnp.zeros(acc.shape, f32) if first else sums[...]
     for c in copies:
         c.wait()
     frame, box, batch, quad = z.frame, z.box, z.batch, z.cells // 4
@@ -251,26 +265,30 @@
     def regrouped():
         return dot(raw[...].astype(bf16), regroup[...])
 
-    for first in range(0, z.own, batch):
-        todo = min(batch, z.own - first)
+    for start in range(0, z.own, batch):
+        todo = min(batch, z.own - start)
         for i in range(batch):
             for k in range(z.span):
                 at = i * frame + k * z.rows
                 if i < todo:
-                    raw[at : at + z.rows, :] = window[k, mine[0, first + i]].astype(f32)
+                    value = window[k, mine[0, start + i]].astype(f32)
+                    if first and k != z.mid:
+                        here_now = (k > z.mid) == (lax.rem(q, 2) == 0)
+                        value = jnp.where(here_now, value, 0.0)
+                    raw[at : at + z.rows, :] = value
                 else:
                     raw[at : at + z.rows, :] = jnp.zeros((z.rows, z.cells), f32)
         done = regrouped()
         for i in range(todo):
-            own[first + i] = done[i * frame : (i + 1) * frame]
+            own[start + i] = done[i * frame : (i + 1) * frame]
 
     lane_in = lax.broadcasted_iota(i32, (box, batch * frame), 1)
     lane_back = lax.broadcasted_iota(i32, (frame, batch * box), 1)
 
     def step(b, _):
-        first = b * batch
+        base = b * batch
         for i in range(batch):
-            color, start = slots[1, first + i], slots[2, first + i]
+            color, start = slots[which, 1, base + i], slots[which, 2, base + i]
             for k in range(z.span):
                 at = i * frame + k * z.rows
                 r = rows + (k * z.rows - start)
@@ -279,7 +297,7 @@
         held[...] = regrouped()
         lhs_in, lhs_back, density = [], [], []
         for i in range(batch):
-            m, sub = slots[0, first + i], slots[3, first + i]
+            m, sub = slots[which, 0, base + i], slots[which, 3, base + i]
             lo = i * frame
             lhs_in.append(jnp.where((lane_in >= lo) & (lane_in < lo + frame), into[sub], 0.0))
             lo = i * box
@@ -300,12 +318,14 @@
         field = jnp.concatenate([a + c, a - c, b_ + d, b_ - d], axis=1)
         v = dot3(split2(jnp.concatenate(lhs_back, 0)), split2(field))
         for i in range(batch):
-            at = pl.ds(slots[0, first + i] * frame, frame)
+            at = pl.ds(slots[which, 0, base + i] * frame, frame)
             lo = i * frame
             acc[at, :] = acc[at, :] + v[lo : lo + frame] * held[lo : lo + frame]
         return 0
 
-    lax.fori_loop(0, (count[0] + batch - 1) // batch, step, 0)
+    lax.fori_loop(0, (count[which] + batch - 1) // batch, step, 0)
+    if first:
+        return
     head, low = split2(acc[...])
     res = dot(head, ungroup[...]) + dot(low, ungroup[...])
     values, codes = coded(res)
@@ -317,30 +337,37 @@
             outs[k][plane, :, lane : lane + LANES] = codes[at : at + z.rows].astype(i16)
 
 
-def pair_part(z, ids, count, slots, mine, here, layout, pieces):
+def pair_part(z, ids, count, slots, mine, here, layout, pieces, sums=None):
+    first = sums is None
     tables = pair_tables(z)
     smem = pl.BlockSpec(memory_space=pltpu.SMEM)
     vmem = pl.BlockSpec(memory_space=pltpu.VMEM)
     hbm = pl.BlockSpec(memory_space=pl.ANY)
-    names = ("regroup", "ungroup", "forward", "backward", "scale", "into", "back")
-    wide = z.batch * z.frame
+    names = ("regroup", "forward", "backward", "scale", "into", "back") + (() if first else ("ungroup",))
+    wide, total = z.batch * z.frame, (z.own * z.frame, z.cells)
+    if first:
+        given, shapes = [], jax.ShapeDtypeStruct(total, f32)
+    else:
+        given, shapes = [sums], [jax.ShapeDtypeStruct((z.planes, z.rows, z.cells), i16)] * z.span
     return pl.pallas_call(
-        functools.partial(pair_kernel, z, layout),
-        out_shape=[jax.ShapeDtypeStruct((z.planes, z.rows, z.cells), i16)] * z.span,
-        in_specs=[smem] * 4 + [hbm] * (1 + len(pieces)) + [vmem] * len(names),
-        out_specs=[vmem] * z.span,
+        functools.partial(pair_kernel, z, first, layout),
+        out_shape=shapes,
+        in_specs=[smem] * 4 + [hbm] * (1 + len(pieces)) + [vmem] * (len(given) + len(names)),
+        out_specs=vmem if first else [vmem] * z.span,
         scratch_shapes=[
             pltpu.VMEM((z.span, z.colors, z.rows, z.cells), bf16),
             pltpu.VMEM((wide, z.cells), f32),
             pltpu.VMEM((z.own, z.frame, z.cells), f32),
             pltpu.VMEM((wide, z.cells), f32),
-            pltpu.VMEM((z.own * z.frame, z.cells), f32),
+            *([] if first else [pltpu.VMEM(total, f32)]),
             pltpu.SemaphoreType.DMA((1 + len(pieces),)),
         ],
         compiler_params=pltpu.CompilerParams(vmem_limit_bytes=34 << 20),
-        cost_estimate=pl.CostEstimate(flops=20_000_000_000, bytes_accessed=16_000_000, transcendentals=0),
-        name="pair_solves",
-    )(ids, count, slots, mine, here, *pieces, *[jnp.asarray(tables[n]) for n in names])
+        cost_estimate=pl.CostEstimate(
+            flops=8_000_000_000 if first else 20_000_000_000, bytes_accessed=16_000_000, transcendentals=0
+        ),
+        name="first_pairs" if first else "pair_solves",
+    )(ids, count, slots, mine, here, *pieces, *given, *[jnp.asarray(tables[n]) for n in names])
 
 
 def plane_kernel(z, per_step, here, potential, plane, out):
@@ -476,9 +503,11 @@
     return lax.ppermute(x, "group", [(i, i ^ bit) for i in range(groups)])
 
 
-def shared(piece, groups):
+def shared(piece, groups, *others):
     have, step = [piece], groups // 2
     while step:
+        if step == 1 and others:
+            have = [after(x, *others) for x in have]
         have += [swapped(x, step, groups) for x in have]
         step //= 2
     return have
@@ -488,18 +517,20 @@
     return lax.optimization_barrier((x, *others))[0]
 
 
-def fetch(z, orbitals, g, early_work, late_work):
+def fetch(z, orbitals, g, early_work, late_work, first_pairs):
     slabs, groups = z.slabs, z.groups
     layout, pieces = [], []
 
-    if z.mid != 2 or slabs % 2 or groups < 2:
-        done = *early_work(), late_work(orbitals)
+    if not z.staged:
+        done = early_work()
+        flat = late_work(orbitals)
+        sums = first_pairs(done, [], [])
         quarter = lax.dynamic_slice_in_dim(orbitals, g * z.part, z.part, 0)
         for k in range(z.span):
             if k != z.mid:
                 pieces += shared(from_slab(quarter, k - z.mid, slabs), groups)
                 layout += [Piece(k, k, flip, groups, z.part, 0, z.part) for flip in butterfly_order(groups)]
-        return layout, pieces, done
+        return layout, pieces, (*done, flat, sums)
     half, lo, hi = z.colors // 2, z.mid - 2, z.mid + 2
     mine = lax.dynamic_slice_in_dim(orbitals, lax.rem(g, 2) * half, half, 0)
     side = moved(mine, lambda i: i + 2 if i % 2 == 0 else i - 2, slabs)
@@ -509,12 +540,18 @@
     far = moved(side, lambda i: i ^ 1, slabs)
     rest = moved(after(mine, side), lambda i: i - 2 if i % 2 == 0 else i + 2, slabs)
     flat = late_work(after(orbitals, side))
-    far = after(far, flat)
-    for x, even, odd in ((near, lo + 3, lo + 1), (side, hi, lo), (far, lo + 1, lo + 3), (rest, lo, hi)):
+
+    def keep(x, even, odd):
         for flip, y in enumerate((x, swapped(x, 1, groups))):
             layout.append(Piece(even, odd, flip, 2, half, 0, half))
             pieces.append(y)
-    return layout, pieces, (*done, flat)
+
+    keep(near, lo + 3, lo + 1)
+    keep(side, hi, lo)
+    sums = first_pairs(done, list(layout), list(pieces))
+    keep(after(far, flat), lo + 1, lo + 3)
+    keep(after(rest, sums), lo, hi)
+    return layout, pieces, (*done, flat, sums)
 
 
 def body(orbitals, potential, box_shift, pair_partner, pair_member):
@@ -529,22 +566,31 @@
         g,
         lambda: plan(z, ids, box_shift, pair_partner, pair_member),
         lambda x: plane_part(z, x, potential, plane),
+        lambda planned, layout, pieces: pair_part(z, ids, *planned[:3], orbitals, layout, pieces),
     )
-    count, slots, home, dst, flat = done
-    beside = [i for i, p in enumerate(layout) if {p.even, p.odd} <= {z.mid - 1, z.mid + 1}]
-    local = along_part(
-        z, ids, box_shift, orbitals, flat, [layout[i] for i in beside], [pieces[i] for i in beside], along
-    )
-    spread = pair_part(z, ids, count, slots, home, orbitals, layout, pieces)
+    count, slots, home, dst, flat, sums = done
+    spread = pair_part(z, ids, count, slots, home, orbitals, layout, pieces, sums)
     parts = [
         spread[k] if k == z.mid else from_slab(spread[k], z.mid - k, slabs) for k in range(z.span)
     ]
     parts[0] = parts[0] + parts[-1]
-    spans = [(0, z.mid)] + [tuple(k for k in range(1, z.width) if k != z.mid)]
-    shares = [
-        y for ks in spans for y in shared(after(jnp.concatenate([parts[k] for k in ks], axis=0), local), groups)
-    ]
-    return finish(z, ids, dst, local, spans, shares)
+    spans = [(z.mid,), tuple(range(z.mid + 1, z.width)), tuple(range(z.mid))]
+    middle = shared(parts[z.mid], groups)
+    near = jnp.concatenate([parts[k] for k in spans[1]], axis=0)
+    beside = [i for i, p in enumerate(layout) if {p.even, p.odd} <= {z.mid - 1, z.mid + 1}]
+    local = along_part(
+        z,
+        ids,
+        box_shift,
+        orbitals,
+        after(flat, near),
+        [layout[i] for i in beside],
+        [pieces[i] for i in beside],
+        along,
+    )
+    far = jnp.concatenate([parts[k] for k in spans[2]], axis=0)
+    near, far = shared(near, groups), shared(far, groups, local)
+    return finish(z, ids, dst, local, spans, middle + near + far)
 
 
 def solution(mesh):

time: 93.9 us -> 88.8 us (0.946); the launches traced: 94.8 us -> 88.7 us
  waiting for transfers between devices: 36.4 us -> 26.6 us
  Pallas kernels: 26 us -> 31.4 us
  starting transfers between devices: 27.1 us -> 25.4 us
    ppermute x8, waiting for transfers between devices: 26.1 us -> 17.6 us  [moved(): lax.ppermute(x, 'orb', [(source(i) % slabs, i) for i in range(slabs)])]
    ppermute x8, starting transfers between devices: 23.4 us -> 16.3 us  [moved(): lax.ppermute(x, 'orb', [(source(i) % slabs, i) for i in range(slabs)])]
    ppermute x10 -> x13, starting transfers between devices: 3.62 us -> 9.06 us  [swapped(): return lax.ppermute(x, 'group', [(i, i ^ bit) for i in range(groups)])]
    pallas_call x1 -> x2, Pallas kernels: 9.04 us -> 13.1 us  [pair_part(): pl.pallas_call(functools.partial(pair_kernel, z, first, layout), out_shap...]
    pallas_call x1, Pallas kernels: 9.18 us -> 10.5 us  [plan(): pl.pallas_call(functools.partial(plan_kernel, z), out_shape=(jax.ShapeDty...]
    ppermute x10 -> x13, waiting for transfers between devices: 10.3 us -> 9.09 us  [swapped(): return lax.ppermute(x, 'group', [(i, i ^ bit) for i in range(groups)])]
    unnamed x32 -> x34, local copies, waits for them, and re-layouts: 2.26 us -> 2.26 us
  transfers between devices with their start and end apart: 18 -> 21, of which waited for: 9 -> 7; matrix products, arithmetic and copies ran while one was open for 1% -> 1% of each run, Pallas kernels for 16% -> 23%
where the time goes in v4:
time: 88.8 us; the launch traced here: 88.7 us
  Pallas kernels  31.4 us (35%)
  waiting for transfers between devices  26.6 us (30%)
  starting transfers between devices  25.4 us (29%)
  local copies, waits for them, and re-layouts  4.32 us (5%)
    ppermute x8, waiting for transfers between devices, moved(): lax.ppermute(x, 'orb', [(source(i) % slabs, i) for i in range(slabs)])  17.6 us
    ppermute x8, starting transfers between devices, moved(): lax.ppermute(x, 'orb', [(source(i) % slabs, i) for i in range(slabs)])  16.3 us
    pallas_call x2, Pallas kernels, pair_part(): pl.pallas_call(functools.partial(pair_kernel, z, first, layout), out_shap...  13.1 us
    pallas_call x1, Pallas kernels, plan(): pl.pallas_call(functools.partial(plan_kernel, z), out_shape=(jax.ShapeDty...  10.5 us
    ppermute x13, waiting for transfers between devices, swapped(): return lax.ppermute(x, 'group', [(i, i ^ bit) for i in range(groups)])  9.09 us
    ppermute x13, starting transfers between devices, swapped(): return lax.ppermute(x, 'group', [(i, i ^ bit) for i in range(groups)])  9.06 us
    pallas_call x1, Pallas kernels, along_part(): pl.pallas_call(functools.partial(along_kernel, z, per_step, layout), grid...  3.05 us
    pallas_call x1, Pallas kernels, plane_part(): pl.pallas_call(functools.partial(plane_kernel, z, per_step), grid=(z.colo...  2.58 us
  transfers between devices with their start and end apart: 21, of which 7 were waited for; matrix products, arithmetic and copies ran while one was open for 1% of the time, Pallas kernels for 23%

profile of v4, /device:TPU:0, one launch (start us, length us, event | category | flops | bytes accessed | tf_op | source)
XLA Modules:
  0.0 88.7 jit_solution(1492355483781675473)
XLA Ops:
  0.0 2.1 %constant_dynamic-slice_fusion = bf16[48,8,1024]{2,1,0:T(8,128)(2,1)} fusion(bf16[96,8,1024]{2,1,0:T(8,128)(2,1)} %here.6, s32[]{:T(128)S(6)} %select_n.3), kind=kLoop, calls=%fused_computation.2 | loop fusion | bytes 1572868 | tf_op jit(solution)/shard_map/dynamic_slice | solution.py:535
  2.1 3.0 %collective-permute-start.1 = (bf16[48,8,1024]{2,1,0:T(8,128)(2,1)}, bf16[48,8,1024]{2,1,0:T(8,128)(2,1)S(1)}, u32[]{:S(2)}, u32[]{:S(2)}) collective-permute-start(bf16[48,8,1024]{2,1,0:T(8,128)(2,1)} %constant_dynamic-slice_fusion), channel_id=1, source_target_pairs={{1,0},{0,1},{3,2},{2,3},{5,4},{4,5},{7,6},{6,7},{9,8},{8,9},{11,10... | collective-permute-start | bytes 2359304 | tf_op jit(solution)/shard_map/ppermute | solution.py:495
  5.0 3.6 %collective-permute-start = (bf16[48,8,1024]{2,1,0:T(8,128)(2,1)}, bf16[48,8,1024]{2,1,0:T(8,128)(2,1)S(1)}, u32[]{:S(2)}, u32[]{:S(2)}) collective-permute-start(bf16[48,8,1024]{2,1,0:T(8,128)(2,1)} %constant_dynamic-slice_fusion), channel_id=1, source_target_pairs={{2,0},{7,1},{4,2},{1,3},{6,4},{3,5},{0,6},{5,7},{10,8},{15,9},{12,... | collective-permute-start | bytes 2359304 | tf_op jit(solution)/shard_map/ppermute | solution.py:495
  9.2 10.5 %plan.1 = (s32[2]{0:T(128)}, s32[2,4,174]{2,1,0:T(4,128)}, s32[2,6]{1,0:T(2,128)}, s32[96]{0:T(128)}) custom-call(s32[2]{0:T(128)} %pad_add_fusion.1.ids, s32[96]{0:T(128)} %shift.3, s32[24,56]{1,0:T(8,128)} %partner.1, s32[24,56]{1,0:T(8,128)} %member.1), custom_call_target="tpu_custom_call" | custom-call | flops 10000000000 | bytes 100000 | tf_op jit(solution)/shard_map/plan/pallas_call | solution.py:197
  19.7 5.7 %collective-permute-done.rest_2_ = bf16[48,8,1024]{2,1,0:T(8,128)(2,1)S(1)} collective-permute-done((bf16[48,8,1024]{2,1,0:T(8,128)(2,1)}, bf16[48,8,1024]{2,1,0:T(8,128)(2,1)S(1)}, u32[]{:S(2)}, u32[]{:S(2)}) %collective-permute-start) | collective-permute-done | bytes 786464 | tf_op jit(solution)/shard_map/ppermute | solution.py:495
  26.1 1.2 %collective-permute-start.4 = (bf16[48,8,1024]{2,1,0:T(8,128)(2,1)S(1)}, bf16[48,8,1024]{2,1,0:T(8,128)(2,1)S(1)}, u32[]{:S(2)}, u32[]{:S(2)}) collective-permute-start(bf16[48,8,1024]{2,1,0:T(8,128)(2,1)S(1)} %collective-permute-done.rest_2_), channel_id=1, source_target_pairs={{1,0},{0,1},{3,2},{2,3},{5,4},{4,5},{7,6},{6,7},{9,8},{8,9},{11,10... | collective-permute-start | bytes 2359304 | tf_op jit(solution)/shard_map/ppermute | solution.py:495
  27.3 2.2 %copy-done.5 = bf16[2,1024,1024]{2,1,0:T(8,128)(2,1)S(1)} copy-done((bf16[2,1024,1024]{2,1,0:T(8,128)(2,1)S(1)}, bf16[2,1024,1024]{2,1,0:T(8,128)(2,1)}, u32[]{:S(2)}) %copy-start.5) | copy-done | bytes 4194328
  29.5 2.6 %plane.2.flat = f32[96,8,1024]{2,1,0:T(8,128)S(1)} custom-call(bf16[96,8,1024]{2,1,0:T(8,128)(2,1)S(1)} %copy-done, f32[8,1024]{1,0:T(8,128)S(1)} %copy-done.3, bf16[2,1024,1024]{2,1,0:T(8,128)(2,1)S(1)} %copy-done.5), custom_call_target="tpu_custom_call" | custom-call | flops 6000000000 | bytes 12000000 | tf_op jit(solution)/shard_map/plane/pallas_call | solution.py:389
  32.2 4.4 %first_pairs.1.rest_8_ = f32[240,1024]{1,0:T(8,128)S(1)} custom-call(s32[2]{0:T(128)S(1)} %copy-done.1, s32[2]{0:T(128)S(1)} %copy-done.16, s32[2,4,174]{2,1,0:T(4,128)S(1)} %copy-done.14, s32[2,6]{1,0:T(2,128)S(1)} %copy-done.15, bf16[96,8,1024]{2,1,0:T(8,128)(2,1)S(1)} %copy-done, bf16[48,8,1024]{2,1,0:T(8,128)(2,1)S(1)} %collective-permute-done.1.rest_0_, ...), custom_call_target="tpu_custom_call" | custom-call | flops 8000000000 | bytes 16000000 | tf_op jit(solution)/shard_map/first_pairs/pallas_call | solution.py:352
  36.7 11.8 %collective-permute-done.6.rest_6_ = bf16[48,8,1024]{2,1,0:T(8,128)(2,1)S(1)} collective-permute-done((bf16[48,8,1024]{2,1,0:T(8,128)(2,1)}, bf16[48,8,1024]{2,1,0:T(8,128)(2,1)S(1)}, u32[]{:S(2)}, u32[]{:S(2)}) %collective-permute-start.6) | collective-permute-done | bytes 786464 | tf_op jit(solution)/shard_map/ppermute | solution.py:495
  49.0 1.8 %collective-permute-done.7.rest_7_ = bf16[48,8,1024]{2,1,0:T(8,128)(2,1)S(1)} collective-permute-done((bf16[48,8,1024]{2,1,0:T(8,128)(2,1)S(1)}, bf16[48,8,1024]{2,1,0:T(8,128)(2,1)S(1)}, u32[]{:S(2)}, u32[]{:S(2)}) %collective-permute-start.7) | collective-permute-done | bytes 786464 | tf_op jit(solution)/shard_map/ppermute | solution.py:503
  50.8 1.1 %collective-permute-done.5.rest_5_.rest_3_ = bf16[48,8,1024]{2,1,0:T(8,128)(2,1)S(1)} collective-permute-done((bf16[48,8,1024]{2,1,0:T(8,128)(2,1)S(1)}, bf16[48,8,1024]{2,1,0:T(8,128)(2,1)S(1)}, u32[]{:S(2)}, u32[]{:S(2)}) %collective-permute-start.5) | collective-permute-done | bytes 786464 | tf_op jit(solution)/shard_map/ppermute | solution.py:503
  51.9 8.7 %pair_solves.1 = (s16[7,8,1024]{2,1,0:T(8,128)(2,1)S(1)}, s16[7,8,1024]{2,1,0:T(8,128)(2,1)S(1)}, s16[7,8,1024]{2,1,0:T(8,128)(2,1)S(1)}, s16[7,8,1024]{2,1,0:T(8,128)(2,1)S(1)}, s16[7,8,1024]{2,1,0:T(8,128)(2,1)S(1)}) custom-call(s32[2]{0:T(128)S(1)} %copy-done.1, s32[2]{0:T(128)S(1)} %copy-done.16, s32[2,4,174]{2,1,0:T(4,128)S(1)} %copy-done.14, ...), custom_call_target="tpu_custom_call" | custom-call | flops 20000000000 | bytes 16000000 | tf_op jit(solution)/shard_map/pair_solves/pallas_call | solution.py:352
  60.6 0.9 %collective-permute-start.8 = (s16[7,8,1024]{2,1,0:T(8,128)(2,1)S(1)}, s16[7,8,1024]{2,1,0:T(8,128)(2,1)S(1)}, u32[]{:S(2)}, u32[]{:S(2)}) collective-permute-start(s16[7,8,1024]{2,1,0:T(8,128)(2,1)S(1)} %get-tuple-element.31), channel_id=1, source_target_pairs={{7,0},{0,1},{1,2},{2,3},{3,4},{4,5},{5,6},{6,7},{15,8},{8,9},{9,10... | collective-permute-start | bytes 344072 | tf_op jit(solution)/shard_map/ppermute | solution.py:495
  61.5 4.2 %collective-permute-start.15 = (s16[7,8,1024]{2,1,0:T(8,128)(2,1)S(1)}, s16[7,8,1024]{2,1,0:T(8,128)(2,1)S(1)}, u32[]{:S(2)}, u32[]{:S(2)}) collective-permute-start(s16[7,8,1024]{2,1,0:T(8,128)(2,1)S(1)} %get-tuple-element.34), channel_id=1, source_target_pairs={{2,0},{3,1},{4,2},{5,3},{6,4},{7,5},{0,6},{1,7},{10,8},{11,9},{12,... | collective-permute-start | bytes 344072 | tf_op jit(solution)/shard_map/ppermute | solution.py:495
  65.6 3.5 %collective-permute-start.17 = (s16[7,8,1024]{2,1,0:T(8,128)(2,1)S(1)}, s16[7,8,1024]{2,1,0:T(8,128)(2,1)S(1)}, u32[]{:S(2)}, u32[]{:S(2)}) collective-permute-start(s16[7,8,1024]{2,1,0:T(8,128)(2,1)S(1)} %get-tuple-element.36), channel_id=1, source_target_pairs={{1,0},{2,1},{3,2},{4,3},{5,4},{6,5},{7,6},{0,7},{9,8},{10,9},{11,1... | collective-permute-start | bytes 344072 | tf_op jit(solution)/shard_map/ppermute | solution.py:495
  69.2 1.7 %collective-permute-start.10 = (s16[7,8,1024]{2,1,0:T(8,128)(2,1)S(1)}, s16[7,8,1024]{2,1,0:T(8,128)(2,1)S(1)}, u32[]{:S(2)}, u32[]{:S(2)}) collective-permute-start(s16[7,8,1024]{2,1,0:T(8,128)(2,1)S(1)} %get-tuple-element.33.rest_0_), channel_id=1, source_target_pairs={{0,8},{8,0},{16,24},{24,16},{1,9},{9,1},{17,25},{25,17},{2,10},{10... | collective-permute-start | bytes 344072 | tf_op jit(solution)/shard_map/ppermute | solution.py:503
  70.9 2.2 %collective-permute-start.9 = (s16[7,8,1024]{2,1,0:T(8,128)(2,1)S(1)}, s16[7,8,1024]{2,1,0:T(8,128)(2,1)S(1)}, u32[]{:S(2)}, u32[]{:S(2)}) collective-permute-start(s16[7,8,1024]{2,1,0:T(8,128)(2,1)S(1)} %get-tuple-element.33.rest_0_), channel_id=1, source_target_pairs={{0,16},{8,24},{16,0},{24,8},{1,17},{9,25},{17,1},{25,9},{2,18},{10... | collective-permute-start | bytes 344072 | tf_op jit(solution)/shard_map/ppermute | solution.py:503
  73.2 3.3 %collective-permute-start.18 = (s16[14,8,1024]{2,1,0:T(8,128)(2,1)S(1)}, s16[14,8,1024]{2,1,0:T(8,128)(2,1)S(1)}, u32[]{:S(2)}, u32[]{:S(2)}) collective-permute-start(s16[14,8,1024]{2,1,0:T(8,128)(2,1)S(1)} %pad_add_fusion.rest_8_), channel_id=1, source_target_pairs={{0,16},{8,24},{16,0},{24,8},{1,17},{9,25},{17,1},{25,9},{2,18},{10... | collective-permute-start | bytes 688136 | tf_op jit(solution)/shard_map/ppermute | solution.py:503
  76.5 3.0 %along.1.local = f32[96,8,1024]{2,1,0:T(8,128)S(1)} custom-call(s32[2]{0:T(128)S(1)} %copy-done.1, s32[96]{0:T(128)S(1)} %copy-done.4, bf16[96,8,1024]{2,1,0:T(8,128)(2,1)S(1)} %copy-done, f32[96,8,1024]{2,1,0:T(8,128)S(1)} %plane.2.flat, bf16[48,8,1024]{2,1,0:T(8,128)(2,1)S(1)} %collective-permute-done.1.rest_0_, ...), custom_call_target="tpu_custom_call" | custom-call | flops 5000000000 | bytes 12000000 | tf_op jit(solution)/shard_map/along/pallas_call | solution.py:442
  79.7 2.4 %collective-permute-done.18.rest_9_ = s16[14,8,1024]{2,1,0:T(8,128)(2,1)S(1)} collective-permute-done((s16[14,8,1024]{2,1,0:T(8,128)(2,1)S(1)}, s16[14,8,1024]{2,1,0:T(8,128)(2,1)S(1)}, u32[]{:S(2)}, u32[]{:S(2)}) %collective-permute-start.18) | collective-permute-done | bytes 229408 | tf_op jit(solution)/shard_map/ppermute | solution.py:503
  82.8 2.4 %collective-permute-done.12.rest_5_ = s16[7,8,1024]{2,1,0:T(8,128)(2,1)S(1)} collective-permute-done((s16[7,8,1024]{2,1,0:T(8,128)(2,1)S(1)}, s16[7,8,1024]{2,1,0:T(8,128)(2,1)S(1)}, u32[]{:S(2)}, u32[]{:S(2)}) %collective-permute-start.12) | collective-permute-done | bytes 114720 | tf_op jit(solution)/shard_map/ppermute | solution.py:503
  85.2 1.3 %collective-permute-done.14.rest_7_ = s16[7,8,1024]{2,1,0:T(8,128)(2,1)S(1)} collective-permute-done((s16[7,8,1024]{2,1,0:T(8,128)(2,1)S(1)}, s16[7,8,1024]{2,1,0:T(8,128)(2,1)S(1)}, u32[]{:S(2)}, u32[]{:S(2)}) %collective-permute-start.14) | collective-permute-done | bytes 114720 | tf_op jit(solution)/shard_map/ppermute | solution.py:503
  86.5 2.2 %finish.1 = f32[96,8,1024]{2,1,0:T(8,128)} custom-call(s32[2]{0:T(128)S(1)} %copy-done.1, s32[96]{0:T(128)S(1)} %copy-done.2, f32[96,8,1024]{2,1,0:T(8,128)S(1)} %along.1.local, s16[7,8,1024]{2,1,0:T(8,128)(2,1)S(1)} %get-tuple-element.33.rest_0_, s16[7,8,1024]{2,1,0:T(8,128)(2,1)S(1)} %collective-permute-done.9.rest_1_, ...), custom_call_target="tpu_custom_call" | custom-call | tf_op jit(solution)/shard_map/finish/pallas_call | solution.py:483
  (62 shorter events, 2.6 us)
Async XLA Ops:
  2.1 23.4 %collective-permute-start.1 = (bf16[48,8,1024]{2,1,0:T(8,128)(2,1)}, bf16[48,8,1024]{2,1,0:T(8,128)(2,1)S(1)}, u32[]{:S(2)}, u32[]{:S(2)}) collective-permute-start(bf16[48,8,1024]{2,1,0:T(8,128)(2,1)} %constant_dynamic-slice_fusion), channel_id=1, source_target_pairs={{1,0},{0,1},{3,2},{2,3},{5,4},{4,5},{7,6},{6,7},{9,8},{8,9},{11,10... | collective-permute-start | bytes 2359304 | tf_op jit(solution)/shard_map/ppermute | solution.py:495
  5.0 20.4 %collective-permute-start = (bf16[48,8,1024]{2,1,0:T(8,128)(2,1)}, bf16[48,8,1024]{2,1,0:T(8,128)(2,1)S(1)}, u32[]{:S(2)}, u32[]{:S(2)}) collective-permute-start(bf16[48,8,1024]{2,1,0:T(8,128)(2,1)} %constant_dynamic-slice_fusion), channel_id=1, source_target_pairs={{2,0},{7,1},{4,2},{1,3},{6,4},{3,5},{0,6},{5,7},{10,8},{15,9},{12,... | collective-permute-start | bytes 2359304 | tf_op jit(solution)/shard_map/ppermute | solution.py:495
  25.5 6.6 %collective-permute-start.2 = (bf16[48,8,1024]{2,1,0:T(8,128)(2,1)S(1)}, bf16[48,8,1024]{2,1,0:T(8,128)(2,1)S(1)}, u32[]{:S(2)}, u32[]{:S(2)}) collective-permute-start(bf16[48,8,1024]{2,1,0:T(8,128)(2,1)S(1)} %collective-permute-done.1.rest_0_), channel_id=1, source_target_pairs={{0,8},{8,0},{16,24},{24,16},{1,9},{9,1},{17,25},{25,17},{2,10},{10... | collective-permute-start | bytes 2359304 | tf_op jit(solution)/shard_map/ppermute | solution.py:503
  25.6 6.5 %collective-permute-start.3 = (bf16[48,8,1024]{2,1,0:T(8,128)(2,1)S(1)}, bf16[48,8,1024]{2,1,0:T(8,128)(2,1)S(1)}, u32[]{:S(2)}, u32[]{:S(2)}) collective-permute-start(bf16[48,8,1024]{2,1,0:T(8,128)(2,1)S(1)} %collective-permute-done.rest_2_), channel_id=1, source_target_pairs={{0,8},{8,0},{16,24},{24,16},{1,9},{9,1},{17,25},{25,17},{2,10},{10... | collective-permute-start | bytes 2359304 | tf_op jit(solution)/shard_map/ppermute | solution.py:503
  26.1 22.4 %collective-permute-start.4 = (bf16[48,8,1024]{2,1,0:T(8,128)(2,1)S(1)}, bf16[48,8,1024]{2,1,0:T(8,128)(2,1)S(1)}, u32[]{:S(2)}, u32[]{:S(2)}) collective-permute-start(bf16[48,8,1024]{2,1,0:T(8,128)(2,1)S(1)} %collective-permute-done.rest_2_), channel_id=1, source_target_pairs={{1,0},{0,1},{3,2},{2,3},{5,4},{4,5},{7,6},{6,7},{9,8},{8,9},{11,10... | collective-permute-start | bytes 2359304 | tf_op jit(solution)/shard_map/ppermute | solution.py:495
  27.2 21.3 %collective-permute-start.6 = (bf16[48,8,1024]{2,1,0:T(8,128)(2,1)}, bf16[48,8,1024]{2,1,0:T(8,128)(2,1)S(1)}, u32[]{:S(2)}, u32[]{:S(2)}) collective-permute-start(bf16[48,8,1024]{2,1,0:T(8,128)(2,1)} %constant_dynamic-slice_fusion), channel_id=1, source_target_pairs={{6,0},{3,1},{0,2},{5,3},{2,4},{7,5},{4,6},{1,7},{14,8},{11,9},{8,1... | collective-permute-start | bytes 2359304 | tf_op jit(solution)/shard_map/ppermute | solution.py:495
  32.1 19.8 %copy-start.7 = (bf16[1024,1024]{1,0:T(8,128)(2,1)S(1)}, bf16[1024,1024]{1,0:T(8,128)(2,1)}, u32[]{:S(2)}) copy-start(bf16[1024,1024]{1,0:T(8,128)(2,1)} %constant.44.clone.rest_15_) | copy-start | bytes 6291460
  36.6 39.8 %copy-start.4 = (s32[96]{0:T(128)S(1)}, s32[96]{0:T(128)}, u32[]{:S(2)}) copy-start(s32[96]{0:T(128)} %shift.3) | copy-start | bytes 1156
  36.7 39.8 %copy-start.11 = (f32[32,8,192]{2,1,0:T(8,128)S(1)}, f32[32,8,192]{2,1,0:T(8,128)}, u32[]{:S(2)}) copy-start(f32[32,8,192]{2,1,0:T(8,128)} %constant.37.clone.rest_4_) | copy-start | bytes 589828
  48.5 2.3 %collective-permute-start.7 = (bf16[48,8,1024]{2,1,0:T(8,128)(2,1)S(1)}, bf16[48,8,1024]{2,1,0:T(8,128)(2,1)S(1)}, u32[]{:S(2)}, u32[]{:S(2)}) collective-permute-start(bf16[48,8,1024]{2,1,0:T(8,128)(2,1)S(1)} %collective-permute-done.6.rest_6_), channel_id=1, source_target_pairs={{0,8},{8,0},{16,24},{24,16},{1,9},{9,1},{17,25},{25,17},{2,10},{10... | collective-permute-start | bytes 2359304 | tf_op jit(solution)/shard_map/ppermute | solution.py:503
  48.5 3.4 %collective-permute-start.5 = (bf16[48,8,1024]{2,1,0:T(8,128)(2,1)S(1)}, bf16[48,8,1024]{2,1,0:T(8,128)(2,1)S(1)}, u32[]{:S(2)}, u32[]{:S(2)}) collective-permute-start(bf16[48,8,1024]{2,1,0:T(8,128)(2,1)S(1)} %collective-permute-done.4.rest_4_.rest_2_), channel_id=1, source_target_pairs={{0,8},{8,0},{16,24},{24,16},{1,9},{9,1},{17,25},{25,17},{2,10},{10... | collective-permute-start | bytes 2359304 | tf_op jit(solution)/shard_map/ppermute | solution.py:503
  60.6 10.3 %collective-permute-start.8 = (s16[7,8,1024]{2,1,0:T(8,128)(2,1)S(1)}, s16[7,8,1024]{2,1,0:T(8,128)(2,1)S(1)}, u32[]{:S(2)}, u32[]{:S(2)}) collective-permute-start(s16[7,8,1024]{2,1,0:T(8,128)(2,1)S(1)} %get-tuple-element.31), channel_id=1, source_target_pairs={{7,0},{0,1},{1,2},{2,3},{3,4},{4,5},{5,6},{6,7},{15,8},{8,9},{9,10... | collective-permute-start | bytes 344072 | tf_op jit(solution)/shard_map/ppermute | solution.py:495
  61.5 11.7 %collective-permute-start.15 = (s16[7,8,1024]{2,1,0:T(8,128)(2,1)S(1)}, s16[7,8,1024]{2,1,0:T(8,128)(2,1)S(1)}, u32[]{:S(2)}, u32[]{:S(2)}) collective-permute-start(s16[7,8,1024]{2,1,0:T(8,128)(2,1)S(1)} %get-tuple-element.34), channel_id=1, source_target_pairs={{2,0},{3,1},{4,2},{5,3},{6,4},{7,5},{0,6},{1,7},{10,8},{11,9},{12,... | collective-permute-start | bytes 344072 | tf_op jit(solution)/shard_map/ppermute | solution.py:495
  65.6 7.5 %collective-permute-start.16 = (s16[7,8,1024]{2,1,0:T(8,128)(2,1)S(1)}, s16[7,8,1024]{2,1,0:T(8,128)(2,1)S(1)}, u32[]{:S(2)}, u32[]{:S(2)}) collective-permute-start(s16[7,8,1024]{2,1,0:T(8,128)(2,1)S(1)} %get-tuple-element.35), channel_id=1, source_target_pairs={{6,0},{7,1},{0,2},{1,3},{2,4},{3,5},{4,6},{5,7},{14,8},{15,9},{8,1... | collective-permute-start | bytes 344072 | tf_op jit(solution)/shard_map/ppermute | solution.py:495
  65.6 7.5 %collective-permute-start.17 = (s16[7,8,1024]{2,1,0:T(8,128)(2,1)S(1)}, s16[7,8,1024]{2,1,0:T(8,128)(2,1)S(1)}, u32[]{:S(2)}, u32[]{:S(2)}) collective-permute-start(s16[7,8,1024]{2,1,0:T(8,128)(2,1)S(1)} %get-tuple-element.36), channel_id=1, source_target_pairs={{1,0},{2,1},{3,2},{4,3},{5,4},{6,5},{7,6},{0,7},{9,8},{10,9},{11,1... | collective-permute-start | bytes 344072 | tf_op jit(solution)/shard_map/ppermute | solution.py:495
  69.2 13.0 %collective-permute-start.10 = (s16[7,8,1024]{2,1,0:T(8,128)(2,1)S(1)}, s16[7,8,1024]{2,1,0:T(8,128)(2,1)S(1)}, u32[]{:S(2)}, u32[]{:S(2)}) collective-permute-start(s16[7,8,1024]{2,1,0:T(8,128)(2,1)S(1)} %get-tuple-element.33.rest_0_), channel_id=1, source_target_pairs={{0,8},{8,0},{16,24},{24,16},{1,9},{9,1},{17,25},{25,17},{2,10},{10... | collective-permute-start | bytes 344072 | tf_op jit(solution)/shard_map/ppermute | solution.py:503
  70.9 11.8 %collective-permute-start.9 = (s16[7,8,1024]{2,1,0:T(8,128)(2,1)S(1)}, s16[7,8,1024]{2,1,0:T(8,128)(2,1)S(1)}, u32[]{:S(2)}, u32[]{:S(2)}) collective-permute-start(s16[7,8,1024]{2,1,0:T(8,128)(2,1)S(1)} %get-tuple-element.33.rest_0_), channel_id=1, source_target_pairs={{0,16},{8,24},{16,0},{24,8},{1,17},{9,25},{17,1},{25,9},{2,18},{10... | collective-permute-start | bytes 344072 | tf_op jit(solution)/shard_map/ppermute | solution.py:503
  73.2 9.0 %collective-permute-start.18 = (s16[14,8,1024]{2,1,0:T(8,128)(2,1)S(1)}, s16[14,8,1024]{2,1,0:T(8,128)(2,1)S(1)}, u32[]{:S(2)}, u32[]{:S(2)}) collective-permute-start(s16[14,8,1024]{2,1,0:T(8,128)(2,1)S(1)} %pad_add_fusion.rest_8_), channel_id=1, source_target_pairs={{0,16},{8,24},{16,0},{24,8},{1,17},{9,25},{17,1},{25,9},{2,18},{10... | collective-permute-start | bytes 688136 | tf_op jit(solution)/shard_map/ppermute | solution.py:503
  79.5 7.0 %collective-permute-start.19 = (s16[14,8,1024]{2,1,0:T(8,128)(2,1)S(1)}, s16[14,8,1024]{2,1,0:T(8,128)(2,1)S(1)}, u32[]{:S(2)}, u32[]{:S(2)}) collective-permute-start(s16[14,8,1024]{2,1,0:T(8,128)(2,1)S(1)} %pad_add_fusion.rest_8_), channel_id=1, source_target_pairs={{0,8},{8,0},{16,24},{24,16},{1,9},{9,1},{17,25},{25,17},{2,10},{10... | collective-permute-start | bytes 688136 | tf_op jit(solution)/shard_map/ppermute | solution.py:503
  79.6 5.6 %collective-permute-start.12 = (s16[7,8,1024]{2,1,0:T(8,128)(2,1)S(1)}, s16[7,8,1024]{2,1,0:T(8,128)(2,1)S(1)}, u32[]{:S(2)}, u32[]{:S(2)}) collective-permute-start(s16[7,8,1024]{2,1,0:T(8,128)(2,1)S(1)} %collective-permute-done.8.rest_4_), channel_id=1, source_target_pairs={{0,16},{8,24},{16,0},{24,8},{1,17},{9,25},{17,1},{25,9},{2,18},{10... | collective-permute-start | bytes 344072 | tf_op jit(solution)/shard_map/ppermute | solution.py:503
  82.2 4.3 %collective-permute-start.20 = (s16[14,8,1024]{2,1,0:T(8,128)(2,1)S(1)}, s16[14,8,1024]{2,1,0:T(8,128)(2,1)S(1)}, u32[]{:S(2)}, u32[]{:S(2)}) collective-permute-start(s16[14,8,1024]{2,1,0:T(8,128)(2,1)S(1)} %collective-permute-done.18.rest_9_), channel_id=1, source_target_pairs={{0,8},{8,0},{16,24},{24,16},{1,9},{9,1},{17,25},{25,17},{2,10},{10... | collective-permute-start | bytes 688136 | tf_op jit(solution)/shard_map/ppermute | solution.py:503
  82.2 3.0 %collective-permute-start.13 = (s16[7,8,1024]{2,1,0:T(8,128)(2,1)S(1)}, s16[7,8,1024]{2,1,0:T(8,128)(2,1)S(1)}, u32[]{:S(2)}, u32[]{:S(2)}) collective-permute-start(s16[7,8,1024]{2,1,0:T(8,128)(2,1)S(1)} %collective-permute-done.8.rest_4_), channel_id=1, source_target_pairs={{0,8},{8,0},{16,24},{24,16},{1,9},{9,1},{17,25},{25,17},{2,10},{10... | collective-permute-start | bytes 344072 | tf_op jit(solution)/shard_map/ppermute | solution.py:503
  82.7 2.5 %collective-permute-start.11 = (s16[7,8,1024]{2,1,0:T(8,128)(2,1)S(1)}, s16[7,8,1024]{2,1,0:T(8,128)(2,1)S(1)}, u32[]{:S(2)}, u32[]{:S(2)}) collective-permute-start(s16[7,8,1024]{2,1,0:T(8,128)(2,1)S(1)} %collective-permute-done.9.rest_1_), channel_id=1, source_target_pairs={{0,8},{8,0},{16,24},{24,16},{1,9},{9,1},{17,25},{25,17},{2,10},{10... | collective-permute-start | bytes 344072 | tf_op jit(solution)/shard_map/ppermute | solution.py:503
  85.2 1.3 %collective-permute-start.14 = (s16[7,8,1024]{2,1,0:T(8,128)(2,1)S(1)}, s16[7,8,1024]{2,1,0:T(8,128)(2,1)S(1)}, u32[]{:S(2)}, u32[]{:S(2)}) collective-permute-start(s16[7,8,1024]{2,1,0:T(8,128)(2,1)S(1)} %collective-permute-done.12.rest_5_), channel_id=1, source_target_pairs={{0,8},{8,0},{16,24},{24,16},{1,9},{9,1},{17,25},{25,17},{2,10},{10... | collective-permute-start | bytes 344072 | tf_op jit(solution)/shard_map/ppermute | solution.py:503
  (14 other events, 90.4 us)

commit v5 on v4

--- a/solution.py
+++ b/solution.py
@@ -536,10 +536,10 @@
     side = moved(mine, lambda i: i + 2 if i % 2 == 0 else i - 2, slabs)
     near = moved(mine, lambda i: i ^ 1, slabs)
     done = early_work()
-    side = after(side, *done)
+    flat = late_work(after(orbitals, done[0]))
+    side = after(side, *done, flat)
     far = moved(side, lambda i: i ^ 1, slabs)
-    rest = moved(after(mine, side), lambda i: i - 2 if i % 2 == 0 else i + 2, slabs)
-    flat = late_work(after(orbitals, side))
+    rest = moved(after(mine, flat), lambda i: i - 2 if i % 2 == 0 else i + 2, slabs)
 
     def keep(x, even, odd):
         for flip, y in enumerate((x, swapped(x, 1, groups))):
@@ -549,7 +549,7 @@
     keep(near, lo + 3, lo + 1)
     keep(side, hi, lo)
     sums = first_pairs(done, list(layout), list(pieces))
-    keep(after(far, flat), lo + 1, lo + 3)
+    keep(after(far, sums), lo + 1, lo + 3)
     keep(after(rest, sums), lo, hi)
     return layout, pieces, (*done, flat, sums)
 

time: 88.8 us -> 88.4 us (level); the launches traced: 88.7 us -> 89.9 us
  starting transfers between devices: 25.4 us -> 21.1 us
  waiting for transfers between devices: 26.6 us -> 29.5 us
  Pallas kernels: 31.4 us -> 34 us
    ppermute x13, starting transfers between devices: 9.06 us -> 3.79 us  [swapped(): return lax.ppermute(x, 'group', [(i, i ^ bit) for i in range(groups)])]
    ppermute x8, waiting for transfers between devices: 17.6 us -> 20.5 us  [moved(): lax.ppermute(x, 'orb', [(source(i) % slabs, i) for i in range(slabs)])]
    pallas_call x2, Pallas kernels: 13.1 us -> 15.7 us  [pair_part(): pl.pallas_call(functools.partial(pair_kernel, z, first, layout), out_shap...]
    ppermute x8, starting transfers between devices: 16.3 us -> 17.3 us  [moved(): lax.ppermute(x, 'orb', [(source(i) % slabs, i) for i in range(slabs)])]
  transfers between devices with their start and end apart: 21 -> 21, of which waited for: 7 -> 10; matrix products, arithmetic and copies ran while one was open for 1% -> 1% of each run, Pallas kernels for 23% -> 23%
where the time goes in v5:
time: 88.4 us; the launch traced here: 89.9 us
  Pallas kernels  34 us (38%)
  waiting for transfers between devices  29.5 us (33%)
  starting transfers between devices  21.1 us (24%)
  local copies, waits for them, and re-layouts  4.32 us (5%)
    ppermute x8, waiting for transfers between devices, moved(): lax.ppermute(x, 'orb', [(source(i) % slabs, i) for i in range(slabs)])  20.5 us
    ppermute x8, starting transfers between devices, moved(): lax.ppermute(x, 'orb', [(source(i) % slabs, i) for i in range(slabs)])  17.3 us
    pallas_call x2, Pallas kernels, pair_part(): pl.pallas_call(functools.partial(pair_kernel, z, first, layout), out_shap...  15.7 us
    pallas_call x1, Pallas kernels, plan(): pl.pallas_call(functools.partial(plan_kernel, z), out_shape=(jax.ShapeDty...  10.5 us
    ppermute x13, waiting for transfers between devices, swapped(): return lax.ppermute(x, 'group', [(i, i ^ bit) for i in range(groups)])  9.03 us
    ppermute x13, starting transfers between devices, swapped(): return lax.ppermute(x, 'group', [(i, i ^ bit) for i in range(groups)])  3.79 us
    pallas_call x1, Pallas kernels, along_part(): pl.pallas_call(functools.partial(along_kernel, z, per_step, layout), grid...  3.07 us
    pallas_call x1, Pallas kernels, plane_part(): pl.pallas_call(functools.partial(plane_kernel, z, per_step), grid=(z.colo...  2.58 us
  transfers between devices with their start and end apart: 21, of which 10 were waited for; matrix products, arithmetic and copies ran while one was open for 1% of the time, Pallas kernels for 23%

profile of v5, /device:TPU:0, one launch (start us, length us, event | category | flops | bytes accessed | tf_op | source)
XLA Modules:
  0.0 89.9 jit_solution(1014972013801267206)
XLA Ops:
  0.0 2.1 %constant_dynamic-slice_fusion = bf16[48,8,1024]{2,1,0:T(8,128)(2,1)} fusion(bf16[96,8,1024]{2,1,0:T(8,128)(2,1)} %here.6, s32[]{:T(128)S(6)} %select_n.3), kind=kLoop, calls=%fused_computation.2 | loop fusion | bytes 1572868 | tf_op jit(solution)/shard_map/dynamic_slice | solution.py:535
  2.1 5.0 %collective-permute-start.2 = (bf16[48,8,1024]{2,1,0:T(8,128)(2,1)}, bf16[48,8,1024]{2,1,0:T(8,128)(2,1)S(1)}, u32[]{:S(2)}, u32[]{:S(2)}) collective-permute-start(bf16[48,8,1024]{2,1,0:T(8,128)(2,1)} %constant_dynamic-slice_fusion), channel_id=1, source_target_pairs={{2,0},{7,1},{4,2},{1,3},{6,4},{3,5},{0,6},{5,7},{10,8},{15,9},{12,... | collective-permute-start | bytes 2359304 | tf_op jit(solution)/shard_map/ppermute | solution.py:495
  7.7 10.5 %plan.1 = (s32[2]{0:T(128)}, s32[2,4,174]{2,1,0:T(4,128)}, s32[2,6]{1,0:T(2,128)}, s32[96]{0:T(128)}) custom-call(s32[2]{0:T(128)} %pad_add_fusion.1.ids, s32[96]{0:T(128)} %shift.3, s32[24,56]{1,0:T(8,128)} %partner.1, s32[24,56]{1,0:T(8,128)} %member.1), custom_call_target="tpu_custom_call" | custom-call | flops 10000000000 | bytes 100000 | tf_op jit(solution)/shard_map/plan/pallas_call | solution.py:197
  18.3 2.2 %copy-done.5 = bf16[2,1024,1024]{2,1,0:T(8,128)(2,1)S(1)} copy-done((bf16[2,1024,1024]{2,1,0:T(8,128)(2,1)S(1)}, bf16[2,1024,1024]{2,1,0:T(8,128)(2,1)}, u32[]{:S(2)}) %copy-start.5) | copy-done | bytes 4194328
  20.5 2.6 %plane.2.flat = f32[96,8,1024]{2,1,0:T(8,128)S(1)} custom-call(bf16[96,8,1024]{2,1,0:T(8,128)(2,1)S(1)} %copy-done, f32[8,1024]{1,0:T(8,128)S(1)} %copy-done.3, bf16[2,1024,1024]{2,1,0:T(8,128)(2,1)S(1)} %copy-done.5), custom_call_target="tpu_custom_call" | custom-call | flops 6000000000 | bytes 12000000 | tf_op jit(solution)/shard_map/plane/pallas_call | solution.py:389
  23.1 1.1 %collective-permute-done.2.rest_2_ = bf16[48,8,1024]{2,1,0:T(8,128)(2,1)S(1)} collective-permute-done((bf16[48,8,1024]{2,1,0:T(8,128)(2,1)}, bf16[48,8,1024]{2,1,0:T(8,128)(2,1)S(1)}, u32[]{:S(2)}, u32[]{:S(2)}) %collective-permute-start.2) | collective-permute-done | bytes 786464 | tf_op jit(solution)/shard_map/ppermute | solution.py:495
  24.2 2.1 %collective-permute-done.rest_0_ = bf16[48,8,1024]{2,1,0:T(8,128)(2,1)S(1)} collective-permute-done((bf16[48,8,1024]{2,1,0:T(8,128)(2,1)}, bf16[48,8,1024]{2,1,0:T(8,128)(2,1)S(1)}, u32[]{:S(2)}, u32[]{:S(2)}) %collective-permute-start) | collective-permute-done | bytes 786464 | tf_op jit(solution)/shard_map/ppermute | solution.py:495
  26.8 1.8 %collective-permute-start.4 = (bf16[48,8,1024]{2,1,0:T(8,128)(2,1)S(1)}, bf16[48,8,1024]{2,1,0:T(8,128)(2,1)S(1)}, u32[]{:S(2)}, u32[]{:S(2)}) collective-permute-start(bf16[48,8,1024]{2,1,0:T(8,128)(2,1)S(1)} %collective-permute-done.2.rest_2_), channel_id=1, source_target_pairs={{1,0},{0,1},{3,2},{2,3},{5,4},{4,5},{7,6},{6,7},{9,8},{8,9},{11,10... | collective-permute-start | bytes 2359304 | tf_op jit(solution)/shard_map/ppermute | solution.py:495
  28.6 1.1 %collective-permute-done.3.rest_3_ = bf16[48,8,1024]{2,1,0:T(8,128)(2,1)S(1)} collective-permute-done((bf16[48,8,1024]{2,1,0:T(8,128)(2,1)S(1)}, bf16[48,8,1024]{2,1,0:T(8,128)(2,1)S(1)}, u32[]{:S(2)}, u32[]{:S(2)}) %collective-permute-start.3) | collective-permute-done | bytes 786464 | tf_op jit(solution)/shard_map/ppermute | solution.py:503
  29.8 4.4 %first_pairs.1.rest_8_ = f32[240,1024]{1,0:T(8,128)S(1)} custom-call(s32[2]{0:T(128)S(1)} %copy-done.1, s32[2]{0:T(128)S(1)} %copy-done.16, s32[2,4,174]{2,1,0:T(4,128)S(1)} %copy-done.14, s32[2,6]{1,0:T(2,128)S(1)} %copy-done.15, bf16[96,8,1024]{2,1,0:T(8,128)(2,1)S(1)} %copy-done, bf16[48,8,1024]{2,1,0:T(8,128)(2,1)S(1)} %collective-permute-done.rest_0_, ...), custom_call_target="tpu_custom_call" | custom-call | flops 8000000000 | bytes 16000000 | tf_op jit(solution)/shard_map/first_pairs/pallas_call | solution.py:352
  34.3 14.0 %collective-permute-done.6.rest_6_ = bf16[48,8,1024]{2,1,0:T(8,128)(2,1)S(1)} collective-permute-done((bf16[48,8,1024]{2,1,0:T(8,128)(2,1)}, bf16[48,8,1024]{2,1,0:T(8,128)(2,1)S(1)}, u32[]{:S(2)}, u32[]{:S(2)}) %collective-permute-start.6) | collective-permute-done | bytes 786464 | tf_op jit(solution)/shard_map/ppermute | solution.py:495
  48.8 1.8 %collective-permute-done.5.rest_5_.rest_3_ = bf16[48,8,1024]{2,1,0:T(8,128)(2,1)S(1)} collective-permute-done((bf16[48,8,1024]{2,1,0:T(8,128)(2,1)S(1)}, bf16[48,8,1024]{2,1,0:T(8,128)(2,1)S(1)}, u32[]{:S(2)}, u32[]{:S(2)}) %collective-permute-start.5) | collective-permute-done | bytes 786464 | tf_op jit(solution)/shard_map/ppermute | solution.py:503
  50.6 1.1 %collective-permute-done.7.rest_7_ = bf16[48,8,1024]{2,1,0:T(8,128)(2,1)S(1)} collective-permute-done((bf16[48,8,1024]{2,1,0:T(8,128)(2,1)S(1)}, bf16[48,8,1024]{2,1,0:T(8,128)(2,1)S(1)}, u32[]{:S(2)}, u32[]{:S(2)}) %collective-permute-start.7) | collective-permute-done | bytes 786464 | tf_op jit(solution)/shard_map/ppermute | solution.py:503
  51.7 11.3 %pair_solves.1 = (s16[7,8,1024]{2,1,0:T(8,128)(2,1)S(1)}, s16[7,8,1024]{2,1,0:T(8,128)(2,1)S(1)}, s16[7,8,1024]{2,1,0:T(8,128)(2,1)S(1)}, s16[7,8,1024]{2,1,0:T(8,128)(2,1)S(1)}, s16[7,8,1024]{2,1,0:T(8,128)(2,1)S(1)}) custom-call(s32[2]{0:T(128)S(1)} %copy-done.1, s32[2]{0:T(128)S(1)} %copy-done.16, s32[2,4,174]{2,1,0:T(4,128)S(1)} %copy-done.14, ...), custom_call_target="tpu_custom_call" | custom-call | flops 20000000000 | bytes 16000000 | tf_op jit(solution)/shard_map/pair_solves/pallas_call | solution.py:352
  63.0 4.8 %collective-permute-start.8 = (s16[7,8,1024]{2,1,0:T(8,128)(2,1)S(1)}, s16[7,8,1024]{2,1,0:T(8,128)(2,1)S(1)}, u32[]{:S(2)}, u32[]{:S(2)}) collective-permute-start(s16[7,8,1024]{2,1,0:T(8,128)(2,1)S(1)} %get-tuple-element.31), channel_id=1, source_target_pairs={{7,0},{0,1},{1,2},{2,3},{3,4},{4,5},{5,6},{6,7},{15,8},{8,9},{9,10... | collective-permute-start | bytes 344072 | tf_op jit(solution)/shard_map/ppermute | solution.py:495
  67.8 2.3 %collective-permute-start.15 = (s16[7,8,1024]{2,1,0:T(8,128)(2,1)S(1)}, s16[7,8,1024]{2,1,0:T(8,128)(2,1)S(1)}, u32[]{:S(2)}, u32[]{:S(2)}) collective-permute-start(s16[7,8,1024]{2,1,0:T(8,128)(2,1)S(1)} %get-tuple-element.34), channel_id=1, source_target_pairs={{2,0},{3,1},{4,2},{5,3},{6,4},{7,5},{0,6},{1,7},{10,8},{11,9},{12,... | collective-permute-start | bytes 344072 | tf_op jit(solution)/shard_map/ppermute | solution.py:495
  70.1 3.3 %collective-permute-start.17 = (s16[7,8,1024]{2,1,0:T(8,128)(2,1)S(1)}, s16[7,8,1024]{2,1,0:T(8,128)(2,1)S(1)}, u32[]{:S(2)}, u32[]{:S(2)}) collective-permute-start(s16[7,8,1024]{2,1,0:T(8,128)(2,1)S(1)} %get-tuple-element.36), channel_id=1, source_target_pairs={{1,0},{2,1},{3,2},{4,3},{5,4},{6,5},{7,6},{0,7},{9,8},{10,9},{11,1... | collective-permute-start | bytes 344072 | tf_op jit(solution)/shard_map/ppermute | solution.py:495
  73.4 3.2 %collective-permute-done.16 = s16[7,8,1024]{2,1,0:T(8,128)(2,1)S(1)} collective-permute-done((s16[7,8,1024]{2,1,0:T(8,128)(2,1)S(1)}, s16[7,8,1024]{2,1,0:T(8,128)(2,1)S(1)}, u32[]{:S(2)}, u32[]{:S(2)}) %collective-permute-start.16) | collective-permute-done | bytes 114720 | tf_op jit(solution)/shard_map/ppermute | solution.py:495
  76.9 3.1 %along.1.local = f32[96,8,1024]{2,1,0:T(8,128)S(1)} custom-call(s32[2]{0:T(128)S(1)} %copy-done.1, s32[96]{0:T(128)S(1)} %copy-done.4, bf16[96,8,1024]{2,1,0:T(8,128)(2,1)S(1)} %copy-done, f32[96,8,1024]{2,1,0:T(8,128)S(1)} %plane.2.flat, bf16[48,8,1024]{2,1,0:T(8,128)(2,1)S(1)} %collective-permute-done.rest_0_, ...), custom_call_target="tpu_custom_call" | custom-call | flops 5000000000 | bytes 12000000 | tf_op jit(solution)/shard_map/along/pallas_call | solution.py:442
  80.0 2.0 %collective-permute-start.12 = (s16[7,8,1024]{2,1,0:T(8,128)(2,1)S(1)}, s16[7,8,1024]{2,1,0:T(8,128)(2,1)S(1)}, u32[]{:S(2)}, u32[]{:S(2)}) collective-permute-start(s16[7,8,1024]{2,1,0:T(8,128)(2,1)S(1)} %collective-permute-done.8.rest_4_), channel_id=1, source_target_pairs={{0,16},{8,24},{16,0},{24,8},{1,17},{9,25},{17,1},{25,9},{2,18},{10... | collective-permute-start | bytes 344072 | tf_op jit(solution)/shard_map/ppermute | solution.py:503
  82.0 2.3 %collective-permute-done.18.rest_9_ = s16[14,8,1024]{2,1,0:T(8,128)(2,1)S(1)} collective-permute-done((s16[14,8,1024]{2,1,0:T(8,128)(2,1)S(1)}, s16[14,8,1024]{2,1,0:T(8,128)(2,1)S(1)}, u32[]{:S(2)}, u32[]{:S(2)}) %collective-permute-start.18) | collective-permute-done | bytes 229408 | tf_op jit(solution)/shard_map/ppermute | solution.py:503
  85.0 1.4 %collective-permute-done.12.rest_5_ = s16[7,8,1024]{2,1,0:T(8,128)(2,1)S(1)} collective-permute-done((s16[7,8,1024]{2,1,0:T(8,128)(2,1)S(1)}, s16[7,8,1024]{2,1,0:T(8,128)(2,1)S(1)}, u32[]{:S(2)}, u32[]{:S(2)}) %collective-permute-start.12) | collective-permute-done | bytes 114720 | tf_op jit(solution)/shard_map/ppermute | solution.py:503
  86.4 1.3 %collective-permute-done.14.rest_7_ = s16[7,8,1024]{2,1,0:T(8,128)(2,1)S(1)} collective-permute-done((s16[7,8,1024]{2,1,0:T(8,128)(2,1)S(1)}, s16[7,8,1024]{2,1,0:T(8,128)(2,1)S(1)}, u32[]{:S(2)}, u32[]{:S(2)}) %collective-permute-start.14) | collective-permute-done | bytes 114720 | tf_op jit(solution)/shard_map/ppermute | solution.py:503
  87.7 2.2 %finish.1 = f32[96,8,1024]{2,1,0:T(8,128)} custom-call(s32[2]{0:T(128)S(1)} %copy-done.1, s32[96]{0:T(128)S(1)} %copy-done.2, f32[96,8,1024]{2,1,0:T(8,128)S(1)} %along.1.local, s16[7,8,1024]{2,1,0:T(8,128)(2,1)S(1)} %get-tuple-element.33.rest_0_, s16[7,8,1024]{2,1,0:T(8,128)(2,1)S(1)} %collective-permute-done.9.rest_1_, ...), custom_call_target="tpu_custom_call" | custom-call | tf_op jit(solution)/shard_map/finish/pallas_call | solution.py:483
  (62 shorter events, 2.5 us)
Async XLA Ops:
  2.1 22.2 %collective-permute-start.2 = (bf16[48,8,1024]{2,1,0:T(8,128)(2,1)}, bf16[48,8,1024]{2,1,0:T(8,128)(2,1)S(1)}, u32[]{:S(2)}, u32[]{:S(2)}) collective-permute-start(bf16[48,8,1024]{2,1,0:T(8,128)(2,1)} %constant_dynamic-slice_fusion), channel_id=1, source_target_pairs={{2,0},{7,1},{4,2},{1,3},{6,4},{3,5},{0,6},{5,7},{10,8},{15,9},{12,... | collective-permute-start | bytes 2359304 | tf_op jit(solution)/shard_map/ppermute | solution.py:495
  7.1 19.2 %collective-permute-start = (bf16[48,8,1024]{2,1,0:T(8,128)(2,1)}, bf16[48,8,1024]{2,1,0:T(8,128)(2,1)S(1)}, u32[]{:S(2)}, u32[]{:S(2)}) collective-permute-start(bf16[48,8,1024]{2,1,0:T(8,128)(2,1)} %constant_dynamic-slice_fusion), channel_id=1, source_target_pairs={{1,0},{0,1},{3,2},{2,3},{5,4},{4,5},{7,6},{6,7},{9,8},{8,9},{11,10... | collective-permute-start | bytes 2359304 | tf_op jit(solution)/shard_map/ppermute | solution.py:495
  24.2 27.5 %copy-start.7 = (bf16[1024,1024]{1,0:T(8,128)(2,1)S(1)}, bf16[1024,1024]{1,0:T(8,128)(2,1)}, u32[]{:S(2)}) copy-start(bf16[1024,1024]{1,0:T(8,128)(2,1)} %constant.44.clone.rest_15_) | copy-start | bytes 6291460
  26.3 2.3 %collective-permute-start.1 = (bf16[48,8,1024]{2,1,0:T(8,128)(2,1)S(1)}, bf16[48,8,1024]{2,1,0:T(8,128)(2,1)S(1)}, u32[]{:S(2)}, u32[]{:S(2)}) collective-permute-start(bf16[48,8,1024]{2,1,0:T(8,128)(2,1)S(1)} %collective-permute-done.rest_0_), channel_id=1, source_target_pairs={{0,8},{8,0},{16,24},{24,16},{1,9},{9,1},{17,25},{25,17},{2,10},{10... | collective-permute-start | bytes 2359304 | tf_op jit(solution)/shard_map/ppermute | solution.py:503
  26.3 3.4 %collective-permute-start.3 = (bf16[48,8,1024]{2,1,0:T(8,128)(2,1)S(1)}, bf16[48,8,1024]{2,1,0:T(8,128)(2,1)S(1)}, u32[]{:S(2)}, u32[]{:S(2)}) collective-permute-start(bf16[48,8,1024]{2,1,0:T(8,128)(2,1)S(1)} %collective-permute-done.2.rest_2_), channel_id=1, source_target_pairs={{0,8},{8,0},{16,24},{24,16},{1,9},{9,1},{17,25},{25,17},{2,10},{10... | collective-permute-start | bytes 2359304 | tf_op jit(solution)/shard_map/ppermute | solution.py:503
  26.8 21.5 %collective-permute-start.6 = (bf16[48,8,1024]{2,1,0:T(8,128)(2,1)}, bf16[48,8,1024]{2,1,0:T(8,128)(2,1)S(1)}, u32[]{:S(2)}, u32[]{:S(2)}) collective-permute-start(bf16[48,8,1024]{2,1,0:T(8,128)(2,1)} %constant_dynamic-slice_fusion), channel_id=1, source_target_pairs={{6,0},{3,1},{0,2},{5,3},{2,4},{7,5},{4,6},{1,7},{14,8},{11,9},{8,1... | collective-permute-start | bytes 2359304 | tf_op jit(solution)/shard_map/ppermute | solution.py:495
  26.8 21.5 %collective-permute-start.4 = (bf16[48,8,1024]{2,1,0:T(8,128)(2,1)S(1)}, bf16[48,8,1024]{2,1,0:T(8,128)(2,1)S(1)}, u32[]{:S(2)}, u32[]{:S(2)}) collective-permute-start(bf16[48,8,1024]{2,1,0:T(8,128)(2,1)S(1)} %collective-permute-done.2.rest_2_), channel_id=1, source_target_pairs={{1,0},{0,1},{3,2},{2,3},{5,4},{4,5},{7,6},{6,7},{9,8},{8,9},{11,10... | collective-permute-start | bytes 2359304 | tf_op jit(solution)/shard_map/ppermute | solution.py:495
  34.3 42.6 %copy-start.4 = (s32[96]{0:T(128)S(1)}, s32[96]{0:T(128)}, u32[]{:S(2)}) copy-start(s32[96]{0:T(128)} %shift.3) | copy-start | bytes 1156
  34.3 42.6 %copy-start.11 = (f32[32,8,192]{2,1,0:T(8,128)S(1)}, f32[32,8,192]{2,1,0:T(8,128)}, u32[]{:S(2)}) copy-start(f32[32,8,192]{2,1,0:T(8,128)} %constant.37.clone.rest_4_) | copy-start | bytes 589828
  48.3 2.3 %collective-permute-start.5 = (bf16[48,8,1024]{2,1,0:T(8,128)(2,1)S(1)}, bf16[48,8,1024]{2,1,0:T(8,128)(2,1)S(1)}, u32[]{:S(2)}, u32[]{:S(2)}) collective-permute-start(bf16[48,8,1024]{2,1,0:T(8,128)(2,1)S(1)} %collective-permute-done.4.rest_4_.rest_2_), channel_id=1, source_target_pairs={{0,8},{8,0},{16,24},{24,16},{1,9},{9,1},{17,25},{25,17},{2,10},{10... | collective-permute-start | bytes 2359304 | tf_op jit(solution)/shard_map/ppermute | solution.py:503
  48.3 3.4 %collective-permute-start.7 = (bf16[48,8,1024]{2,1,0:T(8,128)(2,1)S(1)}, bf16[48,8,1024]{2,1,0:T(8,128)(2,1)S(1)}, u32[]{:S(2)}, u32[]{:S(2)}) collective-permute-start(bf16[48,8,1024]{2,1,0:T(8,128)(2,1)S(1)} %collective-permute-done.6.rest_6_), channel_id=1, source_target_pairs={{0,8},{8,0},{16,24},{24,16},{1,9},{9,1},{17,25},{25,17},{2,10},{10... | collective-permute-start | bytes 2359304 | tf_op jit(solution)/shard_map/ppermute | solution.py:503
  63.0 10.4 %collective-permute-start.8 = (s16[7,8,1024]{2,1,0:T(8,128)(2,1)S(1)}, s16[7,8,1024]{2,1,0:T(8,128)(2,1)S(1)}, u32[]{:S(2)}, u32[]{:S(2)}) collective-permute-start(s16[7,8,1024]{2,1,0:T(8,128)(2,1)S(1)} %get-tuple-element.31), channel_id=1, source_target_pairs={{7,0},{0,1},{1,2},{2,3},{3,4},{4,5},{5,6},{6,7},{15,8},{8,9},{9,10... | collective-permute-start | bytes 344072 | tf_op jit(solution)/shard_map/ppermute | solution.py:495
  67.8 5.6 %collective-permute-start.15 = (s16[7,8,1024]{2,1,0:T(8,128)(2,1)S(1)}, s16[7,8,1024]{2,1,0:T(8,128)(2,1)S(1)}, u32[]{:S(2)}, u32[]{:S(2)}) collective-permute-start(s16[7,8,1024]{2,1,0:T(8,128)(2,1)S(1)} %get-tuple-element.34), channel_id=1, source_target_pairs={{2,0},{3,1},{4,2},{5,3},{6,4},{7,5},{0,6},{1,7},{10,8},{11,9},{12,... | collective-permute-start | bytes 344072 | tf_op jit(solution)/shard_map/ppermute | solution.py:495
  70.1 6.6 %collective-permute-start.16 = (s16[7,8,1024]{2,1,0:T(8,128)(2,1)S(1)}, s16[7,8,1024]{2,1,0:T(8,128)(2,1)S(1)}, u32[]{:S(2)}, u32[]{:S(2)}) collective-permute-start(s16[7,8,1024]{2,1,0:T(8,128)(2,1)S(1)} %get-tuple-element.35), channel_id=1, source_target_pairs={{6,0},{7,1},{0,2},{1,3},{2,4},{3,5},{4,6},{5,7},{14,8},{15,9},{8,1... | collective-permute-start | bytes 344072 | tf_op jit(solution)/shard_map/ppermute | solution.py:495
  70.1 6.6 %collective-permute-start.17 = (s16[7,8,1024]{2,1,0:T(8,128)(2,1)S(1)}, s16[7,8,1024]{2,1,0:T(8,128)(2,1)S(1)}, u32[]{:S(2)}, u32[]{:S(2)}) collective-permute-start(s16[7,8,1024]{2,1,0:T(8,128)(2,1)S(1)} %get-tuple-element.36), channel_id=1, source_target_pairs={{1,0},{2,1},{3,2},{4,3},{5,4},{6,5},{7,6},{0,7},{9,8},{10,9},{11,1... | collective-permute-start | bytes 344072 | tf_op jit(solution)/shard_map/ppermute | solution.py:495
  73.4 11.0 %collective-permute-start.10 = (s16[7,8,1024]{2,1,0:T(8,128)(2,1)S(1)}, s16[7,8,1024]{2,1,0:T(8,128)(2,1)S(1)}, u32[]{:S(2)}, u32[]{:S(2)}) collective-permute-start(s16[7,8,1024]{2,1,0:T(8,128)(2,1)S(1)} %get-tuple-element.33.rest_0_), channel_id=1, source_target_pairs={{0,8},{8,0},{16,24},{24,16},{1,9},{9,1},{17,25},{25,17},{2,10},{10... | collective-permute-start | bytes 344072 | tf_op jit(solution)/shard_map/ppermute | solution.py:503
  73.4 11.5 %collective-permute-start.9 = (s16[7,8,1024]{2,1,0:T(8,128)(2,1)S(1)}, s16[7,8,1024]{2,1,0:T(8,128)(2,1)S(1)}, u32[]{:S(2)}, u32[]{:S(2)}) collective-permute-start(s16[7,8,1024]{2,1,0:T(8,128)(2,1)S(1)} %get-tuple-element.33.rest_0_), channel_id=1, source_target_pairs={{0,16},{8,24},{16,0},{24,8},{1,17},{9,25},{17,1},{25,9},{2,18},{10... | collective-permute-start | bytes 344072 | tf_op jit(solution)/shard_map/ppermute | solution.py:503
  76.8 7.6 %collective-permute-start.18 = (s16[14,8,1024]{2,1,0:T(8,128)(2,1)S(1)}, s16[14,8,1024]{2,1,0:T(8,128)(2,1)S(1)}, u32[]{:S(2)}, u32[]{:S(2)}) collective-permute-start(s16[14,8,1024]{2,1,0:T(8,128)(2,1)S(1)} %pad_add_fusion.rest_8_), channel_id=1, source_target_pairs={{0,16},{8,24},{16,0},{24,8},{1,17},{9,25},{17,1},{25,9},{2,18},{10... | collective-permute-start | bytes 688136 | tf_op jit(solution)/shard_map/ppermute | solution.py:503
  79.9 7.7 %collective-permute-start.19 = (s16[14,8,1024]{2,1,0:T(8,128)(2,1)S(1)}, s16[14,8,1024]{2,1,0:T(8,128)(2,1)S(1)}, u32[]{:S(2)}, u32[]{:S(2)}) collective-permute-start(s16[14,8,1024]{2,1,0:T(8,128)(2,1)S(1)} %pad_add_fusion.rest_8_), channel_id=1, source_target_pairs={{0,8},{8,0},{16,24},{24,16},{1,9},{9,1},{17,25},{25,17},{2,10},{10... | collective-permute-start | bytes 688136 | tf_op jit(solution)/shard_map/ppermute | solution.py:503
  80.0 6.3 %collective-permute-start.12 = (s16[7,8,1024]{2,1,0:T(8,128)(2,1)S(1)}, s16[7,8,1024]{2,1,0:T(8,128)(2,1)S(1)}, u32[]{:S(2)}, u32[]{:S(2)}) collective-permute-start(s16[7,8,1024]{2,1,0:T(8,128)(2,1)S(1)} %collective-permute-done.8.rest_4_), channel_id=1, source_target_pairs={{0,16},{8,24},{16,0},{24,8},{1,17},{9,25},{17,1},{25,9},{2,18},{10... | collective-permute-start | bytes 344072 | tf_op jit(solution)/shard_map/ppermute | solution.py:503
  84.4 3.3 %collective-permute-start.20 = (s16[14,8,1024]{2,1,0:T(8,128)(2,1)S(1)}, s16[14,8,1024]{2,1,0:T(8,128)(2,1)S(1)}, u32[]{:S(2)}, u32[]{:S(2)}) collective-permute-start(s16[14,8,1024]{2,1,0:T(8,128)(2,1)S(1)} %collective-permute-done.18.rest_9_), channel_id=1, source_target_pairs={{0,8},{8,0},{16,24},{24,16},{1,9},{9,1},{17,25},{25,17},{2,10},{10... | collective-permute-start | bytes 688136 | tf_op jit(solution)/shard_map/ppermute | solution.py:503
  84.4 2.0 %collective-permute-start.13 = (s16[7,8,1024]{2,1,0:T(8,128)(2,1)S(1)}, s16[7,8,1024]{2,1,0:T(8,128)(2,1)S(1)}, u32[]{:S(2)}, u32[]{:S(2)}) collective-permute-start(s16[7,8,1024]{2,1,0:T(8,128)(2,1)S(1)} %collective-permute-done.8.rest_4_), channel_id=1, source_target_pairs={{0,8},{8,0},{16,24},{24,16},{1,9},{9,1},{17,25},{25,17},{2,10},{10... | collective-permute-start | bytes 344072 | tf_op jit(solution)/shard_map/ppermute | solution.py:503
  84.9 1.5 %collective-permute-start.11 = (s16[7,8,1024]{2,1,0:T(8,128)(2,1)S(1)}, s16[7,8,1024]{2,1,0:T(8,128)(2,1)S(1)}, u32[]{:S(2)}, u32[]{:S(2)}) collective-permute-start(s16[7,8,1024]{2,1,0:T(8,128)(2,1)S(1)} %collective-permute-done.9.rest_1_), channel_id=1, source_target_pairs={{0,8},{8,0},{16,24},{24,16},{1,9},{9,1},{17,25},{25,17},{2,10},{10... | collective-permute-start | bytes 344072 | tf_op jit(solution)/shard_map/ppermute | solution.py:503
  86.3 1.3 %collective-permute-start.14 = (s16[7,8,1024]{2,1,0:T(8,128)(2,1)S(1)}, s16[7,8,1024]{2,1,0:T(8,128)(2,1)S(1)}, u32[]{:S(2)}, u32[]{:S(2)}) collective-permute-start(s16[7,8,1024]{2,1,0:T(8,128)(2,1)S(1)} %collective-permute-done.12.rest_5_), channel_id=1, source_target_pairs={{0,8},{8,0},{16,24},{24,16},{1,9},{9,1},{17,25},{25,17},{2,10},{10... | collective-permute-start | bytes 344072 | tf_op jit(solution)/shard_map/ppermute | solution.py:503
  (14 other events, 127.2 us)
